TPU v7x, 128 devices: a whole 4x4x4 slice. The times are simulated.
128 devices in a mesh: dp: 16 (over z_hi, y, core), tensor: 8 (over x, z_lo).
Axes of the slice: x: 4, y: 4, z: 4 (z_hi: 2, z_lo: 2; z = z_hi * 2 + z_lo), core: 2. Of those that a mesh axis runs over, the one named last changes fastest.
Arguments:
- hidden_in: float32 [9728, 1024], P('dp'), may hold values from -6 to 6
- segments: int32 [16, 608], P('dp'), may hold values from 0 to 3, never falling along the last dimension, each value on 1 to 304 neighbouring positions
- ln1_gain: float32 [1024], replicated, may hold values from 0.1 to 1.9
- ln1_shift: float32 [1024], replicated, may hold values from -1.75 to 1.75
- qkv_weight: bfloat16 [1024, 3072], P(None, 'tensor'), may hold values from -0.1875 to 0.1875
- query_bias: float32 [1024], P('tensor'), may hold values from -3 to 3
- value_bias: float32 [1024], P('tensor'), may hold values from -3 to 3
- dense_weight: bfloat16 [1024, 1024], P('tensor'), may hold values from -0.75 to 0.75
- dense_bias: float32 [1024], replicated, may hold values from -3 to 3
- ln2_gain: float32 [1024], replicated, may hold values from 0.1 to 1.9
- ln2_shift: float32 [1024], replicated, may hold values from -1.75 to 1.75
- up_weight: bfloat16 [1024, 4096], P(None, 'tensor'), may hold values from -0.1875 to 0.1875
- up_bias: float32 [4096], P('tensor'), may hold values from -3 to 3
- down_weight: bfloat16 [4096, 1024], P('tensor'), may hold values from -0.125 to 0.125
- down_bias: float32 [1024], replicated, may hold values from -3 to 3
- out_grad: float32 [9728, 1024], P('dp'), may hold values from -6 to 6
Outputs:
- block_out: float32 [9728, 1024], P('dp')
- input_grad: float32 [9728, 1024], P('dp')
- ln1_gain_grad: float32 [1024], replicated
- ln1_shift_grad: float32 [1024], replicated
- qkv_weight_grad: float32 [1024, 3072], P(None, 'tensor')
- query_bias_grad: float32 [1024], P('tensor')
- value_bias_grad: float32 [1024], P('tensor')
- dense_weight_grad: float32 [1024, 1024], P('tensor')
- dense_bias_grad: float32 [1024], replicated
- ln2_gain_grad: float32 [1024], replicated
- ln2_shift_grad: float32 [1024], replicated
- up_weight_grad: float32 [1024, 4096], P(None, 'tensor')
- up_bias_grad: float32 [4096], P('tensor')
- down_weight_grad: float32 [4096, 1024], P('tensor')
- down_bias_grad: float32 [1024], replicated
Inputs may be any that keep to these rules, and one draw needn't show every extreme that they name: `segments`: in each packed row the document numbers never fall and every number from 0 to 3 appears; documents hold 1 to 304 tokens, and every row has one of exactly 304.
All inputs are finite; a program needn't handle non-finite values.
Results may differ from a plain program's by a relative error of at most 0.012.
The roundings to bfloat16 on the way count: a program that leaves them out, or rounds other values in their place, can miss the bound.
Values may be sent and summed in bfloat16 or wider, within the bound.
No kernel may reach another device: no remote copies, remote signals or barrier semaphores. Data moves between devices by JAX's collectives and lax.ppermute only.
A program may use at most 128 MiB of HBM per device.

v0:
```python
from functools import partial

import jax
import jax.numpy as jnp
from jax import lax
from jax.experimental import pallas as pl
from jax.experimental.pallas import tpu as pltpu
from jax.sharding import PartitionSpec as P

HEADS = 16
HEAD_DIM = 64
EPS = 1e-05
NEG = -1000000000.0
T = "tensor"
DP = "dp"
NT = 8
BLK = 80
PAD = NT * BLK
BF = jnp.bfloat16
F32 = jnp.float32


def norm_stats(values_in):
    row_mean = jnp.mean(values_in, -1, keepdims=True)
    centred = values_in - row_mean
    variance = jnp.mean(centred * centred, -1, keepdims=True)
    recip = lax.rsqrt(variance + EPS)
    return centred * recip, recip


def norm_backward(grad_out, normal_part, recip, gain_vec):
    scaled = grad_out * gain_vec
    return recip * (
        scaled
        - jnp.mean(scaled, -1, keepdims=True)
        - normal_part * jnp.mean(scaled * normal_part, -1, keepdims=True)
    )


def dot(a, b):
    return jnp.dot(a, b, preferred_element_type=F32)


def dot_nt(a, b):
    return lax.dot_general(a, b, (((1,), (1,)), ((), ())), preferred_element_type=F32)


def dot_tn(a, b):
    return lax.dot_general(a, b, (((0,), (0,)), ((), ())), preferred_element_type=F32)


def pad_rows(a):
    return jnp.pad(a, ((0, PAD - a.shape[0]), (0, 0)))


def block_of(a, j):
    return lax.dynamic_slice_in_dim(a, j * BLK, BLK, 0)


def exchange(a, axis):
    return lax.all_to_all(a, axis, 0, 0, tiled=True)


def gather(piece):
    return exchange(jnp.broadcast_to(piece[None], (NT,) + piece.shape), T)


def hop(a, mask):
    return lax.ppermute(a, DP, [(i, i ^ mask) for i in range(16)])


def pick(a, j, axis=0):
    return lax.dynamic_index_in_dim(a, j, axis, keepdims=False)


def reduce_dp(payload, dp):
    core, y, z = dp % 2, (dp // 2) % 4, dp // 8
    rows, width = payload.shape
    chunk = rows // 16
    parts = payload.reshape(2, 2, 4, chunk, width)
    one = (pick(parts, core).astype(F32) + hop(pick(parts, 1 - core), 1).astype(F32)).astype(BF)
    two = pick(one, y, 1).astype(F32)
    for k in (1, 2, 3):
        two = two + hop(pick(one, y ^ k, 1), 2 * k).astype(F32)
    two = two.astype(BF)
    three = (pick(two, z).astype(F32) + hop(pick(two, 1 - z), 8).astype(F32)).astype(BF)
    by_z = jnp.stack([three, hop(three, 8)])
    by_y = jnp.stack([by_z] + [hop(by_z, 2 * k) for k in (1, 2, 3)])
    return jnp.stack([by_y, hop(by_y, 1)]).reshape(16, chunk, width)


def spread(perm_ref, got_ref, left_ref, right_ref):
    chunk = got_ref.shape[1]
    cut = left_ref.shape[1]
    for i in range(16):
        rows = got_ref[perm_ref[i]].astype(F32)
        left_ref[i * chunk : (i + 1) * chunk, :] = rows[:, :cut]
        right_ref[i * chunk : (i + 1) * chunk, :] = rows[:, cut:]


def natural_chunks(got, dp, cut):
    core, y, z = dp % 2, (dp // 2) % 4, dp // 8
    order = jnp.arange(16)
    c, zz, yy = order // 8, (order // 4) % 2, order % 4
    perm = ((c ^ core) * 8 + (yy ^ y) * 2 + (zz ^ z)).astype(jnp.int32)
    n, chunk, width = got.shape
    left, right = pl.pallas_call(
        spread,
        out_shape=[
            jax.ShapeDtypeStruct((n * chunk, cut), F32),
            jax.ShapeDtypeStruct((n * chunk, width - cut), F32),
        ],
        in_specs=[
            pl.BlockSpec(memory_space=pltpu.SMEM),
            pl.BlockSpec(memory_space=pltpu.VMEM),
        ],
        out_specs=[pl.BlockSpec(memory_space=pltpu.VMEM)] * 2,
        compiler_params=pltpu.CompilerParams(vmem_limit_bytes=32 << 20),
    )(perm, got)
    return left, right.T


def per_device(
    hidden_in,
    segments,
    ln1_gain,
    ln1_shift,
    qkv_weight,
    query_bias,
    value_bias,
    dense_weight,
    dense_bias,
    ln2_gain,
    ln2_shift,
    up_weight,
    up_bias,
    down_weight,
    down_bias,
    out_grad,
):
    seq_len = hidden_in.shape[0]
    seg = segments[0]
    me = lax.axis_index(T)
    dp = lax.axis_index(DP)
    core = dp % 2
    gelu_tanh = partial(jax.nn.gelu, approximate=True)
    scale = HEAD_DIM ** (-0.5)

    half_w = lax.dynamic_slice_in_dim(dense_weight, core * HEAD_DIM, HEAD_DIM, 0)
    own_w = gather(half_w)
    other_w = hop(own_w, 1)

    xhat1, recip1 = norm_stats(hidden_in)
    act_one = (xhat1 * ln1_gain + ln1_shift).astype(BF)
    zero_keys = jnp.zeros((2, HEAD_DIM), F32)
    qkv_bias = jnp.stack(
        [query_bias.reshape(2, HEAD_DIM), zero_keys, value_bias.reshape(2, HEAD_DIM)], axis=1
    ).reshape(-1)
    qkv_low = (dot(act_one, qkv_weight) + qkv_bias).astype(BF)
    pos = jnp.arange(seq_len)
    distance = (pos[None, :] - pos[:, None]).astype(F32)
    allowed = (distance <= 0) & (seg[:, None] == seg[None, :])
    slopes = jnp.exp2(-(8.0 / HEADS) * (me * 2 + jnp.arange(2) + 1).astype(F32))

    def part(h, c):
        start = (h * 3 + c) * HEAD_DIM
        return qkv_low[:, start : start + HEAD_DIM]

    def scores_of(h):
        raw = dot_nt(part(h, 0), part(h, 1)) * scale + slopes[h] * distance
        return jnp.where(allowed, raw, NEG)

    contexts, log_sums = [], []
    for h in range(2):
        s = scores_of(h)
        top = jnp.max(s, -1, keepdims=True)
        e = jnp.exp(s - top)
        total = jnp.sum(e, -1, keepdims=True)
        log_sums.append(top + jnp.log(total))
        contexts.append(dot((e / total).astype(BF), part(h, 2)).astype(BF))

    context = jnp.concatenate(contexts, 1)
    first = jnp.where(core == 0, contexts[0], contexts[1])
    second = jnp.where(core == 0, contexts[1], contexts[0])
    ctx_got = gather(pad_rows(jnp.concatenate([first, second], 1)))

    grad_low = out_grad.astype(BF)
    grad_pad = pad_rows(grad_low)
    gelu_in_grad = dot_nt(grad_pad, down_weight)
    hid_pad = pad_rows(hidden_in)

    ctx_a = jnp.concatenate([ctx_got[i, :, :HEAD_DIM] for i in range(NT)], 1)
    ctx_b = jnp.concatenate([ctx_got[i, :, HEAD_DIM:] for i in range(NT)], 1)
    attn = dot(ctx_a, own_w.reshape(NT * HEAD_DIM, -1)) + dot(
        ctx_b, other_w.reshape(NT * HEAD_DIM, -1)
    )
    middle = hid_pad + (attn + dense_bias)
    xhat2, recip2 = norm_stats(middle)
    act_two = (xhat2 * ln2_gain + ln2_shift).astype(BF)

    up_value = dot(act_two, up_weight) + up_bias
    gelu_val, gelu_vjp = jax.vjp(gelu_tanh, up_value)
    gelu_low = gelu_val.astype(BF)
    up_low = gelu_vjp(gelu_in_grad)[0].astype(BF)
    norm_two_part = dot_nt(up_low, up_weight).astype(BF)
    norm_two_in = jnp.sum(exchange(norm_two_part.reshape(NT, BLK, -1), T).astype(F32), 0)

    mlp_sum = lax.psum(dot(gelu_low[:seq_len], down_weight).astype(BF), T)
    up_bias_part = jnp.sum(up_low, 0, dtype=F32)
    down_bias_part = jnp.sum(grad_low, 0, dtype=F32)
    early = jnp.concatenate([dot_tn(act_two, up_low), dot_tn(grad_pad, gelu_low)], 1).astype(BF)
    early_got = reduce_dp(early, dp)
    up_weight_grad, down_weight_grad = natural_chunks(early_got, dp, 512)

    middle_own = block_of(middle, me)
    xhat2_own, recip2_own = norm_stats(middle_own)
    out_grad_own = block_of(pad_rows(out_grad), me)
    back_two = norm_backward(norm_two_in, xhat2_own, recip2_own, ln2_gain)
    branch_own = (out_grad_own + back_two).astype(BF)
    branch = gather(branch_own).reshape(PAD, -1)[:seq_len]
    ctx_grad = dot_nt(branch, dense_weight).astype(BF)

    grads = []
    for h in range(2):
        probs = jnp.exp(scores_of(h) - log_sums[h])
        cg = ctx_grad[:, h * HEAD_DIM : (h + 1) * HEAD_DIM]
        prob_grad = dot_nt(cg, part(h, 2))
        value_grad = dot_tn(probs.astype(BF), cg)
        score_low = (
            probs * (prob_grad - jnp.sum(prob_grad * probs, -1, keepdims=True))
        ).astype(BF)
        query_grad = dot(score_low, part(h, 1)) * scale
        key_grad = dot_tn(score_low, part(h, 0)) * scale
        grads += [query_grad, key_grad, value_grad]
    qkv_grad_low = jnp.concatenate(grads, 1).astype(BF)
    norm_one_part = dot_nt(qkv_grad_low, qkv_weight)
    gain_one_part = jnp.sum(norm_one_part * xhat1, 0)
    shift_one_part = jnp.sum(norm_one_part, 0)
    got = exchange(pad_rows(norm_one_part.astype(BF)).reshape(NT, BLK, -1), T)
    norm_one_in = jnp.sum(got.astype(F32), 0)
    hid_own = block_of(hid_pad, me)
    xhat1_own, recip1_own = norm_stats(hid_own)
    in_delta = (back_two + norm_backward(norm_one_in, xhat1_own, recip1_own, ln1_gain)).astype(BF)
    in_got, mlp_sum = lax.optimization_barrier((gather(in_delta), mlp_sum))
    input_grad = out_grad + in_got.reshape(PAD, -1)[:seq_len].astype(F32)
    block_out = middle[:seq_len] + (mlp_sum.astype(F32) + down_bias)

    late = jnp.concatenate([dot_tn(act_one, qkv_grad_low), dot_tn(branch, context)], 1).astype(BF)
    late_got = reduce_dp(late, dp)
    qkv_weight_grad, dense_weight_grad = natural_chunks(late_got, dp, 384)

    part_sums = jnp.sum(qkv_grad_low, 0, dtype=F32)
    rows = [
        gain_one_part,
        shift_one_part,
        jnp.sum(norm_two_in * xhat2_own, 0),
        jnp.sum(norm_two_in, 0),
        jnp.sum(branch_own, 0, dtype=F32),
        down_bias_part,
        jnp.concatenate([up_bias_part, part_sums, jnp.zeros((128,), F32)]),
        jnp.zeros((1024,), F32),
    ]
    summed = jnp.concatenate([r.reshape(8, 128) for r in rows], 0)
    for mask in (1, 2, 4, 8):
        summed = summed + hop(summed, mask)
    shared = summed[:40]
    for k in (1, 2, 4):
        shared = shared + lax.ppermute(shared, T, [(i, i ^ k) for i in range(NT)])
    shared = shared.reshape(5, 1024)
    last = summed[48:56].reshape(1024)
    sums = last[512:896].reshape(2, 3, HEAD_DIM)

    return (
        block_out,
        input_grad,
        shared[0],
        shared[1],
        qkv_weight_grad,
        sums[:, 0].reshape(-1),
        sums[:, 2].reshape(-1),
        dense_weight_grad,
        shared[4],
        shared[2],
        shared[3],
        up_weight_grad,
        last[:512],
        down_weight_grad,
        summed[40:48].reshape(1024),
    )


def solution(mesh):
    placed = (
        P("dp", None),
        P("dp", None),
        P(),
        P(),
        P(None, "tensor"),
        P("tensor"),
        P("tensor"),
        P("tensor", None),
        P(),
        P(),
        P(),
        P(None, "tensor"),
        P("tensor"),
        P("tensor", None),
        P(),
        P("dp", None),
    )
    return jax.shard_map(
        per_device,
        mesh=mesh,
        in_specs=placed,
        out_specs=(
            P("dp", None),
            P("dp", None),
            P(),
            P(),
            P(None, "tensor"),
            P("tensor"),
            P("tensor"),
            P("tensor", None),
            P(),
            P(),
            P(),
            P(None, "tensor"),
            P("tensor"),
            P("tensor", None),
            P(),
        ),
        check_vma=False,
    )
```

profile of v0, /device:TPU:0, one launch (start us, length us, event | category | flops | bytes accessed | tf_op | source)
XLA Modules:
  0.0 280.9 jit_solution(6602552604516857847)
XLA Ops:
  9.4 5.9 %all-to-all-start.1 = ((bf16[8,64,1024]{2,1,0:T(8,128)(2,1)}), bf16[8,64,1024]{2,1,0:T(8,128)(2,1)}, u32[]{:S(2)}, u32[]{:S(2)}) async-start(bf16[8,64,1024]{2,1,0:T(8,128)(2,1)} %broadcast_in_dim.19), calls=%async_computation.1 | async-start | bytes 2097152 | tf_op jit(solution)/shard_map/all_to_all | solution.py:61
  20.5 1.5 fusion.92
  22.0 1.5 fusion.91
  26.4 1.7 copy.52
  28.2 1.6 pad.19.clone
  29.7 1.4 all-to-all-done.1
  31.2 2.1 broadcast_in_dim.18
  33.3 4.3 %all-to-all-start = ((bf16[8,640,128]{2,1,0:T(8,128)(2,1)}), bf16[8,640,128]{2,1,0:T(8,128)(2,1)}, u32[]{:S(2)}, u32[]{:S(2)}) async-start(bf16[8,640,128]{2,1,0:T(8,128)(2,1)} %broadcast_in_dim.18), calls=%async_computation | async-start | bytes 2621440 | tf_op jit(solution)/shard_map/all_to_all | solution.py:61
  40.3 1.9 convert_reduce_fusion.3
  42.2 14.1 %all-to-all-done = bf16[8,640,128]{2,1,0:T(8,128)(2,1)} async-done(((bf16[8,640,128]{2,1,0:T(8,128)(2,1)}), bf16[8,640,128]{2,1,0:T(8,128)(2,1)}, u32[]{:S(2)}, u32[]{:S(2)}) %all-to-all-start) | async-done | bytes 1310752 | tf_op jit(solution)/shard_map/all_to_all | solution.py:61
  56.3 3.6 %slice_bitcast_fusion = (bf16[640,64]{1,0:T(8,128)(2,1)}, bf16[640,64]{1,0:T(8,128)(2,1)}, bf16[640,64]{1,0:T(8,128)(2,1)}, bf16[640,64]{1,0:T(8,128)(2,1)}, bf1...) fusion(bf16[8,640,128]{2,1,0:T(8,128)(2,1)} %all-to-all-done), kind=kLoop, calls=%fused_computation.133 | loop fusion | bytes 2621440 | tf_op jit(solution)/shard_map/squeeze | solution.py:193
  60.0 2.4 concatenate.42
  62.3 2.3 concatenate.41
  64.7 2.3 fusion.94
  67.1 2.3 fusion.93
  70.2 2.0 multiply_convert_fusion.2
  72.3 2.2 convert_reduce_fusion.4
  74.5 1.9 convolution_convert_fusion
  76.4 4.4 %all-to-all-start.2 = ((bf16[8,80,1024]{2,1,0:T(8,128)(2,1)}), bf16[8,80,1024]{2,1,0:T(8,128)(2,1)}, u32[]{:S(2)}, u32[]{:S(2)}) async-start(bf16[8,80,1024]{2,1,0:T(8,128)(2,1)} %bitcast.171), calls=%async_computation.2 | async-start | bytes 2621440 | tf_op jit(solution)/shard_map/all_to_all | solution.py:61
  80.9 2.5 convolution_convert_fusion.2
  87.3 11.5 %all-to-all-done.2 = bf16[8,80,1024]{2,1,0:T(8,128)(2,1)} async-done(((bf16[8,80,1024]{2,1,0:T(8,128)(2,1)}), bf16[8,80,1024]{2,1,0:T(8,128)(2,1)}, u32[]{:S(2)}, u32[]{:S(2)}) %all-to-all-start.2) | async-done | bytes 1310752 | tf_op jit(solution)/shard_map/all_to_all | solution.py:61
  98.8 2.4 convert_reduce_fusion
  101.2 1.8 multiply_reduce_fusion.5
  103.0 1.8 convert_reduce_fusion.6
  106.1 4.4 %all-to-all-start.3 = ((bf16[8,80,1024]{2,1,0:T(8,128)(2,1)}), bf16[8,80,1024]{2,1,0:T(8,128)(2,1)}, u32[]{:S(2)}, u32[]{:S(2)}) async-start(bf16[8,80,1024]{2,1,0:T(8,128)(2,1)} %broadcast_in_dim.20), calls=%async_computation.3 | async-start | bytes 2621440 | tf_op jit(solution)/shard_map/all_to_all | solution.py:61
  111.7 1.6 fusion
  114.2 1.6 collective-permute-start.19
  115.8 2.2 collective-permute-start.21
  118.8 4.9 %collective-permute-done.19 = bf16[2,64,1024]{2,1,0:T(8,128)(2,1)S(1)} collective-permute-done((bf16[2,64,1024]{2,1,0:T(8,128)(2,1)}, bf16[2,64,1024]{2,1,0:T(8,128)(2,1)S(1)}, u32[]{:S(2)}, u32[]{:S(2)}) %collective-permute-start.19) | collective-permute-done | bytes 262176 | tf_op jit(solution)/shard_map/ppermute | solution.py:69
  123.7 4.1 %collective-permute-done.21 = bf16[2,64,1024]{2,1,0:T(8,128)(2,1)} collective-permute-done((bf16[2,64,1024]{2,1,0:T(8,128)(2,1)}, bf16[2,64,1024]{2,1,0:T(8,128)(2,1)}, u32[]{:S(2)}, u32[]{:S(2)}) %collective-permute-start.21) | collective-permute-done | bytes 262176 | tf_op jit(solution)/shard_map/ppermute | solution.py:69
  127.8 1.5 collective-permute-done.20
  131.3 12.1 %collective-permute-start.22 = (bf16[64,1024]{1,0:T(8,128)(2,1)}, bf16[64,1024]{1,0:T(8,128)(2,1)}, u32[]{:S(2)}, u32[]{:S(2)}) collective-permute-start(bf16[64,1024]{1,0:T(8,128)(2,1)} %dynamic-slice_bitcast_fusion.3), channel_id=1, source_target_pairs={{0,64},{8,72},{16,80},{24,88},{32,96},{40,104},{48,112},{56,120},{... | collective-permute-start | bytes 393224 | tf_op jit(solution)/shard_map/ppermute | solution.py:69
  143.5 1.9 convolution_convert_fusion.6
  152.5 2.1 fusion.88
  154.6 1.9 convolution_convert_fusion.5
  159.9 1.9 collective-permute-start.9
  161.9 2.2 collective-permute-start.11
  164.1 1.8 convolution_convert_fusion.1
  165.9 2.4 pad.22
  168.4 5.1 %all-to-all-start.4 = ((bf16[8,80,1024]{2,1,0:T(8,128)(2,1)}), bf16[8,80,1024]{2,1,0:T(8,128)(2,1)}, u32[]{:S(2)}, u32[]{:S(2)}) async-start(bf16[8,80,1024]{2,1,0:T(8,128)(2,1)} %bitcast.169), calls=%async_computation.4 | async-start | bytes 2621440 | tf_op jit(solution)/shard_map/all_to_all | solution.py:61
  173.5 3.6 %collective-permute-start.3 = (f32[64,128]{1,0:T(8,128)S(1)}, f32[64,128]{1,0:T(8,128)S(1)}, u32[]{:S(2)}, u32[]{:S(2)}) collective-permute-start(f32[64,128]{1,0:T(8,128)S(1)} %add.335), channel_id=1, source_target_pairs={{0,32},{8,40},{16,48},{24,56},{32,0},{40,8},{48,16},{56,24},{64,96... | collective-permute-start | bytes 98312 | tf_op jit(solution)/shard_map/ppermute | solution.py:69
  179.0 2.1 collective-permute-start.24
  181.1 2.4 collective-permute-start.26
  183.5 3.7 %collective-permute-start.4 = (f32[64,128]{1,0:T(8,128)S(1)}, f32[64,128]{1,0:T(8,128)S(1)}, u32[]{:S(2)}, u32[]{:S(2)}) collective-permute-start(f32[64,128]{1,0:T(8,128)S(1)} %add.336), channel_id=1, source_target_pairs={{0,64},{8,72},{16,80},{24,88},{32,96},{40,104},{48,112},{56,120},{... | collective-permute-start | bytes 98312 | tf_op jit(solution)/shard_map/ppermute | solution.py:69
  190.9 1.5 collective-permute-done.26
  192.4 1.5 fusion.87
  193.9 2.6 collective-permute-done.4
  196.5 2.6 collective-permute-done.12
  200.6 5.2 %collective-permute-start.5 = (f32[40,128]{1,0:T(8,128)}, f32[40,128]{1,0:T(8,128)}, u32[]{:S(2)}, u32[]{:S(2)}) collective-permute-start(f32[40,128]{1,0:T(8,128)} %slice.217), channel_id=1, source_target_pairs={{0,1},{1,0},{2,3},{3,2},{4,5},{5,4},{6,7},{7,6},{8,9},{9,8},{10,11... | collective-permute-start | bytes 61448 | tf_op jit(solution)/shard_map/ppermute | solution.py:268
  205.8 2.1 collective-permute-done.13
  208.6 3.8 %collective-permute-start.15 = (bf16[2,64,512]{2,1,0:T(8,128)(2,1)}, bf16[2,64,512]{2,1,0:T(8,128)(2,1)}, u32[]{:S(2)}, u32[]{:S(2)}) collective-permute-start(bf16[2,64,512]{2,1,0:T(8,128)(2,1)} %get-tuple-element.108), channel_id=1, source_target_pairs={{0,32},{8,40},{16,48},{24,56},{32,0},{40,8},{48,16},{56,24},{64,96... | collective-permute-start | bytes 393224 | tf_op jit(solution)/shard_map/ppermute | solution.py:69
  213.1 1.6 convert_reduce_fusion.2
  218.2 11.3 %all-to-all-start.5 = ((bf16[8,80,1024]{2,1,0:T(8,128)(2,1)}), bf16[8,80,1024]{2,1,0:T(8,128)(2,1)S(1)}, u32[]{:S(2)}, u32[]{:S(2)}) async-start(bf16[8,80,1024]{2,1,0:T(8,128)(2,1)} %broadcast_in_dim.21), calls=%async_computation.5 | async-start | bytes 2621440 | tf_op jit(solution)/shard_map/all_to_all | solution.py:61
  230.4 2.0 collective-permute-start.6
  232.4 2.1 fusion.86
  235.2 9.1 %collective-permute-done.6 = f32[40,128]{1,0:T(8,128)S(1)} collective-permute-done((f32[40,128]{1,0:T(8,128)S(1)}, f32[40,128]{1,0:T(8,128)S(1)}, u32[]{:S(2)}, u32[]{:S(2)}) %collective-permute-start.6) | collective-permute-done | bytes 20512 | tf_op jit(solution)/shard_map/ppermute | solution.py:268
  244.3 3.2 %collective-permute-start.7 = (f32[40,128]{1,0:T(8,128)S(1)}, f32[40,128]{1,0:T(8,128)S(1)}, u32[]{:S(2)}, u32[]{:S(2)}) collective-permute-start(f32[40,128]{1,0:T(8,128)S(1)} %add.339), channel_id=1, source_target_pairs={{0,4},{1,5},{2,6},{3,7},{4,0},{5,1},{6,2},{7,3},{8,12},{9,13},{10,... | collective-permute-start | bytes 61448 | tf_op jit(solution)/shard_map/ppermute | solution.py:268
  250.2 1.4 pad_maximum_fusion
  251.6 2.0 shard_map.272
  253.7 1.8 copy.45
  256.8 1.8 shard_map.271
  259.6 8.5 %all-reduce.7.cloned.1.call-done = bf16[608,1024]{1,0:T(8,128)(2,1)} async-done(((bf16[608,1024]{1,0:T(8,128)(2,1)}), bf16[608,1024]{1,0:T(8,128)(2,1)}) %all-reduce.7.cloned.1.call-update) | async-done | bytes 1245200 | tf_op jit(solution)/shard_map/psum | solution.py:208
  268.1 3.9 %convert_add_fusion = f32[608,1024]{1,0:T(8,128)} fusion(f32[608,1024]{1,0:T(8,128)} %param.31, bf16[640,1024]{1,0:T(8,128)(2,1)S(1)} %bitcast.170), kind=kLoop, calls=%fused_computation.11 | loop fusion | flops 1245184 | bytes 6225920 | tf_op jit(solution)/shard_map/add | solution.py:245
  272.0 1.9 slice_add_fusion
  (304 shorter events, 52.4 us)
Async XLA Ops:
  7.2 62.6 %copy-start = (bf16[1024,512]{1,0:T(8,128)(2,1)S(1)}, bf16[1024,512]{1,0:T(8,128)(2,1)}, u32[]{:S(2)}) copy-start(bf16[1024,512]{1,0:T(8,128)(2,1)} %param.27) | copy-start | bytes 3145732
  8.2 7.6 %copy-start.74 = (f32[128]{0:T(128)S(1)}, f32[128]{0:T(128)}, u32[]{:S(2)}) copy-start(f32[128]{0:T(128)} %param.21) | copy-start | bytes 1540
  8.2 7.7 %copy-start.75 = (f32[128]{0:T(128)S(1)}, f32[128]{0:T(128)}, u32[]{:S(2)}) copy-start(f32[128]{0:T(128)} %param.22) | copy-start | bytes 1540
  8.2 8.6 %copy-start.63 = (s32[1,608]{1,0:T(1,128)S(1)}, s32[1,608]{1,0:T(1,128)}, u32[]{:S(2)}) copy-start(s32[1,608]{1,0:T(1,128)} %param.17) | copy-start | bytes 7300
  8.3 9.2 %copy-start.2 = (f32[608,1024]{1,0:T(8,128)S(1)}, f32[608,1024]{1,0:T(8,128)}, u32[]{:S(2)}) copy-start(f32[608,1024]{1,0:T(8,128)} %param.16) | copy-start | bytes 7471108
  9.4 21.8 %all-to-all-start.1 = ((bf16[8,64,1024]{2,1,0:T(8,128)(2,1)}), bf16[8,64,1024]{2,1,0:T(8,128)(2,1)}, u32[]{:S(2)}, u32[]{:S(2)}) async-start(bf16[8,64,1024]{2,1,0:T(8,128)(2,1)} %broadcast_in_dim.19), calls=%async_computation.1 | async-start | bytes 2097152 | tf_op jit(solution)/shard_map/all_to_all | solution.py:61
  20.5 4.0 %copy-start.17 = (bf16[608,384]{1,0:T(8,128)(2,1)}, bf16[608,384]{1,0:T(8,128)(2,1)S(1)}, u32[]{:S(2)}) copy-start(bf16[608,384]{1,0:T(8,128)(2,1)S(1)} %fusion.11) | copy-start | bytes 1400836
  33.3 23.0 %all-to-all-start = ((bf16[8,640,128]{2,1,0:T(8,128)(2,1)}), bf16[8,640,128]{2,1,0:T(8,128)(2,1)}, u32[]{:S(2)}, u32[]{:S(2)}) async-start(bf16[8,640,128]{2,1,0:T(8,128)(2,1)} %broadcast_in_dim.18), calls=%async_computation | async-start | bytes 2621440 | tf_op jit(solution)/shard_map/all_to_all | solution.py:61
  39.2 27.8 %collective-permute-start = (bf16[8,64,1024]{2,1,0:T(8,128)(2,1)}, bf16[8,64,1024]{2,1,0:T(8,128)(2,1)}, u32[]{:S(2)}, u32[]{:S(2)}) collective-permute-start(bf16[8,64,1024]{2,1,0:T(8,128)(2,1)} %all-to-all-done.1), channel_id=1, source_target_pairs={{0,8},{8,0},{16,24},{24,16},{32,40},{40,32},{48,56},{56,48},{64,72... | collective-permute-start | bytes 3145736 | tf_op jit(solution)/shard_map/ppermute | solution.py:69
  69.4 2.9 %copy-start.3 = (f32[640,1024]{1,0:T(8,128)}, f32[640,1024]{1,0:T(8,128)S(1)}, u32[]{:S(2)}) copy-start(f32[640,1024]{1,0:T(8,128)S(1)} %get-tuple-element.122) | copy-start | bytes 7864324
  69.4 2.8 %copy-start.44 = (f32[640]{0:T(1024)}, f32[640]{0:T(1024)S(1)}, u32[]{:S(2)}) copy-start(f32[640]{0:T(1024)S(1)} %broadcast_multiply_fusion) | copy-start | bytes 7684
  76.4 4.4 %copy-start.76 = (bf16[640,512]{1,0:T(8,128)(2,1)S(1)}, bf16[640,512]{1,0:T(8,128)(2,1)}, u32[]{:S(2)}) copy-start(bf16[640,512]{1,0:T(8,128)(2,1)} %get-tuple-element.128) | copy-start | bytes 1966084
  76.4 22.4 %all-to-all-start.2 = ((bf16[8,80,1024]{2,1,0:T(8,128)(2,1)}), bf16[8,80,1024]{2,1,0:T(8,128)(2,1)}, u32[]{:S(2)}, u32[]{:S(2)}) async-start(bf16[8,80,1024]{2,1,0:T(8,128)(2,1)} %bitcast.171), calls=%async_computation.2 | async-start | bytes 2621440 | tf_op jit(solution)/shard_map/all_to_all | solution.py:61
  87.0 24.7 %collective-permute-start.18 = (bf16[2,4,64,1024]{3,2,0,1:T(8,128)(2,1)}, bf16[2,4,64,1024]{3,2,0,1:T(8,128)(2,1)}, u32[]{:S(2)}, u32[]{:S(2)}) collective-permute-start(bf16[2,4,64,1024]{3,2,0,1:T(8,128)(2,1)} %bitcast.163), channel_id=1, source_target_pairs={{0,8},{8,0},{16,24},{24,16},{32,40},{40,32},{48,56},{56,48},{64,72... | collective-permute-start | bytes 3145736 | tf_op jit(solution)/shard_map/ppermute | solution.py:69
  87.1 17.7 %copy-start.47 = (f32[80]{0:T(128)}, f32[80]{0:T(128)S(1)}, u32[]{:S(2)}) copy-start(f32[80]{0:T(128)S(1)} %broadcast_multiply_fusion.7) | copy-start | bytes 964
  87.3 17.5 %copy-start.49 = (f32[80]{0:T(128)}, f32[80]{0:T(128)S(1)}, u32[]{:S(2)}) copy-start(f32[80]{0:T(128)S(1)} %add_rsqrt_fusion.3) | copy-start | bytes 964
  101.2 3.7 %copy-start.11 = (f32[80,1024]{1,0:T(8,128)}, f32[80,1024]{1,0:T(8,128)S(1)}, u32[]{:S(2)}) copy-start(f32[80,1024]{1,0:T(8,128)S(1)} %get-tuple-element.62) | copy-start | bytes 983044
  106.1 5.6 %copy-start.13 = (bf16[1,2,4,64,1024]{4,3,2,1,0:T(8,128)(2,1)S(1)}, bf16[1,2,4,64,1024]{4,3,2,1,0:T(8,128)(2,1)}, u32[]{:S(2)}) copy-start(bf16[1,2,4,64,1024]{4,3,2,1,0:T(8,128)(2,1)} %get-tuple-element.73) | copy-start | bytes 3145732
  106.1 37.4 %all-to-all-start.3 = ((bf16[8,80,1024]{2,1,0:T(8,128)(2,1)}), bf16[8,80,1024]{2,1,0:T(8,128)(2,1)}, u32[]{:S(2)}, u32[]{:S(2)}) async-start(bf16[8,80,1024]{2,1,0:T(8,128)(2,1)} %broadcast_in_dim.20), calls=%async_computation.3 | async-start | bytes 2621440 | tf_op jit(solution)/shard_map/all_to_all | solution.py:61
  110.5 157.6 %all-reduce.7.cloned.1.call-start = ((), (), s32[]{:S(2)}) async-start(), calls=%async_computation.6 | async-start | bytes 2490368 | tf_op jit(solution)/shard_map/psum | solution.py:208
  113.3 4.7 %copy-start.14 = (bf16[2,4,64,1024]{3,2,0,1:T(8,128)(2,1)}, bf16[2,4,64,1024]{3,2,0,1:T(8,128)(2,1)S(1)}, u32[]{:S(2)}) copy-start(bf16[2,4,64,1024]{3,2,0,1:T(8,128)(2,1)S(1)} %fusion) | copy-start | bytes 3145732
  113.4 5.4 %copy-start.33 = (f32[608]{0:T(1024)S(1)}, f32[608]{0:T(1024)}, u32[]{:S(2)}) copy-start(f32[608]{0:T(1024)} %copy-done.32) | copy-start | bytes 7300
  113.4 5.4 %copy-start.35 = (f32[608]{0:T(1024)S(1)}, f32[608]{0:T(1024)}, u32[]{:S(2)}) copy-start(f32[608]{0:T(1024)} %copy-done.34) | copy-start | bytes 7300
  114.2 9.5 %collective-permute-start.19 = (bf16[2,64,1024]{2,1,0:T(8,128)(2,1)}, bf16[2,64,1024]{2,1,0:T(8,128)(2,1)S(1)}, u32[]{:S(2)}, u32[]{:S(2)}) collective-permute-start(bf16[2,64,1024]{2,1,0:T(8,128)(2,1)} %get-tuple-element.93), channel_id=1, source_target_pairs={{0,16},{8,24},{16,0},{24,8},{32,48},{40,56},{48,32},{56,40},{64,80... | collective-permute-start | bytes 786440 | tf_op jit(solution)/shard_map/ppermute | solution.py:69
  115.8 12.0 %collective-permute-start.21 = (bf16[2,64,1024]{2,1,0:T(8,128)(2,1)}, bf16[2,64,1024]{2,1,0:T(8,128)(2,1)}, u32[]{:S(2)}, u32[]{:S(2)}) collective-permute-start(bf16[2,64,1024]{2,1,0:T(8,128)(2,1)} %get-tuple-element.94), channel_id=1, source_target_pairs={{0,48},{8,56},{16,32},{24,40},{32,16},{40,24},{48,0},{56,8},{64,11... | collective-permute-start | bytes 786440 | tf_op jit(solution)/shard_map/ppermute | solution.py:69
  118.0 11.3 %collective-permute-start.20 = (bf16[2,64,1024]{2,1,0:T(8,128)(2,1)S(1)}, bf16[2,64,1024]{2,1,0:T(8,128)(2,1)}, u32[]{:S(2)}, u32[]{:S(2)}) collective-permute-start(bf16[2,64,1024]{2,1,0:T(8,128)(2,1)S(1)} %get-tuple-element.95), channel_id=1, source_target_pairs={{0,32},{8,40},{16,48},{24,56},{32,0},{40,8},{48,16},{56,24},{64,96... | collective-permute-start | bytes 786440 | tf_op jit(solution)/shard_map/ppermute | solution.py:69
  118.8 26.7 %copy-start.18 = (bf16[608,384]{1,0:T(8,128)(2,1)S(1)}, bf16[608,384]{1,0:T(8,128)(2,1)}, u32[]{:S(2)}) copy-start(bf16[608,384]{1,0:T(8,128)(2,1)} %copy-done.17) | copy-start | bytes 1400836
  130.6 15.3 %copy-start.24 = (bf16[2,64,1024]{2,1,0:T(8,128)(2,1)}, bf16[2,64,1024]{2,1,0:T(8,128)(2,1)S(1)}, u32[]{:S(2)}) copy-start(bf16[2,64,1024]{2,1,0:T(8,128)(2,1)S(1)} %fusion.43) | copy-start | bytes 786436
  131.3 26.3 %collective-permute-start.22 = (bf16[64,1024]{1,0:T(8,128)(2,1)}, bf16[64,1024]{1,0:T(8,128)(2,1)}, u32[]{:S(2)}, u32[]{:S(2)}) collective-permute-start(bf16[64,1024]{1,0:T(8,128)(2,1)} %dynamic-slice_bitcast_fusion.3), channel_id=1, source_target_pairs={{0,64},{8,72},{16,80},{24,88},{32,96},{40,104},{48,112},{56,120},{... | collective-permute-start | bytes 393224 | tf_op jit(solution)/shard_map/ppermute | solution.py:69
  156.7 2.4 collective-permute-start.8
  157.3 6.8 %copy-start.68 = (bf16[512,1024]{1,0:T(8,128)(2,1)S(1)}, bf16[512,1024]{1,0:T(8,128)(2,1)}, u32[]{:S(2)}) copy-start(bf16[512,1024]{1,0:T(8,128)(2,1)} %param.29) | copy-start | bytes 3145732
  157.3 6.7 %copy-start.77 = (bf16[640,512]{1,0:T(8,128)(2,1)S(1)}, bf16[640,512]{1,0:T(8,128)(2,1)}, u32[]{:S(2)}) copy-start(bf16[640,512]{1,0:T(8,128)(2,1)} %get-tuple-element.128) | copy-start | bytes 1966084
  157.4 1.5 collective-permute-start.1
  158.7 18.4 %collective-permute-start.23 = (bf16[64,1024]{1,0:T(8,128)(2,1)S(1)}, bf16[64,1024]{1,0:T(8,128)(2,1)S(1)}, u32[]{:S(2)}, u32[]{:S(2)}) collective-permute-start(bf16[64,1024]{1,0:T(8,128)(2,1)S(1)} %fusion.46), channel_id=1, source_target_pairs={{0,64},{8,72},{16,80},{24,88},{32,96},{40,104},{48,112},{56,120},{... | collective-permute-start | bytes 393224 | tf_op jit(solution)/shard_map/ppermute | solution.py:69
  158.8 14.6 %collective-permute-start.2 = (f32[64,128]{1,0:T(8,128)S(1)}, f32[64,128]{1,0:T(8,128)S(1)}, u32[]{:S(2)}, u32[]{:S(2)}) collective-permute-start(f32[64,128]{1,0:T(8,128)S(1)} %add.334), channel_id=1, source_target_pairs={{0,16},{8,24},{16,0},{24,8},{32,48},{40,56},{48,32},{56,40},{64,80... | collective-permute-start | bytes 98312 | tf_op jit(solution)/shard_map/ppermute | solution.py:69
  159.9 21.2 %collective-permute-start.9 = (bf16[2,64,512]{2,1,0:T(8,128)(2,1)}, bf16[2,64,512]{2,1,0:T(8,128)(2,1)}, u32[]{:S(2)}, u32[]{:S(2)}) collective-permute-start(bf16[2,64,512]{2,1,0:T(8,128)(2,1)} %get-tuple-element.100), channel_id=1, source_target_pairs={{0,16},{8,24},{16,0},{24,8},{32,48},{40,56},{48,32},{56,40},{64,80... | collective-permute-start | bytes 393224 | tf_op jit(solution)/shard_map/ppermute | solution.py:69
  161.9 21.6 %collective-permute-start.11 = (bf16[2,64,512]{2,1,0:T(8,128)(2,1)}, bf16[2,64,512]{2,1,0:T(8,128)(2,1)}, u32[]{:S(2)}, u32[]{:S(2)}) collective-permute-start(bf16[2,64,512]{2,1,0:T(8,128)(2,1)} %get-tuple-element.101), channel_id=1, source_target_pairs={{0,48},{8,56},{16,32},{24,40},{32,16},{40,24},{48,0},{56,8},{64,11... | collective-permute-start | bytes 393224 | tf_op jit(solution)/shard_map/ppermute | solution.py:69
  164.1 23.1 %collective-permute-start.10 = (bf16[2,64,512]{2,1,0:T(8,128)(2,1)}, bf16[2,64,512]{2,1,0:T(8,128)(2,1)}, u32[]{:S(2)}, u32[]{:S(2)}) collective-permute-start(bf16[2,64,512]{2,1,0:T(8,128)(2,1)} %get-tuple-element.102), channel_id=1, source_target_pairs={{0,32},{8,40},{16,48},{24,56},{32,0},{40,8},{48,16},{56,24},{64,96... | collective-permute-start | bytes 393224 | tf_op jit(solution)/shard_map/ppermute | solution.py:69
  168.4 44.7 %all-to-all-start.4 = ((bf16[8,80,1024]{2,1,0:T(8,128)(2,1)}), bf16[8,80,1024]{2,1,0:T(8,128)(2,1)}, u32[]{:S(2)}, u32[]{:S(2)}) async-start(bf16[8,80,1024]{2,1,0:T(8,128)(2,1)} %bitcast.169), calls=%async_computation.4 | async-start | bytes 2621440 | tf_op jit(solution)/shard_map/all_to_all | solution.py:61
  173.5 5.5 %collective-permute-start.3 = (f32[64,128]{1,0:T(8,128)S(1)}, f32[64,128]{1,0:T(8,128)S(1)}, u32[]{:S(2)}, u32[]{:S(2)}) collective-permute-start(f32[64,128]{1,0:T(8,128)S(1)} %add.335), channel_id=1, source_target_pairs={{0,32},{8,40},{16,48},{24,56},{32,0},{40,8},{48,16},{56,24},{64,96... | collective-permute-start | bytes 98312 | tf_op jit(solution)/shard_map/ppermute | solution.py:69
  178.7 10.8 %collective-permute-start.25 = (bf16[2,64,1024]{2,1,0:T(8,128)(2,1)S(1)}, bf16[2,64,1024]{2,1,0:T(8,128)(2,1)S(1)}, u32[]{:S(2)}, u32[]{:S(2)}) collective-permute-start(bf16[2,64,1024]{2,1,0:T(8,128)(2,1)S(1)} %get-tuple-element.104), channel_id=1, source_target_pairs={{0,32},{8,40},{16,48},{24,56},{32,0},{40,8},{48,16},{56,24},{64,96... | collective-permute-start | bytes 786440 | tf_op jit(solution)/shard_map/ppermute | solution.py:69
  179.0 11.9 %collective-permute-start.24 = (bf16[2,64,1024]{2,1,0:T(8,128)(2,1)S(1)}, bf16[2,64,1024]{2,1,0:T(8,128)(2,1)S(1)}, u32[]{:S(2)}, u32[]{:S(2)}) collective-permute-start(bf16[2,64,1024]{2,1,0:T(8,128)(2,1)S(1)} %get-tuple-element.104), channel_id=1, source_target_pairs={{0,16},{8,24},{16,0},{24,8},{32,48},{40,56},{48,32},{56,40},{64,80... | collective-permute-start | bytes 786440 | tf_op jit(solution)/shard_map/ppermute | solution.py:69
  181.1 11.3 %collective-permute-start.26 = (bf16[2,64,1024]{2,1,0:T(8,128)(2,1)S(1)}, bf16[2,64,1024]{2,1,0:T(8,128)(2,1)S(1)}, u32[]{:S(2)}, u32[]{:S(2)}) collective-permute-start(bf16[2,64,1024]{2,1,0:T(8,128)(2,1)S(1)} %get-tuple-element.104), channel_id=1, source_target_pairs={{0,48},{8,56},{16,32},{24,40},{32,16},{40,24},{48,0},{56,8},{64,11... | collective-permute-start | bytes 786440 | tf_op jit(solution)/shard_map/ppermute | solution.py:69
  183.5 13.0 %collective-permute-start.4 = (f32[64,128]{1,0:T(8,128)S(1)}, f32[64,128]{1,0:T(8,128)S(1)}, u32[]{:S(2)}, u32[]{:S(2)}) collective-permute-start(f32[64,128]{1,0:T(8,128)S(1)} %add.336), channel_id=1, source_target_pairs={{0,64},{8,72},{16,80},{24,88},{32,96},{40,104},{48,112},{56,120},{... | collective-permute-start | bytes 98312 | tf_op jit(solution)/shard_map/ppermute | solution.py:69
  188.3 10.8 %collective-permute-start.12 = (bf16[64,512]{1,0:T(8,128)(2,1)S(1)}, bf16[64,512]{1,0:T(8,128)(2,1)S(1)}, u32[]{:S(2)}, u32[]{:S(2)}) collective-permute-start(bf16[64,512]{1,0:T(8,128)(2,1)S(1)} %dynamic-slice_bitcast_fusion.7), channel_id=1, source_target_pairs={{0,64},{8,72},{16,80},{24,88},{32,96},{40,104},{48,112},{56,120},{... | collective-permute-start | bytes 196616 | tf_op jit(solution)/shard_map/ppermute | solution.py:69
  193.9 20.8 %copy-start.56 = (f32[80]{0:T(128)S(1)}, f32[80]{0:T(128)}, u32[]{:S(2)}) copy-start(f32[80]{0:T(128)} %copy-done.55) | copy-start | bytes 964
  193.9 20.9 %copy-start.66 = (f32[80]{0:T(128)S(1)}, f32[80]{0:T(128)}, u32[]{:S(2)}) copy-start(f32[80]{0:T(128)} %add_rsqrt_fusion.2) | copy-start | bytes 964
  193.9 56.3 %collective-permute-start.27 = (bf16[4,2,64,1024]{3,2,1,0:T(8,128)(2,1)}, bf16[4,2,64,1024]{3,2,1,0:T(8,128)(2,1)}, u32[]{:S(2)}, u32[]{:S(2)}) collective-permute-start(bf16[4,2,64,1024]{3,2,1,0:T(8,128)(2,1)} %get-tuple-element.92), channel_id=1, source_target_pairs={{0,8},{8,0},{16,24},{24,16},{32,40},{40,32},{48,56},{56,48},{64,72... | collective-permute-start | bytes 3145736 | tf_op jit(solution)/shard_map/ppermute | solution.py:69
  196.5 18.6 %copy-start.27 = (f32[64,128]{1,0:T(8,128)}, f32[64,128]{1,0:T(8,128)S(1)}, u32[]{:S(2)}) copy-start(f32[64,128]{1,0:T(8,128)S(1)} %add.337) | copy-start | bytes 98308
  199.1 8.8 %collective-permute-start.13 = (bf16[64,512]{1,0:T(8,128)(2,1)S(1)}, bf16[64,512]{1,0:T(8,128)(2,1)S(1)}, u32[]{:S(2)}, u32[]{:S(2)}) collective-permute-start(bf16[64,512]{1,0:T(8,128)(2,1)S(1)} %fusion.71), channel_id=1, source_target_pairs={{0,64},{8,72},{16,80},{24,88},{32,96},{40,104},{48,112},{56,120},{... | collective-permute-start | bytes 196616 | tf_op jit(solution)/shard_map/ppermute | solution.py:69
  200.6 28.9 %collective-permute-start.5 = (f32[40,128]{1,0:T(8,128)}, f32[40,128]{1,0:T(8,128)}, u32[]{:S(2)}, u32[]{:S(2)}) collective-permute-start(f32[40,128]{1,0:T(8,128)} %slice.217), channel_id=1, source_target_pairs={{0,1},{1,0},{2,3},{3,2},{4,5},{5,4},{6,7},{7,6},{8,9},{9,8},{10,11... | collective-permute-start | bytes 61448 | tf_op jit(solution)/shard_map/ppermute | solution.py:268
  208.6 23.8 %collective-permute-start.15 = (bf16[2,64,512]{2,1,0:T(8,128)(2,1)}, bf16[2,64,512]{2,1,0:T(8,128)(2,1)}, u32[]{:S(2)}, u32[]{:S(2)}) collective-permute-start(bf16[2,64,512]{2,1,0:T(8,128)(2,1)} %get-tuple-element.108), channel_id=1, source_target_pairs={{0,32},{8,40},{16,48},{24,56},{32,0},{40,8},{48,16},{56,24},{64,96... | collective-permute-start | bytes 393224 | tf_op jit(solution)/shard_map/ppermute | solution.py:69
  212.5 19.9 %collective-permute-start.14 = (bf16[2,64,512]{2,1,0:T(8,128)(2,1)}, bf16[2,64,512]{2,1,0:T(8,128)(2,1)}, u32[]{:S(2)}, u32[]{:S(2)}) collective-permute-start(bf16[2,64,512]{2,1,0:T(8,128)(2,1)} %get-tuple-element.108), channel_id=1, source_target_pairs={{0,16},{8,24},{16,0},{24,8},{32,48},{40,56},{48,32},{56,40},{64,80... | collective-permute-start | bytes 393224 | tf_op jit(solution)/shard_map/ppermute | solution.py:69
  212.5 19.9 %collective-permute-start.16 = (bf16[2,64,512]{2,1,0:T(8,128)(2,1)}, bf16[2,64,512]{2,1,0:T(8,128)(2,1)}, u32[]{:S(2)}, u32[]{:S(2)}) collective-permute-start(bf16[2,64,512]{2,1,0:T(8,128)(2,1)} %get-tuple-element.108), channel_id=1, source_target_pairs={{0,48},{8,56},{16,32},{24,40},{32,16},{40,24},{48,0},{56,8},{64,11... | collective-permute-start | bytes 393224 | tf_op jit(solution)/shard_map/ppermute | solution.py:69
  218.2 11.3 %copy-start.28 = (f32[64,128]{1,0:T(8,128)S(1)}, f32[64,128]{1,0:T(8,128)}, u32[]{:S(2)}) copy-start(f32[64,128]{1,0:T(8,128)} %copy-done.27) | copy-start | bytes 98308
  218.2 14.2 %copy-start.26 = (bf16[1,2,64,512]{3,2,1,0:T(8,128)(2,1)S(1)}, bf16[1,2,64,512]{3,2,1,0:T(8,128)(2,1)}, u32[]{:S(2)}) copy-start(bf16[1,2,64,512]{3,2,1,0:T(8,128)(2,1)} %get-tuple-element.107) | copy-start | bytes 393220
  218.2 49.8 %all-to-all-start.5 = ((bf16[8,80,1024]{2,1,0:T(8,128)(2,1)}), bf16[8,80,1024]{2,1,0:T(8,128)(2,1)S(1)}, u32[]{:S(2)}, u32[]{:S(2)}) async-start(bf16[8,80,1024]{2,1,0:T(8,128)(2,1)} %broadcast_in_dim.21), calls=%async_computation.5 | async-start | bytes 2621440 | tf_op jit(solution)/shard_map/all_to_all | solution.py:61
  229.5 20.7 %copy-start.15 = (bf16[1,4,2,64,1024]{4,3,2,1,0:T(8,128)(2,1)S(1)}, bf16[1,4,2,64,1024]{4,3,2,1,0:T(8,128)(2,1)}, u32[]{:S(2)}) copy-start(bf16[1,4,2,64,1024]{4,3,2,1,0:T(8,128)(2,1)} %get-tuple-element.91) | copy-start | bytes 3145732
  230.4 13.9 %collective-permute-start.6 = (f32[40,128]{1,0:T(8,128)S(1)}, f32[40,128]{1,0:T(8,128)S(1)}, u32[]{:S(2)}, u32[]{:S(2)}) collective-permute-start(f32[40,128]{1,0:T(8,128)S(1)} %slice_add_fusion.1), channel_id=1, source_target_pairs={{0,2},{1,3},{2,0},{3,1},{4,6},{5,7},{6,4},{7,5},{8,10},{9,11},{10,... | collective-permute-start | bytes 61448 | tf_op jit(solution)/shard_map/ppermute | solution.py:268
  234.5 21.0 %collective-permute-start.17 = (bf16[4,2,64,512]{3,2,1,0:T(8,128)(2,1)}, bf16[4,2,64,512]{3,2,1,0:T(8,128)(2,1)}, u32[]{:S(2)}, u32[]{:S(2)}) collective-permute-start(bf16[4,2,64,512]{3,2,1,0:T(8,128)(2,1)} %get-tuple-element.99), channel_id=1, source_target_pairs={{0,8},{8,0},{16,24},{24,16},{32,40},{40,32},{48,56},{56,48},{64,72... | collective-permute-start | bytes 1572872 | tf_op jit(solution)/shard_map/ppermute | solution.py:69
  244.3 5.3 %collective-permute-start.7 = (f32[40,128]{1,0:T(8,128)S(1)}, f32[40,128]{1,0:T(8,128)S(1)}, u32[]{:S(2)}, u32[]{:S(2)}) collective-permute-start(f32[40,128]{1,0:T(8,128)S(1)} %add.339), channel_id=1, source_target_pairs={{0,4},{1,5},{2,6},{3,7},{4,0},{5,1},{6,2},{7,3},{8,12},{9,13},{10,... | collective-permute-start | bytes 61448 | tf_op jit(solution)/shard_map/ppermute | solution.py:268
  268.1 3.9 %copy-start.5 = (f32[640,1024]{1,0:T(8,128)S(1)}, f32[640,1024]{1,0:T(8,128)}, u32[]{:S(2)}) copy-start(f32[640,1024]{1,0:T(8,128)} %copy-done.3) | copy-start | bytes 7864324
  268.1 3.9 %copy-start.22 = (bf16[608,1024]{1,0:T(8,128)(2,1)S(1)}, bf16[608,1024]{1,0:T(8,128)(2,1)}, u32[]{:S(2)}) copy-start(bf16[608,1024]{1,0:T(8,128)(2,1)} %all-reduce.7.cloned.1.call-done) | copy-start | bytes 3735556
  268.1 3.9 %copy-start.62 = (f32[1024]{0:T(1024)S(1)}, f32[1024]{0:T(1024)}, u32[]{:S(2)}) copy-start(f32[1024]{0:T(1024)} %param.30) | copy-start | bytes 12292
  (54 other events, 74.9 us)
Sparse Core Ops, SparseCore 0:
  166.1 101.9 all-reduce.6
where the time goes:
time: 284 us; the launch traced here: 281 us
  starting transfers between devices  84.2 us (30%)
  waiting for transfers between devices  67.7 us (24%)
  other arithmetic  39.5 us (14%)
  local copies, waits for them, and re-layouts  38.5 us (14%)
  matrix products  31.8 us (11%)
  between operations  15.4 us (5%)
  Pallas kernels  3.83 us (1%)
    ppermute x25, starting transfers between devices, hop(): return lax.ppermute(a, DP, [(i, i ^ mask) for i in range(16)])  38.5 us
    all_to_all x6, starting transfers between devices, exchange(): return lax.all_to_all(a, axis, 0, 0, tiled=True)  35.3 us
    all_to_all x6, waiting for transfers between devices, exchange(): return lax.all_to_all(a, axis, 0, 0, tiled=True)  27 us
    ppermute x25, waiting for transfers between devices, hop(): return lax.ppermute(a, DP, [(i, i ^ mask) for i in range(16)])  22.1 us
    dot_general x8, matrix products, dot_nt(): lax.dot_general(a, b, (((1,), (1,)), ((), ())), preferred_element_type=F32)  12.1 us
    unnamed x177, local copies, waits for them, and re-layouts  11.9 us
    dot_general x9, matrix products, dot(): return jnp.dot(a, b, preferred_element_type=F32)  11.5 us
    ppermute x3, starting transfers between devices, per_device(): shared = shared + lax.ppermute(shared, T, [(i, i ^ k) for i in range(NT)])  10.4 us
  transfers between devices with their start and end apart: 35, of which 16 were waited for; matrix products, arithmetic and copies ran while one was open for 30% of the time, Pallas kernels for 1%

commit v1 on v0

v1 whole, which is shorter than its diff:
```python
from functools import partial

import jax
import jax.numpy as jnp
from jax import lax
from jax.experimental import pallas as pl
from jax.experimental.pallas import tpu as pltpu
from jax.sharding import PartitionSpec as P

HEADS = 16
HEAD_DIM = 64
EPS = 1e-05
NEG = -1000000000.0
T = "tensor"
DP = "dp"
NT = 8
BLK = 80
PAD = NT * BLK
BF = jnp.bfloat16
F32 = jnp.float32


def norm_stats(values_in):
    row_mean = jnp.mean(values_in, -1, keepdims=True)
    centred = values_in - row_mean
    variance = jnp.mean(centred * centred, -1, keepdims=True)
    recip = lax.rsqrt(variance + EPS)
    return centred * recip, recip


def norm_backward(grad_out, normal_part, recip, gain_vec):
    scaled = grad_out * gain_vec
    return recip * (
        scaled
        - jnp.mean(scaled, -1, keepdims=True)
        - normal_part * jnp.mean(scaled * normal_part, -1, keepdims=True)
    )


def dot(a, b):
    return jnp.dot(a, b, preferred_element_type=F32)


def dot_nt(a, b):
    return lax.dot_general(a, b, (((1,), (1,)), ((), ())), preferred_element_type=F32)


def dot_tn(a, b):
    return lax.dot_general(a, b, (((0,), (0,)), ((), ())), preferred_element_type=F32)


def pad_rows(a):
    return jnp.pad(a, ((0, PAD - a.shape[0]), (0, 0)))


def block_of(a, j):
    return lax.dynamic_slice_in_dim(a, j * BLK, BLK, 0)


def exchange(a, axis):
    return lax.all_to_all(a, axis, 0, 0, tiled=True)


def gather(piece):
    return exchange(jnp.broadcast_to(piece[None], (NT,) + piece.shape), T)


def hop(a, mask):
    return lax.ppermute(a, DP, [(i, i ^ mask) for i in range(16)])


def tensor_hop(a, mask):
    return lax.ppermute(a, T, [(i, i ^ mask) for i in range(NT)])


def pick(a, j, axis=0):
    return lax.dynamic_index_in_dim(a, j, axis, keepdims=False)


def place(dp):
    return dp % 2, (dp // 2) % 4, dp // 8


def z_add(two, got):
    return (two.astype(F32) + got.astype(F32)).astype(BF)


def y_spread(by_z):
    return tuple(hop(by_z, 2 * k) for k in (1, 2, 3))


def spread(where_ref, own_ref, other_ref, left_ref, right_ref):
    chunk = own_ref.shape[2]
    cut = left_ref.shape[1]
    core, y = where_ref[0], where_ref[1]
    for c in range(2):
        for z in range(2):
            for pair in (0, 2):
                parts = []
                for j in (pair, pair + 1):
                    a, b = own_ref[y ^ j, z], other_ref[y ^ j, z]
                    parts.append(jnp.where(core == c, a.astype(F32), b.astype(F32)))
                rows = jnp.concatenate(parts, 0)
                lo = (c * 8 + z * 4 + pair) * chunk
                left_ref[lo : lo + 2 * chunk, :] = rows[:, :cut]
                right_ref[:, lo : lo + 2 * chunk] = jnp.transpose(rows[:, cut:])


def natural_chunks(own, other, dp, cut):
    core, y, _ = place(dp)
    n, chunk, width = 16, own.shape[2], own.shape[3]
    return pl.pallas_call(
        spread,
        out_shape=[shaped(n * chunk, cut), shaped(width - cut, n * chunk)],
        in_specs=[SMEM_SPEC] + whole(2),
        out_specs=whole(2),
        compiler_params=BIG,
        cost_estimate=SHORT,
    )(jnp.stack([core, y]).astype(jnp.int32), *far(own, other))


def attend_forward(
    where_ref, hid_ref, gain_ref, shift_ref, w_ref, qb_ref, vb_ref, srow_ref, scol_ref,
    act_ref, qkv_ref, ctx_ref, send_ref, lse_ref,
):
    seq_len = hid_ref.shape[0]
    for lo, hi in row_blocks(seq_len):
        xhat, _ = norm_stats(hid_ref[lo:hi, :])
        act_ref[lo:hi, :] = (xhat * gain_ref[...] + shift_ref[...]).astype(BF)
    none = jnp.zeros((1, HEAD_DIM), F32)
    cut = HEAD_DIM
    bias = jnp.concatenate(
        [qb_ref[:, :cut], none, vb_ref[:, :cut], qb_ref[:, cut:], none, vb_ref[:, cut:]], 1
    )
    for lo, hi in halves(seq_len):
        qkv_ref[lo:hi, :] = (dot(act_ref[lo:hi, :], w_ref[...]) + bias).astype(BF)
    even = where_ref[1] == 0
    slopes = head_slopes(where_ref)
    for lo, hi in row_blocks(seq_len):
        allowed, distance = masks(lo, hi, srow_ref, scol_ref)
        outs = []
        for h in range(2):
            s = head_scores(qkv_ref, slopes, h, lo, hi, allowed, distance)
            top = jnp.max(s, -1, keepdims=True)
            e = jnp.exp(s - top)
            total = jnp.sum(e, -1, keepdims=True)
            lse_ref[h, lo:hi, :] = top + jnp.log(total)
            p = (e / total).astype(BF)
            outs.append(dot(p, qkv_ref[:hi, head_part(h, 2)]).astype(BF))
        ctx_ref[lo:hi, :] = jnp.concatenate(outs, 1)
        first = jnp.where(even, outs[0].astype(F32), outs[1].astype(F32))
        second = jnp.where(even, outs[1].astype(F32), outs[0].astype(F32))
        both = jnp.concatenate([first, second], 1).astype(BF)
        for i in range(NT):
            send_ref[i, lo:hi, :] = both
    pad = jnp.zeros((PAD - seq_len, 2 * HEAD_DIM), BF)
    for i in range(NT):
        send_ref[i, seq_len:, :] = pad


def row_blocks(n):
    return [(lo, min(lo + 128, n)) for lo in range(0, n, 128)]


def halves(n):
    return [(0, 304), (304, n)]


def head_part(h, c):
    start = (h * 3 + c) * HEAD_DIM
    return slice(start, start + HEAD_DIM)


def head_slopes(where_ref):
    first = (where_ref[0] * 2).astype(F32)
    return [
        jnp.exp2(jnp.full((1, 1), -(8.0 / HEADS), F32) * (first + (h + 1.0))) for h in range(2)
    ]


def masks(lo, hi, srow_ref, scol_ref):
    shape = (hi - lo, hi)
    diff = lax.broadcasted_iota(jnp.int32, shape, 1) - lax.broadcasted_iota(jnp.int32, shape, 0) - lo
    allowed = (diff <= 0) & (scol_ref[lo:hi, :] == srow_ref[:, :hi])
    return allowed, diff.astype(F32)


def head_scores(qkv_ref, slopes, h, lo, hi, allowed, distance):
    raw = dot_nt(qkv_ref[lo:hi, head_part(h, 0)], qkv_ref[:hi, head_part(h, 1)])
    return jnp.where(allowed, raw * HEAD_DIM ** (-0.5) + slopes[h] * distance, NEG)


def attend_backward(
    where_ref, branch_ref, wd_ref, qkv_ref, lse_ref, srow_ref, scol_ref, w_ref,
    grad_ref, part_ref, acc_ref, cg_ref,
):
    seq_len = qkv_ref.shape[0]
    scale = HEAD_DIM ** (-0.5)
    for i in (0, 4):
        rows = jnp.concatenate([branch_ref[j, :BLK, :] for j in range(i, i + 4)], 0)
        cg_ref[i * BLK : (i + 4) * BLK, :] = dot_nt(rows, wd_ref[...]).astype(BF)
    total = branch_ref[0, BLK:, :].astype(F32)
    for j in range(1, NT):
        total = total + branch_ref[j, BLK:, :].astype(F32)
    total = total.astype(BF)
    for j in range(NT):
        part_ref[j, BLK:, :] = total
    acc_ref[...] = jnp.zeros_like(acc_ref)
    slopes = head_slopes(where_ref)
    for lo, hi in row_blocks(seq_len):
        allowed, distance = masks(lo, hi, srow_ref, scol_ref)
        cg_all = cg_ref[lo:hi, :]
        for h in range(2):
            s = head_scores(qkv_ref, slopes, h, lo, hi, allowed, distance)
            p = jnp.exp(s - lse_ref[h, lo:hi, :])
            cg = cg_all[:, h * HEAD_DIM : (h + 1) * HEAD_DIM]
            pg = dot_nt(cg, qkv_ref[:hi, head_part(h, 2)])
            acc_ref[2 * h + 1, :, :hi] += dot_tn(cg, p.astype(BF))
            sg = (p * (pg - jnp.sum(pg * p, -1, keepdims=True))).astype(BF)
            grad_ref[lo:hi, head_part(h, 0)] = (
                dot(sg, qkv_ref[:hi, head_part(h, 1)]) * scale
            ).astype(BF)
            acc_ref[2 * h, :, :hi] += dot_tn(qkv_ref[lo:hi, head_part(h, 0)], sg)
    for h in range(2):
        kg = jnp.transpose(acc_ref[2 * h, :, :]) * scale
        vg = jnp.transpose(acc_ref[2 * h + 1, :, :])
        grad_ref[:, head_part(h, 1)] = kg.astype(BF)
        grad_ref[:, head_part(h, 2)] = vg.astype(BF)
    for h in range(2):
        grad_ref[seq_len:, head_part(h, 0)] = jnp.zeros((PAD - seq_len, HEAD_DIM), BF)
    for lo in range(0, PAD, 320):
        part = dot_nt(grad_ref[lo : lo + 320, :], w_ref[...]).astype(BF)
        for j in range(4):
            part_ref[lo // BLK + j, :BLK, :] = part[j * BLK : (j + 1) * BLK, :]


def feed(
    ctx_ref, own_ref, other_ref, hid_ref, db_ref, gain_ref, shift_ref, up_ref, ub_ref, gin_ref,
    mid_ref, act_ref, gelu_ref, low_ref, part_ref, sum_ref,
):
    step = pl.program_id(0)
    ctx_a = jnp.concatenate([ctx_ref[i, :, :HEAD_DIM] for i in range(NT)], 1)
    ctx_b = jnp.concatenate([ctx_ref[i, :, HEAD_DIM:] for i in range(NT)], 1)
    attn = dot(ctx_a, own_ref[...]) + dot(ctx_b, other_ref[...])
    middle = hid_ref[...] + (attn + db_ref[...])
    mid_ref[...] = middle
    xhat, _ = norm_stats(middle)
    act = (xhat * gain_ref[...] + shift_ref[...]).astype(BF)
    act_ref[...] = act
    x = dot(act, up_ref[...]) + ub_ref[...]
    a = 0.7978845608028654
    t = jnp.tanh(a * (x + 0.044715 * x * x * x))
    gelu_ref[...] = (x * (0.5 * (1.0 + t))).astype(BF)
    slope = 0.5 * (1.0 + t) + 0.5 * x * (1.0 - t * t) * (a * (1.0 + 3 * 0.044715 * x * x))
    low = (gin_ref[...] * slope).astype(BF)
    low_ref[...] = low
    part_ref[...] = dot_nt(low, up_ref[...]).astype(BF)

    @pl.when(step == 0)
    def _():
        sum_ref[...] = jnp.zeros_like(sum_ref)

    sum_ref[...] += jnp.sum(low.astype(F32), 0, keepdims=True)


def norm_two_back(
    me_ref, got_ref, mid_ref, og_ref, gain_ref, mlp_ref, back_ref, send_ref, sum_ref
):
    total = got_ref[0].astype(F32)
    for i in range(1, NT):
        total = total + got_ref[i].astype(F32)
    xhat, recip = norm_stats(mid_ref[...])
    back = norm_backward(total, xhat, recip, gain_ref[...])
    back_ref[...] = back
    branch = (og_ref[...] + back).astype(BF)
    for i in range(NT):
        send_ref[i, :BLK, :] = branch
        send_ref[i, BLK:, :] = mlp_ref[i]
    sum_ref[0:1, :] = jnp.sum(total * xhat, 0, keepdims=True)
    sum_ref[1:2, :] = jnp.sum(total, 0, keepdims=True)
    sum_ref[2:3, :] = jnp.sum(branch.astype(F32), 0, keepdims=True)
    sum_ref[3:8, :] = jnp.zeros((5, sum_ref.shape[1]), F32)


def norm_one_back(me_ref, got_ref, hid_ref, back_ref, gain_ref, vec_ref, send_ref):
    total = got_ref[0].astype(F32)
    for i in range(1, NT):
        total = total + got_ref[i].astype(F32)
    xhat, recip = norm_stats(hid_ref[...])
    delta = (back_ref[...] + norm_backward(total, xhat, recip, gain_ref[...])).astype(BF)
    pairs = [vec_ref[2 * i : 2 * i + 2, :] for i in range(8)]
    vec = jnp.concatenate([jnp.concatenate([p[:1], p[1:]], 1) for p in pairs], 0)
    both = jnp.concatenate(split(vec), 0)
    for i in range(NT):
        send_ref[i, :BLK, :] = delta
        send_ref[i, BLK:, :] = both


def mlp_out(gelu_ref, w_ref, out_ref):
    for lo in (0, 320):
        out_ref[lo : lo + 320, :] = dot(gelu_ref[lo : lo + 320, :], w_ref[...]).astype(BF)


def early_grads(where_ref, act_ref, low_ref, grad_ref, gelu_ref, keep_ref, give_ref, sum_ref):
    half = keep_ref.shape[0]
    for ref, side in ((keep_ref, where_ref[1]), (give_ref, 1 - where_ref[1])):
        cols = pl.ds(pl.multiple_of(side * half, half), half)
        ref[:, :512] = dot_tn(act_ref[:, cols], low_ref[...]).astype(BF)
        ref[:, 512:] = dot_tn(grad_ref[:, cols], gelu_ref[...]).astype(BF)
    sum_ref[...] = jnp.sum(grad_ref[...].astype(F32), 0, keepdims=True)


def split(v):
    high = v.astype(BF)
    return high, (v - high.astype(F32)).astype(BF)


def join(high, low):
    return high.astype(F32) + low.astype(F32)


def late_grads(
    where_ref, act_ref, grad_ref, branch_ref, ctx_ref, part_ref, hid_ref, two_ref, up_ref,
    down_ref, keep_ref, give_ref, vec_ref,
):
    seq_len, width = act_ref.shape
    half = width // 2
    for ref, side in ((keep_ref, where_ref[1]), (give_ref, 1 - where_ref[1])):
        cols = pl.ds(pl.multiple_of(side * half, half), half)
        ref[:half, :384] = dot_tn(act_ref[:, cols], grad_ref[:seq_len, :]).astype(BF)
        branch = jnp.concatenate([branch_ref[j, :BLK, cols] for j in range(NT)], 0)
        ref[:half, 384:] = dot_tn(branch[:seq_len], ctx_ref[...]).astype(BF)
    gain = jnp.zeros((1, width), F32)
    shift = gain
    for j in range(NT):
        lo, hi = j * BLK, min(j * BLK + BLK, seq_len)
        xhat, _ = norm_stats(hid_ref[lo:hi, :])
        part = part_ref[j, : hi - lo, :].astype(F32)
        gain = gain + jnp.sum(part * xhat, 0, keepdims=True)
        shift = shift + jnp.sum(part, 0, keepdims=True)
    sums = jnp.sum(grad_ref[...].astype(F32), 0, keepdims=True)
    last = jnp.concatenate([up_ref[...], sums, jnp.zeros((1, 128), F32)], 1)
    vectors = [
        gain, shift, two_ref[0:1, :], two_ref[1:2, :], two_ref[2:3, :], down_ref[...], last,
        jnp.zeros_like(last),
    ]
    for i, v in enumerate(vectors):
        vec_ref[2 * i : 2 * i + 1, :] = v[:, :half]
        vec_ref[2 * i + 1 : 2 * i + 2, :] = v[:, half:]
    high, low = split(vec_ref[...])
    give_ref[half : half + 16, :] = high
    give_ref[half + 16 :, :] = low


def early_core(where_ref, keep_ref, got_ref, own_ref, one_ref, two_ref, three_ref):
    y = where_ref[2]
    for k, ref in enumerate((own_ref, one_ref, two_ref, three_ref)):
        for z in range(2):
            total = keep_ref[z, y ^ k].astype(F32) + got_ref[z, y ^ k].astype(F32)
            ref[z] = total.astype(BF)


def late_core(
    where_ref, keep_ref, got_ref, vec_ref, own_ref, one_ref, two_ref, three_ref, out_ref
):
    y = where_ref[2]
    chunk = keep_ref.shape[2]
    half = 8 * chunk
    vec = vec_ref[...] + join(got_ref[half : half + 16, :], got_ref[half + 16 :, :])
    out_ref[...] = vec
    parts = split(vec)
    for k, ref in enumerate((own_ref, one_ref, two_ref, three_ref)):
        for z in range(2):
            rows = pl.ds(pl.multiple_of((z * 4 + (y ^ k)) * chunk, chunk), chunk)
            total = keep_ref[z, y ^ k].astype(F32) + got_ref[rows, :].astype(F32)
            ref[z, :chunk, :] = total.astype(BF)
            ref[z, chunk:, :] = parts[z]


def late_y(own_ref, one_ref, two_ref, three_ref, vec_ref, out_ref, sum_ref):
    chunk = own_ref.shape[1] - 16
    vec = vec_ref[...]
    for ref in (one_ref, two_ref, three_ref):
        vec = vec + join(ref[0, chunk:, :], ref[1, chunk:, :])
    sum_ref[...] = vec
    parts = split(vec)
    for z in range(2):
        total = own_ref[z, :chunk, :].astype(F32)
        for ref in (one_ref, two_ref, three_ref):
            total = total + ref[z, :chunk, :].astype(F32)
        out_ref[z, :chunk, :] = total.astype(BF)
        out_ref[z, chunk:, :] = parts[z]


def late_z(own_ref, got_ref, vec_ref, out_ref, sum_ref):
    chunk = out_ref.shape[1]
    sum_ref[...] = vec_ref[...] + join(got_ref[0, chunk:, :], got_ref[1, chunk:, :])
    for z in range(2):
        total = own_ref[z, :chunk, :].astype(F32) + got_ref[z, :chunk, :].astype(F32)
        out_ref[z] = total.astype(BF)


def add_rows(mid_ref, got_ref, bias_ref, out_ref):
    out_ref[...] = mid_ref[...] + (got_ref[0].astype(F32) + bias_ref[...])


def simple(kernel, outs, *args):
    return pl.pallas_call(
        kernel,
        out_shape=outs,
        in_specs=whole(len(args)),
        out_specs=whole(len(outs)),
        compiler_params=BIG,
        cost_estimate=TINY,
    )(*far(*args))


def simple_at(kernel, outs, where, *args, cost=None):
    return pl.pallas_call(
        kernel,
        out_shape=outs,
        in_specs=[SMEM_SPEC] + whole(len(args)),
        out_specs=whole(len(outs)),
        compiler_params=BIG,
        cost_estimate=cost or TINY,
    )(where, *far(*args))


def whole(n):
    return [pl.BlockSpec(memory_space=pltpu.VMEM)] * n


SMEM_SPEC = pl.BlockSpec(memory_space=pltpu.SMEM)
LONG = pl.CostEstimate(flops=4 << 30, bytes_accessed=24 << 20, transcendentals=0)
SHORT = pl.CostEstimate(flops=1 << 20, bytes_accessed=10 << 20, transcendentals=0)
TINY = pl.CostEstimate(flops=1, bytes_accessed=1, transcendentals=0)
BIG = pltpu.CompilerParams(vmem_limit_bytes=40 << 20)


def shaped(*shape, dtype=F32):
    return pltpu.HBM(shape, dtype)


def far(*arrays):
    return [pltpu.with_memory_space_constraint(a, pltpu.HBM) for a in arrays]


def tie(*arrays):
    return lax.optimization_barrier(arrays)


def per_device(
    hidden_in,
    segments,
    ln1_gain,
    ln1_shift,
    qkv_weight,
    query_bias,
    value_bias,
    dense_weight,
    dense_bias,
    ln2_gain,
    ln2_shift,
    up_weight,
    up_bias,
    down_weight,
    down_bias,
    out_grad,
):
    seq_len, width = hidden_in.shape
    me = lax.axis_index(T)
    dp = lax.axis_index(DP)
    core = dp % 2
    row = lambda v: v.reshape(1, -1)
    where = jnp.stack([me, core, (dp // 2) % 4]).astype(jnp.int32)

    half_w = lax.dynamic_slice_in_dim(dense_weight, core * HEAD_DIM, HEAD_DIM, 0)
    own_w = gather(half_w).reshape(NT * HEAD_DIM, width)
    other_w = hop(own_w, 1)

    seg_col = segments.reshape(seq_len, 1)
    act_one, qkv_low, context, ctx_send, lse = pl.pallas_call(
        attend_forward,
        out_shape=[
            shaped(seq_len, width, dtype=BF),
            shaped(seq_len, 384, dtype=BF),
            shaped(seq_len, 128, dtype=BF),
            shaped(NT, PAD, 128, dtype=BF),
            shaped(2, seq_len, 1),
        ],
        in_specs=[SMEM_SPEC] + whole(8),
        out_specs=whole(5),
        compiler_params=BIG,
        cost_estimate=LONG,
    )(
        where,
        *far(hidden_in),
        row(ln1_gain),
        row(ln1_shift),
        *far(qkv_weight),
        row(query_bias),
        row(value_bias),
        segments,
        seg_col,
    )
    ctx_got = exchange(ctx_send, T)

    grad_pad = pad_rows(out_grad.astype(BF))
    gelu_in_grad = dot_nt(grad_pad, down_weight)
    hid_pad = pad_rows(hidden_in)
    out_grad_pad = pad_rows(out_grad)

    rows = 320
    tile = lambda w: pl.BlockSpec((rows, w), lambda i: (i, 0))
    fixed = lambda *shape: pl.BlockSpec(shape, lambda i: (0,) * len(shape))
    middle, act_two, gelu_low, up_low, norm_two_part, up_bias_part = pl.pallas_call(
        feed,
        grid=(PAD // rows,),
        out_shape=[
            shaped(PAD, width),
            shaped(PAD, width, dtype=BF),
            shaped(PAD, 512, dtype=BF),
            shaped(PAD, 512, dtype=BF),
            shaped(PAD, width, dtype=BF),
            shaped(1, 512),
        ],
        in_specs=[
            pl.BlockSpec((NT, rows, 128), lambda i: (0, i, 0)),
            fixed(512, width),
            fixed(512, width),
            tile(width),
            fixed(1, width),
            fixed(1, width),
            fixed(1, width),
            fixed(width, 512),
            fixed(1, 512),
            tile(512),
        ],
        out_specs=[tile(width), tile(width), tile(512), tile(512), tile(width), fixed(1, 512)],
        compiler_params=BIG,
        cost_estimate=TINY,
    )(
        *far(ctx_got, own_w, other_w, hid_pad),
        row(dense_bias),
        row(ln2_gain),
        row(ln2_shift),
        *far(up_weight),
        row(up_bias),
        *far(gelu_in_grad),
    )
    two_got = exchange(norm_two_part.reshape(NT, BLK, width), T)

    mlp_part = pl.pallas_call(
        mlp_out,
        out_shape=shaped(PAD, width, dtype=BF),
        in_specs=whole(2),
        out_specs=whole(1)[0],
        compiler_params=BIG,
        cost_estimate=TINY,
    )(*far(gelu_low, down_weight))
    e_keep, e_give, down_bias_part = simple_at(
        early_grads,
        [shaped(512, width, dtype=BF), shaped(512, width, dtype=BF), shaped(1, width)],
        where, act_two, up_low, grad_pad, gelu_low,
    )
    e_core = hop(e_give, 1)
    two_got, e_core, mlp_part = tie(two_got, e_core, mlp_part)

    mine = pl.BlockSpec((BLK, width), lambda i, m: (m[0], 0))
    zero = lambda *shape: pl.BlockSpec(shape, lambda i, m: (0,) * len(shape))
    back_two, branch_send, sums_two = pl.pallas_call(
        norm_two_back,
        out_shape=[shaped(BLK, width), shaped(NT, 2 * BLK, width, dtype=BF), shaped(8, width)],
        grid_spec=pltpu.PrefetchScalarGridSpec(
            num_scalar_prefetch=1,
            grid=(1,),
            in_specs=[
                zero(NT, BLK, width), mine, mine, zero(1, width), zero(NT, BLK, width)
            ],
            out_specs=[zero(BLK, width), zero(NT, 2 * BLK, width), zero(8, width)],
        ),
        compiler_params=BIG,
        cost_estimate=TINY,
    )(
        me.reshape(1),
        *far(two_got, middle, out_grad_pad),
        row(ln2_gain),
        *far(mlp_part.reshape(NT, BLK, width)),
    )
    branch = exchange(branch_send, T)

    e_core, branch_send = tie(e_core, branch_send)
    e_own, *e_y = simple_at(
        early_core,
        [shaped(2, 64, width, dtype=BF)] * 4,
        where, e_keep.reshape(2, 4, 64, width), e_core.reshape(2, 4, 64, width),
    )
    e_y = tie(*[hop(e, 2 * (k + 1)) for k, e in enumerate(e_y)])
    e_two = sum([e.astype(F32) for e in e_y], e_own.astype(F32)).astype(BF)
    branch, e_two = tie(branch, e_two)
    e_z = hop(e_two, 8)

    qkv_grad_low, norm_one_part = pl.pallas_call(
        attend_backward,
        out_shape=[shaped(PAD, 384, dtype=BF), shaped(NT, 2 * BLK, width, dtype=BF)],
        in_specs=[SMEM_SPEC] + whole(7),
        out_specs=whole(2),
        scratch_shapes=[pltpu.VMEM((4, HEAD_DIM, PAD), F32), pltpu.VMEM((PAD, 128), BF)],
        compiler_params=BIG,
        cost_estimate=LONG,
    )(where, *far(branch, dense_weight, qkv_low, lse), segments, seg_col, *far(qkv_weight))
    norm_one_part, e_z = tie(norm_one_part, e_z)
    one_got = exchange(norm_one_part, T)

    e_three = z_add(e_two, e_z)
    e_y = y_spread(e_three)
    l_keep, l_give, vec = simple_at(
        late_grads,
        [shaped(512, 512, dtype=BF), shaped(544, 512, dtype=BF), shaped(16, 512)],
        where, act_one, qkv_grad_low, branch, context, norm_one_part, hidden_in, sums_two,
        up_bias_part, down_bias_part, cost=LONG,
    )
    l_core, *e_y = tie(hop(l_give, 1), *e_y)
    l_own, *l_y, vec = simple_at(
        late_core,
        [shaped(2, 80, 512, dtype=BF)] * 4 + [shaped(16, 512)],
        where, l_keep.reshape(2, 4, 64, 512), l_core, vec,
    )
    e_by_y = jnp.stack([e_three, *e_y])
    e_core, *l_y = tie(hop(e_by_y, 1), *[hop(p, 2 * (k + 1)) for k, p in enumerate(l_y)])
    l_two, vec = simple(
        late_y, [shaped(2, 80, 512, dtype=BF), shaped(16, 512)], l_own, *l_y, vec
    )
    one_got, l_two, vec, e_core, e_by_y = tie(one_got, l_two, vec, e_core, e_by_y)
    l_three, vec = simple(
        late_z, [shaped(2, 64, 512, dtype=BF), shaped(16, 512)], l_two, hop(l_two, 8), vec
    )

    in_send = pl.pallas_call(
        norm_one_back,
        out_shape=shaped(NT, BLK + 16, width, dtype=BF),
        grid_spec=pltpu.PrefetchScalarGridSpec(
            num_scalar_prefetch=1,
            grid=(1,),
            in_specs=[
                zero(NT, BLK, width), mine, zero(BLK, width), zero(1, width), zero(16, 512)
            ],
            out_specs=zero(NT, BLK + 16, width),
        ),
        compiler_params=BIG,
        cost_estimate=TINY,
    )(me.reshape(1), *far(one_got, hid_pad, back_two), row(ln1_gain), *far(vec))
    in_send, l_three, one_got, e_core, e_by_y = tie(in_send, l_three, one_got, e_core, e_by_y)
    in_got = exchange(in_send, T)

    l_by_y = jnp.stack([l_three, *y_spread(l_three)])
    up_weight_grad, down_weight_grad = natural_chunks(e_by_y, e_core, dp, 512)
    block_out = pl.pallas_call(
        add_rows,
        grid=(NT,),
        out_shape=shaped(seq_len, width),
        in_specs=[
            pl.BlockSpec((BLK, width), lambda i: (i, 0)),
            pl.BlockSpec((1, BLK, width), lambda i: (i, 1, 0)),
            fixed(1, width),
        ],
        out_specs=pl.BlockSpec((BLK, width), lambda i: (i, 0)),
        compiler_params=BIG,
        cost_estimate=SHORT,
    )(*far(middle, one_got), row(down_bias))
    in_got, l_by_y, up_weight_grad, down_weight_grad, block_out = tie(
        in_got, l_by_y, up_weight_grad, down_weight_grad, block_out
    )
    l_core = hop(l_by_y, 1)
    shared = jnp.sum(in_got[:, BLK : BLK + 8].astype(F32) + in_got[:, BLK + 8 :].astype(F32), 0)
    summed = vec.reshape(8, 1024)
    input_grad = out_grad + in_got[:, :BLK].reshape(PAD, width)[:seq_len].astype(F32)
    qkv_weight_grad, dense_weight_grad = natural_chunks(l_by_y, l_core, dp, 384)
    last = summed[6]
    sums = last[512:896].reshape(2, 3, HEAD_DIM)

    return (
        block_out,
        input_grad,
        shared[0],
        shared[1],
        qkv_weight_grad,
        sums[:, 0].reshape(-1),
        sums[:, 2].reshape(-1),
        dense_weight_grad,
        shared[4],
        shared[2],
        shared[3],
        up_weight_grad,
        last[:512],
        down_weight_grad,
        summed[5],
    )


def solution(mesh):
    placed = (
        P("dp", None),
        P("dp", None),
        P(),
        P(),
        P(None, "tensor"),
        P("tensor"),
        P("tensor"),
        P("tensor", None),
        P(),
        P(),
        P(),
        P(None, "tensor"),
        P("tensor"),
        P("tensor", None),
        P(),
        P("dp", None),
    )
    return jax.shard_map(
        per_device,
        mesh=mesh,
        in_specs=placed,
        out_specs=(
            P("dp", None),
            P("dp", None),
            P(),
            P(),
            P(None, "tensor"),
            P("tensor"),
            P("tensor"),
            P("tensor", None),
            P(),
            P(),
            P(),
            P(None, "tensor"),
            P("tensor"),
            P("tensor", None),
            P(),
        ),
        check_vma=False,
    )
```

time: 284 us -> 234 us (0.82)
  Pallas kernels: 3.83 us -> 69.8 us
  other arithmetic: 39.5 us -> 4.61 us
  starting transfers between devices: 84.2 us -> 51.6 us
  matrix products: 31.8 us -> 1.94 us
  local copies, waits for them, and re-layouts: 38.5 us -> 20.6 us
  between operations: 15.4 us -> 0.99 us
  waiting for transfers between devices: 67.7 us -> 81.8 us
    pallas_call x2 -> x15, Pallas kernels: 3.83 us -> 69.8 us  [the longest x4 16.6 us: simple_at(): pl.pallas_call(kernel, out_shape=outs, in_specs=[SMEM_SPEC] + whole(len(a...]
    dot_general x17 -> x0, matrix products: 19.7 us -> none  [the longest x9 11.5 us: dot(): return jnp.dot(a, b, preferred_element_type=F32)]
    ppermute x25 -> x19, waiting for transfers between devices: 22.1 us -> 40.5 us  [hop(): return lax.ppermute(a, DP, [(i, i ^ mask) for i in range(16)])]
    all_to_all x6, waiting for transfers between devices: 27 us -> 41.3 us  [exchange(): return lax.all_to_all(a, axis, 0, 0, tiled=True)]
    ppermute x25 -> x19, starting transfers between devices: 38.5 us -> 24.4 us  [hop(): return lax.ppermute(a, DP, [(i, i ^ mask) for i in range(16)])]
    reduce_sum x16 -> x1, other arithmetic: 12.5 us -> 1.01 us  [per_device(): jnp.sum(in_got[:, BLK:BLK + 8].astype(F32) + in_got[:, BLK + 8:].astype(F...]
    ppermute x3 -> x0, starting transfers between devices: 10.4 us -> none  [per_device(): shared = shared + lax.ppermute(shared, T, [(i, i ^ k) for i in range(NT)])]
    dot_general x8 -> x1, matrix products: 12.1 us -> 1.94 us  [dot_nt(): lax.dot_general(a, b, (((1,), (1,)), ((), ())), preferred_element_type=F32)]
  transfers between devices with their start and end apart: 35 -> 25, of which waited for: 16 -> 15; matrix products, arithmetic and copies ran while one was open for 30% -> 8% of each run, Pallas kernels for 1% -> 21%
where the time goes in v1:
time: 234 us; the launch traced here: 231 us
  waiting for transfers between devices  81.8 us (35%)
  Pallas kernels  69.8 us (30%)
  starting transfers between devices  51.6 us (22%)
  local copies, waits for them, and re-layouts  20.6 us (9%)
  other arithmetic  4.61 us (2%)
    all_to_all x6, waiting for transfers between devices, exchange(): return lax.all_to_all(a, axis, 0, 0, tiled=True)  41.3 us
    ppermute x19, waiting for transfers between devices, hop(): return lax.ppermute(a, DP, [(i, i ^ mask) for i in range(16)])  40.5 us
    all_to_all x6, starting transfers between devices, exchange(): return lax.all_to_all(a, axis, 0, 0, tiled=True)  27.3 us
    ppermute x19, starting transfers between devices, hop(): return lax.ppermute(a, DP, [(i, i ^ mask) for i in range(16)])  24.4 us
    pallas_call x4, Pallas kernels, simple_at(): pl.pallas_call(kernel, out_shape=outs, in_specs=[SMEM_SPEC] + whole(len(a...  16.6 us
    pallas_call x1, Pallas kernels, per_device(): pl.pallas_call(attend_backward, out_shape=[shaped(PAD, 384, dtype=BF), sh...  9.27 us
    pallas_call x1, Pallas kernels, per_device(): pl.pallas_call(feed, grid=(PAD // rows,), out_shape=[shaped(PAD, width),...  9.12 us
    pad x3, local copies, waits for them, and re-layouts, pad_rows(): return jnp.pad(a, ((0, PAD - a.shape[0]), (0, 0)))  7.92 us
  transfers between devices with their start and end apart: 25, of which 15 were waited for; matrix products, arithmetic and copies ran while one was open for 8% of the time, Pallas kernels for 21%

profile of v1, /device:TPU:0, one launch (start us, length us, event | category | flops | bytes accessed | tf_op | source)
XLA Modules:
  0.0 231.4 jit_solution(7115383835043708050)
XLA Ops:
  0.7 0.9 constant_dynamic-slice_fusion
  1.6 1.1 broadcast_in_dim.2
  2.7 5.7 %all-to-all-start.1 = ((bf16[8,64,1024]{2,1,0:T(8,128)(2,1)}), bf16[8,64,1024]{2,1,0:T(8,128)(2,1)S(1)}, u32[]{:S(2)}, u32[]{:S(2)}) async-start(bf16[8,64,1024]{2,1,0:T(8,128)(2,1)} %broadcast_in_dim.2), calls=%async_computation.1 | async-start | bytes 2097152 | tf_op jit(solution)/shard_map/all_to_all | solution.py:61
  8.8 7.9 %shard_map.271 = (bf16[608,1024]{1,0:T(8,128)(2,1)}, bf16[608,384]{1,0:T(8,128)(2,1)}, bf16[608,128]{1,0:T(8,128)(2,1)}, bf16[8,640,128]{2,1,0:T(8,128)(2,1)}, f32[2,608,1]{2,1,0:T(8,128)}) custom-call(s32[3]{0:T(128)S(1)} %pad_add_fusion.where_ref, f32[608,1024]{1,0:T(8,128)} %hid_ref.3, f32[1,1024]{1,0:T(1,128)S(1)} %bitcast.46, f32[1,1024]{1,0:T(1,128)S(1)} %bitcast.50, ...), custom_call_target="tpu_custom_call" | custom-call | flops 4294967296 | bytes 25165824 | tf_op jit(solution)/shard_map/pallas_call | solution.py:482
  16.6 7.7 %all-to-all-done.1 = bf16[8,64,1024]{2,1,0:T(8,128)(2,1)S(1)} async-done(((bf16[8,64,1024]{2,1,0:T(8,128)(2,1)}), bf16[8,64,1024]{2,1,0:T(8,128)(2,1)S(1)}, u32[]{:S(2)}, u32[]{:S(2)}) %all-to-all-start.1) | async-done | bytes 1048608 | tf_op jit(solution)/shard_map/all_to_all | solution.py:61
  24.3 4.3 %all-to-all-start = ((bf16[8,640,128]{2,1,0:T(8,128)(2,1)}), bf16[8,640,128]{2,1,0:T(8,128)(2,1)}, u32[]{:S(2)}, u32[]{:S(2)}) async-start(bf16[8,640,128]{2,1,0:T(8,128)(2,1)} %get-tuple-element.88), calls=%async_computation | async-start | bytes 2621440 | tf_op jit(solution)/shard_map/all_to_all | solution.py:61
  28.7 3.7 %pad.11.hid_ref = f32[640,1024]{1,0:T(8,128)} pad(f32[608,1024]{1,0:T(8,128)} %hid_ref.3, f32[]{:T(128)} %constant.63.clone.1), padding=0_32x0_0 | pad | bytes 5111812 | tf_op jit(solution)/shard_map/jit(_pad)/pad | solution.py:53
  32.6 1.0 copy-done.13
  33.9 1.9 fusion.gin_ref
  35.8 11.2 %all-to-all-done.ctx_ref = bf16[8,640,128]{2,1,0:T(8,128)(2,1)} async-done(((bf16[8,640,128]{2,1,0:T(8,128)(2,1)}), bf16[8,640,128]{2,1,0:T(8,128)(2,1)}, u32[]{:S(2)}, u32[]{:S(2)}) %all-to-all-start) | async-done | bytes 1310752 | tf_op jit(solution)/shard_map/all_to_all | solution.py:61
  47.1 9.1 %shard_map.272 = (f32[640,1024]{1,0:T(8,128)}, bf16[640,1024]{1,0:T(8,128)(2,1)}, bf16[640,512]{1,0:T(8,128)(2,1)}, bf16[640,512]{1,0:T(8,128)(2,1)}, bf16[640,1024]{1,0:T(8,128)(2,1)}, /*index=5*/f32[1,512]{1,0:T(1,128)}) custom-call(bf16[8,640,128]{2,1,0:T(8,128)(2,1)} %all-to-all-done.ctx_ref, bf16[512,1024]{1,0:T(8,128)(2,1)} %bitcast.56, ...), custom_call_target="tpu_custom_call" | custom-call | flops 1 | bytes 1 | tf_op jit(solution)/shard_map/pallas_call | solution.py:516
  56.2 4.3 %all-to-all-start.2 = ((bf16[8,80,1024]{2,1,0:T(8,128)(2,1)}), bf16[8,80,1024]{2,1,0:T(8,128)(2,1)}, u32[]{:S(2)}, u32[]{:S(2)}) async-start(bf16[8,80,1024]{2,1,0:T(8,128)(2,1)} %bitcast.57), calls=%async_computation.2 | async-start | bytes 2621440 | tf_op jit(solution)/shard_map/all_to_all | solution.py:61
  60.5 2.4 %pad.12.grad_ref = bf16[640,1024]{1,0:T(8,128)(2,1)} pad(bf16[608,1024]{1,0:T(8,128)(2,1)} %copy-done.13, bf16[]{:T(256)} %constant.64.clone.1), padding=0_32x0_0 | pad | bytes 2555906 | tf_op jit(solution)/shard_map/jit(_pad)/pad | solution.py:53
  62.9 5.0 %shard_map.273 = (bf16[512,1024]{1,0:T(8,128)(2,1)}, bf16[512,1024]{1,0:T(8,128)(2,1)}, f32[1,1024]{1,0:T(1,128)}) custom-call(s32[3]{0:T(128)S(1)} %pad_add_fusion.where_ref, bf16[640,1024]{1,0:T(8,128)(2,1)} %get-tuple-element.90.act_ref, bf16[640,512]{1,0:T(8,128)(2,1)} %get-tuple-element.91.low_ref, bf16[640,1024]{1,0:T(8,128)(2,1)} %pad.12.grad_ref, ...), custom_call_target="tpu_custom_call" | custom-call | flops 1 | bytes 1 | tf_op jit(solution)/shard_map/pallas_call | solution.py:419
  67.9 1.8 pad.13.og_ref
  69.7 3.3 %shard_map.274 = bf16[640,1024]{1,0:T(8,128)(2,1)} custom-call(bf16[640,512]{1,0:T(8,128)(2,1)} %get-tuple-element.92.gelu_ref, bf16[512,1024]{1,0:T(8,128)(2,1)} %w_ref.4), custom_call_target="tpu_custom_call" | custom-call | flops 1 | bytes 1 | tf_op jit(solution)/shard_map/pallas_call | solution.py:553
  73.0 5.3 %all-to-all-done.2.got_ref = bf16[8,80,1024]{2,1,0:T(8,128)(2,1)} async-done(((bf16[8,80,1024]{2,1,0:T(8,128)(2,1)}), bf16[8,80,1024]{2,1,0:T(8,128)(2,1)}, u32[]{:S(2)}, u32[]{:S(2)}) %all-to-all-start.2) | async-done | bytes 1310752 | tf_op jit(solution)/shard_map/all_to_all | solution.py:61
  78.4 4.2 %shard_map.275 = (f32[80,1024]{1,0:T(8,128)}, bf16[8,160,1024]{2,1,0:T(8,128)(2,1)}, f32[8,1024]{1,0:T(8,128)}) custom-call(s32[1]{0:T(128)} %bitcast.me_ref, bf16[8,80,1024]{2,1,0:T(8,128)(2,1)} %all-to-all-done.2.got_ref, f32[640,1024]{1,0:T(8,128)} %get-tuple-element.95.mid_ref, f32[640,1024]{1,0:T(8,128)} %pad.13.og_ref, f32[1,1024]{1,0:T(1,128)S(1)} %bitcast.42, ...), custom_call_target="tpu_custom_call" | custom-call | flops 1 | bytes 1 | tf_op jit(solution)/shard_map/pallas_call | solution.py:571
  82.5 3.6 %all-to-all-start.3 = ((bf16[8,160,1024]{2,1,0:T(8,128)(2,1)}), bf16[8,160,1024]{2,1,0:T(8,128)(2,1)S(1)}, u32[]{:S(2)}, u32[]{:S(2)}) async-start(bf16[8,160,1024]{2,1,0:T(8,128)(2,1)} %get-tuple-element.97), calls=%async_computation.3 | async-start | bytes 5242880 | tf_op jit(solution)/shard_map/all_to_all | solution.py:61
  86.2 2.7 %shard_map.276 = (bf16[2,64,1024]{2,1,0:T(8,128)(2,1)}, bf16[2,64,1024]{2,1,0:T(8,128)(2,1)}, bf16[2,64,1024]{2,1,0:T(8,128)(2,1)}, bf16[2,64,1024]{2,1,0:T(8,128)(2,1)}) custom-call(s32[3]{0:T(128)S(1)} %pad_add_fusion.where_ref, bf16[2,4,64,1024]{3,2,1,0:T(8,128)(2,1)} %bitcast.58, bf16[2,4,64,1024]{3,2,1,0:T(8,128)(2,1)} %bitcast.16.got_ref), custom_call_target="tpu_custom_call" | custom-call | flops 1 | bytes 1 | tf_op jit(solution)/shard_map/pallas_call | solution.py:419
  88.8 1.6 collective-permute-start.2
  90.4 2.9 %collective-permute-start.3 = (bf16[2,64,1024]{2,1,0:T(8,128)(2,1)}, bf16[2,64,1024]{2,1,0:T(8,128)(2,1)S(1)}, u32[]{:S(2)}, u32[]{:S(2)}) collective-permute-start(bf16[2,64,1024]{2,1,0:T(8,128)(2,1)} %get-tuple-element.103), channel_id=1, source_target_pairs={{0,32},{8,40},{16,48},{24,56},{32,0},{40,8},{48,16},{56,24},{64,96... | collective-permute-start | bytes 786440 | tf_op jit(solution)/shard_map/ppermute | solution.py:69
  93.5 4.8 %collective-permute-done.2 = bf16[2,64,1024]{2,1,0:T(8,128)(2,1)S(1)} collective-permute-done((bf16[2,64,1024]{2,1,0:T(8,128)(2,1)}, bf16[2,64,1024]{2,1,0:T(8,128)(2,1)S(1)}, u32[]{:S(2)}, u32[]{:S(2)}) %collective-permute-start.2) | collective-permute-done | bytes 262176 | tf_op jit(solution)/shard_map/ppermute | solution.py:69
  98.3 5.5 %collective-permute-done.3 = bf16[2,64,1024]{2,1,0:T(8,128)(2,1)S(1)} collective-permute-done((bf16[2,64,1024]{2,1,0:T(8,128)(2,1)}, bf16[2,64,1024]{2,1,0:T(8,128)(2,1)S(1)}, u32[]{:S(2)}, u32[]{:S(2)}) %collective-permute-start.3) | collective-permute-done | bytes 262176 | tf_op jit(solution)/shard_map/ppermute | solution.py:69
  103.8 2.6 %collective-permute-done.4 = bf16[2,64,1024]{2,1,0:T(8,128)(2,1)S(1)} collective-permute-done((bf16[2,64,1024]{2,1,0:T(8,128)(2,1)}, bf16[2,64,1024]{2,1,0:T(8,128)(2,1)S(1)}, u32[]{:S(2)}, u32[]{:S(2)}) %collective-permute-start.4) | collective-permute-done | bytes 262176 | tf_op jit(solution)/shard_map/ppermute | solution.py:69
  106.4 1.1 add_convert_fusion.1
  107.5 15.2 %all-to-all-done.3.branch_ref = bf16[8,160,1024]{2,1,0:T(8,128)(2,1)S(1)} async-done(((bf16[8,160,1024]{2,1,0:T(8,128)(2,1)}), bf16[8,160,1024]{2,1,0:T(8,128)(2,1)S(1)}, u32[]{:S(2)}, u32[]{:S(2)}) %all-to-all-start.3) | async-done | bytes 2621472 | tf_op jit(solution)/shard_map/all_to_all | solution.py:61
  122.8 3.6 %collective-permute-start.5 = (bf16[2,64,1024]{2,1,0:T(8,128)(2,1)S(1)}, bf16[2,64,1024]{2,1,0:T(8,128)(2,1)S(1)}, u32[]{:S(2)}, u32[]{:S(2)}) collective-permute-start(bf16[2,64,1024]{2,1,0:T(8,128)(2,1)S(1)} %add_convert_fusion.1), channel_id=1, source_target_pairs={{0,64},{8,72},{16,80},{24,88},{32,96},{40,104},{48,112},{56,120},{... | collective-permute-start | bytes 786440 | tf_op jit(solution)/shard_map/ppermute | solution.py:69
  126.3 9.3 %shard_map.277 = (bf16[640,384]{1,0:T(8,128)(2,1)}, bf16[8,160,1024]{2,1,0:T(8,128)(2,1)}) custom-call(s32[3]{0:T(128)S(1)} %pad_add_fusion.where_ref, bf16[8,160,1024]{2,1,0:T(8,128)(2,1)} %copy-done.16, bf16[128,1024]{1,0:T(8,128)(2,1)} %wd_ref.1, bf16[608,384]{1,0:T(8,128)(2,1)} %get-tuple-element.109.qkv_ref, f32[2,608,1]{2,1,0:T(8,128)} %get-tuple-element.110.lse_ref, ...), custom_call_target="tpu_custom_call" | custom-call | flops 4294967296 | bytes 25165824 | tf_op jit(solution)/shard_map/pallas_call | solution.py:603
  135.6 3.6 %all-to-all-start.4 = ((bf16[8,160,1024]{2,1,0:T(8,128)(2,1)}), bf16[8,160,1024]{2,1,0:T(8,128)(2,1)S(1)}, u32[]{:S(2)}, u32[]{:S(2)}) async-start(bf16[8,160,1024]{2,1,0:T(8,128)(2,1)} %get-tuple-element.113.part_ref), calls=%async_computation.4 | async-start | bytes 5242880 | tf_op jit(solution)/shard_map/all_to_all | solution.py:61
  139.2 6.9 %shard_map.278 = (bf16[512,512]{1,0:T(8,128)(2,1)}, bf16[544,512]{1,0:T(8,128)(2,1)}, f32[16,512]{1,0:T(8,128)}) custom-call(s32[3]{0:T(128)S(1)} %pad_add_fusion.where_ref, bf16[608,1024]{1,0:T(8,128)(2,1)} %get-tuple-element.114.act_ref, bf16[640,384]{1,0:T(8,128)(2,1)} %get-tuple-element.115.grad_ref, bf16[8,160,1024]{2,1,0:T(8,128)(2,1)} %copy-done.16, ...), custom_call_target="tpu_custom_call" | custom-call | flops 4294967296 | bytes 25165824 | tf_op jit(solution)/shard_map/pallas_call | solution.py:419
  146.2 1.6 collective-permute-start.7
  147.8 2.9 %collective-permute-start.8 = (bf16[2,64,1024]{2,1,0:T(8,128)(2,1)S(1)}, bf16[2,64,1024]{2,1,0:T(8,128)(2,1)S(1)}, u32[]{:S(2)}, u32[]{:S(2)}) collective-permute-start(bf16[2,64,1024]{2,1,0:T(8,128)(2,1)S(1)} %add_convert_fusion), channel_id=1, source_target_pairs={{0,32},{8,40},{16,48},{24,56},{32,0},{40,8},{48,16},{56,24},{64,96... | collective-permute-start | bytes 786440 | tf_op jit(solution)/shard_map/ppermute | solution.py:69
  151.0 4.4 %collective-permute-done.7 = bf16[2,64,1024]{2,1,0:T(8,128)(2,1)S(1)} collective-permute-done((bf16[2,64,1024]{2,1,0:T(8,128)(2,1)S(1)}, bf16[2,64,1024]{2,1,0:T(8,128)(2,1)S(1)}, u32[]{:S(2)}, u32[]{:S(2)}) %collective-permute-start.7) | collective-permute-done | bytes 262176 | tf_op jit(solution)/shard_map/ppermute | solution.py:69
  155.4 7.8 %collective-permute-done.8 = bf16[2,64,1024]{2,1,0:T(8,128)(2,1)S(1)} collective-permute-done((bf16[2,64,1024]{2,1,0:T(8,128)(2,1)S(1)}, bf16[2,64,1024]{2,1,0:T(8,128)(2,1)S(1)}, u32[]{:S(2)}, u32[]{:S(2)}) %collective-permute-start.8) | collective-permute-done | bytes 262176 | tf_op jit(solution)/shard_map/ppermute | solution.py:69
  163.1 2.6 %collective-permute-done.9 = bf16[2,64,1024]{2,1,0:T(8,128)(2,1)S(1)} collective-permute-done((bf16[2,64,1024]{2,1,0:T(8,128)(2,1)S(1)}, bf16[2,64,1024]{2,1,0:T(8,128)(2,1)S(1)}, u32[]{:S(2)}, u32[]{:S(2)}) %collective-permute-start.9) | collective-permute-done | bytes 262176 | tf_op jit(solution)/shard_map/ppermute | solution.py:69
  166.5 2.1 shard_map.279
  168.6 1.7 collective-permute-start.12
  170.4 3.0 %collective-permute-start.13 = (bf16[2,80,512]{2,1,0:T(8,128)(2,1)}, bf16[2,80,512]{2,1,0:T(8,128)(2,1)S(1)}, u32[]{:S(2)}, u32[]{:S(2)}) collective-permute-start(bf16[2,80,512]{2,1,0:T(8,128)(2,1)} %get-tuple-element.131), channel_id=1, source_target_pairs={{0,48},{8,56},{16,32},{24,40},{32,16},{40,24},{48,0},{56,8},{64,11... | collective-permute-start | bytes 491528 | tf_op jit(solution)/shard_map/ppermute | solution.py:69
  173.3 2.6 %collective-permute-done.11.one_ref = bf16[2,80,512]{2,1,0:T(8,128)(2,1)S(1)} collective-permute-done((bf16[2,80,512]{2,1,0:T(8,128)(2,1)}, bf16[2,80,512]{2,1,0:T(8,128)(2,1)S(1)}, u32[]{:S(2)}, u32[]{:S(2)}) %collective-permute-start.11) | collective-permute-done | bytes 163872 | tf_op jit(solution)/shard_map/ppermute | solution.py:69
  175.9 2.3 collective-permute-done.12.two_ref
  178.2 2.5 %collective-permute-done.13.three_ref = bf16[2,80,512]{2,1,0:T(8,128)(2,1)S(1)} collective-permute-done((bf16[2,80,512]{2,1,0:T(8,128)(2,1)}, bf16[2,80,512]{2,1,0:T(8,128)(2,1)S(1)}, u32[]{:S(2)}, u32[]{:S(2)}) %collective-permute-start.13) | collective-permute-done | bytes 163872 | tf_op jit(solution)/shard_map/ppermute | solution.py:69
  180.7 0.6 copy-done.25
  181.8 1.9 shard_map.280
  183.7 1.6 collective-permute-start.14
  185.3 5.5 %collective-permute-done.14.got_ref = bf16[2,80,512]{2,1,0:T(8,128)(2,1)S(1)} collective-permute-done((bf16[2,80,512]{2,1,0:T(8,128)(2,1)}, bf16[2,80,512]{2,1,0:T(8,128)(2,1)S(1)}, u32[]{:S(2)}, u32[]{:S(2)}) %collective-permute-start.14) | collective-permute-done | bytes 163872 | tf_op jit(solution)/shard_map/ppermute | solution.py:69
  190.9 0.7 copy-done.22
  191.5 1.7 shard_map.281
  193.2 3.1 %shard_map.282 = bf16[8,96,1024]{2,1,0:T(8,128)(2,1)} custom-call(s32[1]{0:T(128)} %bitcast.me_ref, bf16[8,160,1024]{2,1,0:T(8,128)(2,1)} %copy-done.10, f32[640,1024]{1,0:T(8,128)} %pad.11.hid_ref, f32[80,1024]{1,0:T(8,128)} %get-tuple-element.140.back_ref, f32[1,1024]{1,0:T(1,128)S(1)} %bitcast.47, f32[16,512]{1,0:T(8,128)} %get-tuple-element.143.vec_ref), custom_call_target="tpu_custom_call" | custom-call | flops 1 | bytes 1 | tf_op jit(solution)/shard_map/pallas_call | solution.py:639
  196.3 5.7 %all-to-all-start.5 = ((bf16[8,96,1024]{2,1,0:T(8,128)(2,1)}), bf16[8,96,1024]{2,1,0:T(8,128)(2,1)}, u32[]{:S(2)}, u32[]{:S(2)}) async-start(bf16[8,96,1024]{2,1,0:T(8,128)(2,1)} %shard_map.282), calls=%async_computation.5 | async-start | bytes 3145728 | tf_op jit(solution)/shard_map/all_to_all | solution.py:61
  202.2 4.4 %collective-permute-start.16 = (bf16[2,64,512]{2,1,0:T(8,128)(2,1)S(1)}, bf16[2,64,512]{2,1,0:T(8,128)(2,1)S(1)}, u32[]{:S(2)}, u32[]{:S(2)}) collective-permute-start(bf16[2,64,512]{2,1,0:T(8,128)(2,1)S(1)} %copy-done.26), channel_id=1, source_target_pairs={{0,32},{8,40},{16,48},{24,56},{32,0},{40,8},{48,16},{56,24},{64,96... | collective-permute-start | bytes 393224 | tf_op jit(solution)/shard_map/ppermute | solution.py:69
  206.9 0.8 slice_bitcast_fusion
  207.7 1.3 slice.64
  209.1 0.6 reshape_squeeze.6
  210.3 0.6 copy.34
  210.9 6.1 %shard_map.284 = f32[608,1024]{1,0:T(8,128)} custom-call(f32[640,1024]{1,0:T(8,128)} %get-tuple-element.95.mid_ref, bf16[8,160,1024]{2,1,0:T(8,128)(2,1)} %copy-done.10, f32[1,1024]{1,0:T(1,128)S(1)} %bitcast.45), custom_call_target="tpu_custom_call" | custom-call | flops 1048576 | bytes 10485760 | tf_op jit(solution)/shard_map/pallas_call | solution.py:658
  217.0 4.0 %shard_map.283 = (f32[1024,512]{1,0:T(8,128)}, f32[512,1024]{1,0:T(8,128)}) custom-call(s32[2]{0:T(128)S(1)} %pad_add_fusion.1.where_ref, bf16[4,2,64,1024]{3,2,1,0:T(8,128)(2,1)} %copy-done.15, bf16[4,2,64,1024]{3,2,1,0:T(8,128)(2,1)} %copy-done.19), custom_call_target="tpu_custom_call" | custom-call | flops 1048576 | bytes 10485760 | tf_op jit(solution)/shard_map/pallas_call | solution.py:112
  221.0 1.8 all-to-all-done.5
  222.8 1.4 slice.51
  224.2 1.0 add_reduce_fusion
  225.3 0.6 fusion.2
  226.0 1.9 convert_add_fusion
  227.8 0.8 copy-done.21
  228.7 2.7 %shard_map.285 = (f32[1024,384]{1,0:T(8,128)}, f32[128,1024]{1,0:T(8,128)}) custom-call(s32[2]{0:T(128)S(1)} %pad_add_fusion.1.where_ref, bf16[4,2,64,512]{3,2,1,0:T(8,128)(2,1)} %copy-done.17, bf16[4,2,64,512]{3,2,1,0:T(8,128)(2,1)} %copy-done.21), custom_call_target="tpu_custom_call" | custom-call | flops 1048576 | bytes 10485760 | tf_op jit(solution)/shard_map/pallas_call | solution.py:112
  (82 shorter events, 3.9 us)
Async XLA Ops:
  1.6 6.9 %copy-start.5 = (s32[1,608]{1,0:T(1,128)S(1)}, s32[1,608]{1,0:T(1,128)}, u32[]{:S(2)}) copy-start(s32[1,608]{1,0:T(1,128)} %srow_ref.3) | copy-start | bytes 7300
  1.6 7.1 %copy-start.4 = (f32[1024]{0:T(1024)S(1)}, f32[1024]{0:T(1024)}, u32[]{:S(2)}) copy-start(f32[1024]{0:T(1024)} %param.18) | copy-start | bytes 12292
  1.6 7.1 %copy-start.7 = (f32[1024]{0:T(1024)S(1)}, f32[1024]{0:T(1024)}, u32[]{:S(2)}) copy-start(f32[1024]{0:T(1024)} %param.19) | copy-start | bytes 12292
  1.6 7.1 %copy-start.8 = (f32[128]{0:T(128)S(1)}, f32[128]{0:T(128)}, u32[]{:S(2)}) copy-start(f32[128]{0:T(128)} %param.21) | copy-start | bytes 1540
  1.6 7.1 %copy-start.9 = (f32[128]{0:T(128)S(1)}, f32[128]{0:T(128)}, u32[]{:S(2)}) copy-start(f32[128]{0:T(128)} %param.22) | copy-start | bytes 1540
  2.7 21.6 %all-to-all-start.1 = ((bf16[8,64,1024]{2,1,0:T(8,128)(2,1)}), bf16[8,64,1024]{2,1,0:T(8,128)(2,1)S(1)}, u32[]{:S(2)}, u32[]{:S(2)}) async-start(bf16[8,64,1024]{2,1,0:T(8,128)(2,1)} %broadcast_in_dim.2), calls=%async_computation.1 | async-start | bytes 2097152 | tf_op jit(solution)/shard_map/all_to_all | solution.py:61
  24.3 4.3 %copy-start.14 = (bf16[8,64,1024]{2,1,0:T(8,128)(2,1)}, bf16[8,64,1024]{2,1,0:T(8,128)(2,1)S(1)}, u32[]{:S(2)}) copy-start(bf16[8,64,1024]{2,1,0:T(8,128)(2,1)S(1)} %all-to-all-done.1) | copy-start | bytes 3145732
  24.3 22.7 %all-to-all-start = ((bf16[8,640,128]{2,1,0:T(8,128)(2,1)}), bf16[8,640,128]{2,1,0:T(8,128)(2,1)}, u32[]{:S(2)}, u32[]{:S(2)}) async-start(bf16[8,640,128]{2,1,0:T(8,128)(2,1)} %get-tuple-element.88), calls=%async_computation | async-start | bytes 2621440 | tf_op jit(solution)/shard_map/all_to_all | solution.py:61
  28.6 3.8 %copy-start.11 = (f32[608,1024]{1,0:T(8,128)S(1)}, f32[608,1024]{1,0:T(8,128)}, u32[]{:S(2)}) copy-start(f32[608,1024]{1,0:T(8,128)} %param.31) | copy-start | bytes 7471108
  28.6 18.4 %collective-permute-start = (bf16[512,1024]{1,0:T(8,128)(2,1)}, bf16[512,1024]{1,0:T(8,128)(2,1)}, u32[]{:S(2)}, u32[]{:S(2)}) collective-permute-start(bf16[512,1024]{1,0:T(8,128)(2,1)} %bitcast.55), channel_id=1, source_target_pairs={{0,8},{8,0},{16,24},{24,16},{32,40},{40,32},{48,56},{56,48},{64,72... | collective-permute-start | bytes 3145736 | tf_op jit(solution)/shard_map/ppermute | solution.py:69
  32.4 1.5 copy-start.18
  32.6 1.0 copy-start.13
  33.9 13.1 %copy-start = (f32[1024]{0:T(1024)S(1)}, f32[1024]{0:T(1024)}, u32[]{:S(2)}) copy-start(f32[1024]{0:T(1024)} %param.25) | copy-start | bytes 12292
  33.9 13.1 %copy-start.1 = (f32[1024]{0:T(1024)S(1)}, f32[1024]{0:T(1024)}, u32[]{:S(2)}) copy-start(f32[1024]{0:T(1024)} %param.24) | copy-start | bytes 12292
  33.9 13.1 %copy-start.2 = (f32[1024]{0:T(1024)S(1)}, f32[1024]{0:T(1024)}, u32[]{:S(2)}) copy-start(f32[1024]{0:T(1024)} %param.26) | copy-start | bytes 12292
  33.9 13.2 %copy-start.6 = (f32[512]{0:T(512)S(1)}, f32[512]{0:T(512)}, u32[]{:S(2)}) copy-start(f32[512]{0:T(512)} %param.28) | copy-start | bytes 6148
  56.2 22.2 %all-to-all-start.2 = ((bf16[8,80,1024]{2,1,0:T(8,128)(2,1)}), bf16[8,80,1024]{2,1,0:T(8,128)(2,1)}, u32[]{:S(2)}, u32[]{:S(2)}) async-start(bf16[8,80,1024]{2,1,0:T(8,128)(2,1)} %bitcast.57), calls=%async_computation.2 | async-start | bytes 2621440 | tf_op jit(solution)/shard_map/all_to_all | solution.py:61
  67.9 5.1 %collective-permute-start.1 = (bf16[512,1024]{1,0:T(8,128)(2,1)}, bf16[512,1024]{1,0:T(8,128)(2,1)}, u32[]{:S(2)}, u32[]{:S(2)}) collective-permute-start(bf16[512,1024]{1,0:T(8,128)(2,1)} %get-tuple-element.93), channel_id=1, source_target_pairs={{0,8},{8,0},{16,24},{24,16},{32,40},{40,32},{48,56},{56,48},{64,72... | collective-permute-start | bytes 3145736 | tf_op jit(solution)/shard_map/ppermute | solution.py:69
  82.5 40.2 %all-to-all-start.3 = ((bf16[8,160,1024]{2,1,0:T(8,128)(2,1)}), bf16[8,160,1024]{2,1,0:T(8,128)(2,1)S(1)}, u32[]{:S(2)}, u32[]{:S(2)}) async-start(bf16[8,160,1024]{2,1,0:T(8,128)(2,1)} %get-tuple-element.97), calls=%async_computation.3 | async-start | bytes 5242880 | tf_op jit(solution)/shard_map/all_to_all | solution.py:61
  88.8 9.5 %collective-permute-start.2 = (bf16[2,64,1024]{2,1,0:T(8,128)(2,1)}, bf16[2,64,1024]{2,1,0:T(8,128)(2,1)S(1)}, u32[]{:S(2)}, u32[]{:S(2)}) collective-permute-start(bf16[2,64,1024]{2,1,0:T(8,128)(2,1)} %get-tuple-element.102), channel_id=1, source_target_pairs={{0,16},{8,24},{16,0},{24,8},{32,48},{40,56},{48,32},{56,40},{64,80... | collective-permute-start | bytes 786440 | tf_op jit(solution)/shard_map/ppermute | solution.py:69
  90.4 13.4 %collective-permute-start.3 = (bf16[2,64,1024]{2,1,0:T(8,128)(2,1)}, bf16[2,64,1024]{2,1,0:T(8,128)(2,1)S(1)}, u32[]{:S(2)}, u32[]{:S(2)}) collective-permute-start(bf16[2,64,1024]{2,1,0:T(8,128)(2,1)} %get-tuple-element.103), channel_id=1, source_target_pairs={{0,32},{8,40},{16,48},{24,56},{32,0},{40,8},{48,16},{56,24},{64,96... | collective-permute-start | bytes 786440 | tf_op jit(solution)/shard_map/ppermute | solution.py:69
  93.3 13.1 %collective-permute-start.4 = (bf16[2,64,1024]{2,1,0:T(8,128)(2,1)}, bf16[2,64,1024]{2,1,0:T(8,128)(2,1)S(1)}, u32[]{:S(2)}, u32[]{:S(2)}) collective-permute-start(bf16[2,64,1024]{2,1,0:T(8,128)(2,1)} %get-tuple-element.104), channel_id=1, source_target_pairs={{0,48},{8,56},{16,32},{24,40},{32,16},{40,24},{48,0},{56,8},{64,11... | collective-permute-start | bytes 786440 | tf_op jit(solution)/shard_map/ppermute | solution.py:69
  122.8 3.6 %copy-start.16 = (bf16[8,160,1024]{2,1,0:T(8,128)(2,1)}, bf16[8,160,1024]{2,1,0:T(8,128)(2,1)S(1)}, u32[]{:S(2)}) copy-start(bf16[8,160,1024]{2,1,0:T(8,128)(2,1)S(1)} %all-to-all-done.3.branch_ref) | copy-start | bytes 7864324
  122.8 12.9 %collective-permute-start.5 = (bf16[2,64,1024]{2,1,0:T(8,128)(2,1)S(1)}, bf16[2,64,1024]{2,1,0:T(8,128)(2,1)S(1)}, u32[]{:S(2)}, u32[]{:S(2)}) collective-permute-start(bf16[2,64,1024]{2,1,0:T(8,128)(2,1)S(1)} %add_convert_fusion.1), channel_id=1, source_target_pairs={{0,64},{8,72},{16,80},{24,88},{32,96},{40,104},{48,112},{56,120},{... | collective-permute-start | bytes 786440 | tf_op jit(solution)/shard_map/ppermute | solution.py:69
  135.6 48.1 %all-to-all-start.4 = ((bf16[8,160,1024]{2,1,0:T(8,128)(2,1)}), bf16[8,160,1024]{2,1,0:T(8,128)(2,1)S(1)}, u32[]{:S(2)}, u32[]{:S(2)}) async-start(bf16[8,160,1024]{2,1,0:T(8,128)(2,1)} %get-tuple-element.113.part_ref), calls=%async_computation.4 | async-start | bytes 5242880 | tf_op jit(solution)/shard_map/all_to_all | solution.py:61
  146.1 19.6 %collective-permute-start.6 = (bf16[544,512]{1,0:T(8,128)(2,1)}, bf16[544,512]{1,0:T(8,128)(2,1)S(1)}, u32[]{:S(2)}, u32[]{:S(2)}) collective-permute-start(bf16[544,512]{1,0:T(8,128)(2,1)} %get-tuple-element.121), channel_id=1, source_target_pairs={{0,8},{8,0},{16,24},{24,16},{32,40},{40,32},{48,56},{56,48},{64,72... | collective-permute-start | bytes 1671176 | tf_op jit(solution)/shard_map/ppermute | solution.py:69
  146.2 9.2 %collective-permute-start.7 = (bf16[2,64,1024]{2,1,0:T(8,128)(2,1)S(1)}, bf16[2,64,1024]{2,1,0:T(8,128)(2,1)S(1)}, u32[]{:S(2)}, u32[]{:S(2)}) collective-permute-start(bf16[2,64,1024]{2,1,0:T(8,128)(2,1)S(1)} %add_convert_fusion), channel_id=1, source_target_pairs={{0,16},{8,24},{16,0},{24,8},{32,48},{40,56},{48,32},{56,40},{64,80... | collective-permute-start | bytes 786440 | tf_op jit(solution)/shard_map/ppermute | solution.py:69
  147.8 15.3 %collective-permute-start.8 = (bf16[2,64,1024]{2,1,0:T(8,128)(2,1)S(1)}, bf16[2,64,1024]{2,1,0:T(8,128)(2,1)S(1)}, u32[]{:S(2)}, u32[]{:S(2)}) collective-permute-start(bf16[2,64,1024]{2,1,0:T(8,128)(2,1)S(1)} %add_convert_fusion), channel_id=1, source_target_pairs={{0,32},{8,40},{16,48},{24,56},{32,0},{40,8},{48,16},{56,24},{64,96... | collective-permute-start | bytes 786440 | tf_op jit(solution)/shard_map/ppermute | solution.py:69
  150.7 15.0 %collective-permute-start.9 = (bf16[2,64,1024]{2,1,0:T(8,128)(2,1)S(1)}, bf16[2,64,1024]{2,1,0:T(8,128)(2,1)S(1)}, u32[]{:S(2)}, u32[]{:S(2)}) collective-permute-start(bf16[2,64,1024]{2,1,0:T(8,128)(2,1)S(1)} %add_convert_fusion), channel_id=1, source_target_pairs={{0,48},{8,56},{16,32},{24,40},{32,16},{40,24},{48,0},{56,8},{64,11... | collective-permute-start | bytes 786440 | tf_op jit(solution)/shard_map/ppermute | solution.py:69
  165.7 0.8 copy-start.20
  165.9 14.8 %copy-start.15 = (bf16[4,2,64,1024]{3,2,1,0:T(8,128)(2,1)}, bf16[4,2,64,1024]{3,2,1,0:T(8,128)(2,1)S(1)}, u32[]{:S(2)}) copy-start(bf16[4,2,64,1024]{3,2,1,0:T(8,128)(2,1)S(1)} %pad_maximum_fusion.own_ref) | copy-start | bytes 3145732
  165.9 14.8 %collective-permute-start.10 = (bf16[4,2,64,1024]{3,2,1,0:T(8,128)(2,1)S(1)}, bf16[4,2,64,1024]{3,2,1,0:T(8,128)(2,1)S(1)}, u32[]{:S(2)}, u32[]{:S(2)}) collective-permute-start(bf16[4,2,64,1024]{3,2,1,0:T(8,128)(2,1)S(1)} %pad_maximum_fusion.own_ref), channel_id=1, source_target_pairs={{0,8},{8,0},{16,24},{24,16},{32,40},{40,32},{48,56},{56,48},{64,72... | collective-permute-start | bytes 3145736 | tf_op jit(solution)/shard_map/ppermute | solution.py:69
  168.6 7.3 %collective-permute-start.11 = (bf16[2,80,512]{2,1,0:T(8,128)(2,1)}, bf16[2,80,512]{2,1,0:T(8,128)(2,1)S(1)}, u32[]{:S(2)}, u32[]{:S(2)}) collective-permute-start(bf16[2,80,512]{2,1,0:T(8,128)(2,1)} %get-tuple-element.129), channel_id=1, source_target_pairs={{0,16},{8,24},{16,0},{24,8},{32,48},{40,56},{48,32},{56,40},{64,80... | collective-permute-start | bytes 491528 | tf_op jit(solution)/shard_map/ppermute | solution.py:69
  168.6 9.6 %collective-permute-start.12 = (bf16[2,80,512]{2,1,0:T(8,128)(2,1)}, bf16[2,80,512]{2,1,0:T(8,128)(2,1)S(1)}, u32[]{:S(2)}, u32[]{:S(2)}) collective-permute-start(bf16[2,80,512]{2,1,0:T(8,128)(2,1)} %get-tuple-element.130), channel_id=1, source_target_pairs={{0,32},{8,40},{16,48},{24,56},{32,0},{40,8},{48,16},{56,24},{64,96... | collective-permute-start | bytes 491528 | tf_op jit(solution)/shard_map/ppermute | solution.py:69
  170.4 10.3 %collective-permute-start.13 = (bf16[2,80,512]{2,1,0:T(8,128)(2,1)}, bf16[2,80,512]{2,1,0:T(8,128)(2,1)S(1)}, u32[]{:S(2)}, u32[]{:S(2)}) collective-permute-start(bf16[2,80,512]{2,1,0:T(8,128)(2,1)} %get-tuple-element.131), channel_id=1, source_target_pairs={{0,48},{8,56},{16,32},{24,40},{32,16},{40,24},{48,0},{56,8},{64,11... | collective-permute-start | bytes 491528 | tf_op jit(solution)/shard_map/ppermute | solution.py:69
  175.9 4.8 %copy-start.23 = (bf16[2,80,512]{2,1,0:T(8,128)(2,1)}, bf16[2,80,512]{2,1,0:T(8,128)(2,1)S(1)}, u32[]{:S(2)}) copy-start(bf16[2,80,512]{2,1,0:T(8,128)(2,1)S(1)} %collective-permute-done.11.one_ref) | copy-start | bytes 491524
  178.2 2.5 %copy-start.24 = (bf16[2,80,512]{2,1,0:T(8,128)(2,1)}, bf16[2,80,512]{2,1,0:T(8,128)(2,1)S(1)}, u32[]{:S(2)}) copy-start(bf16[2,80,512]{2,1,0:T(8,128)(2,1)S(1)} %collective-permute-done.12.two_ref) | copy-start | bytes 491524
  180.7 0.7 copy-start.25
  180.7 1.1 copy-start.19
  183.7 9.5 %copy-start.10 = (bf16[8,160,1024]{2,1,0:T(8,128)(2,1)}, bf16[8,160,1024]{2,1,0:T(8,128)(2,1)S(1)}, u32[]{:S(2)}) copy-start(bf16[8,160,1024]{2,1,0:T(8,128)(2,1)S(1)} %all-to-all-done.4.got_ref) | copy-start | bytes 7864324
  183.7 7.2 %collective-permute-start.14 = (bf16[2,80,512]{2,1,0:T(8,128)(2,1)}, bf16[2,80,512]{2,1,0:T(8,128)(2,1)S(1)}, u32[]{:S(2)}, u32[]{:S(2)}) collective-permute-start(bf16[2,80,512]{2,1,0:T(8,128)(2,1)} %get-tuple-element.141.own_ref), channel_id=1, source_target_pairs={{0,64},{8,72},{16,80},{24,88},{32,96},{40,104},{48,112},{56,120},{... | collective-permute-start | bytes 491528 | tf_op jit(solution)/shard_map/ppermute | solution.py:69
  190.9 0.7 copy-start.22
  196.3 5.8 %copy-start.26 = (bf16[2,64,512]{2,1,0:T(8,128)(2,1)S(1)}, bf16[2,64,512]{2,1,0:T(8,128)(2,1)}, u32[]{:S(2)}) copy-start(bf16[2,64,512]{2,1,0:T(8,128)(2,1)} %get-tuple-element.148) | copy-start | bytes 393220
  196.3 14.5 %copy-start.3 = (f32[1024]{0:T(1024)S(1)}, f32[1024]{0:T(1024)}, u32[]{:S(2)}) copy-start(f32[1024]{0:T(1024)} %param.30) | copy-start | bytes 12292
  196.3 26.5 %all-to-all-start.5 = ((bf16[8,96,1024]{2,1,0:T(8,128)(2,1)}), bf16[8,96,1024]{2,1,0:T(8,128)(2,1)}, u32[]{:S(2)}, u32[]{:S(2)}) async-start(bf16[8,96,1024]{2,1,0:T(8,128)(2,1)} %shard_map.282), calls=%async_computation.5 | async-start | bytes 3145728 | tf_op jit(solution)/shard_map/all_to_all | solution.py:61
  202.2 18.8 %collective-permute-start.15 = (bf16[2,64,512]{2,1,0:T(8,128)(2,1)S(1)}, bf16[2,64,512]{2,1,0:T(8,128)(2,1)S(1)}, u32[]{:S(2)}, u32[]{:S(2)}) collective-permute-start(bf16[2,64,512]{2,1,0:T(8,128)(2,1)S(1)} %copy-done.26), channel_id=1, source_target_pairs={{0,16},{8,24},{16,0},{24,8},{32,48},{40,56},{48,32},{56,40},{64,80... | collective-permute-start | bytes 393224 | tf_op jit(solution)/shard_map/ppermute | solution.py:69
  202.2 18.7 %collective-permute-start.16 = (bf16[2,64,512]{2,1,0:T(8,128)(2,1)S(1)}, bf16[2,64,512]{2,1,0:T(8,128)(2,1)S(1)}, u32[]{:S(2)}, u32[]{:S(2)}) collective-permute-start(bf16[2,64,512]{2,1,0:T(8,128)(2,1)S(1)} %copy-done.26), channel_id=1, source_target_pairs={{0,32},{8,40},{16,48},{24,56},{32,0},{40,8},{48,16},{56,24},{64,96... | collective-permute-start | bytes 393224 | tf_op jit(solution)/shard_map/ppermute | solution.py:69
  206.6 14.3 %collective-permute-start.17 = (bf16[2,64,512]{2,1,0:T(8,128)(2,1)S(1)}, bf16[2,64,512]{2,1,0:T(8,128)(2,1)S(1)}, u32[]{:S(2)}, u32[]{:S(2)}) collective-permute-start(bf16[2,64,512]{2,1,0:T(8,128)(2,1)S(1)} %copy-done.26), channel_id=1, source_target_pairs={{0,48},{8,56},{16,32},{24,40},{32,16},{40,24},{48,0},{56,8},{64,11... | collective-permute-start | bytes 393224 | tf_op jit(solution)/shard_map/ppermute | solution.py:69
  221.0 6.8 %copy-start.17 = (bf16[4,2,64,512]{3,2,1,0:T(8,128)(2,1)}, bf16[4,2,64,512]{3,2,1,0:T(8,128)(2,1)S(1)}, u32[]{:S(2)}) copy-start(bf16[4,2,64,512]{3,2,1,0:T(8,128)(2,1)S(1)} %pad_maximum_fusion.1.own_ref) | copy-start | bytes 1572868
  221.0 4.9 %copy-start.12 = (f32[608,1024]{1,0:T(8,128)S(1)}, f32[608,1024]{1,0:T(8,128)}, u32[]{:S(2)}) copy-start(f32[608,1024]{1,0:T(8,128)} %param.31) | copy-start | bytes 7471108
  225.2 2.6 %collective-permute-start.18 = (bf16[4,2,64,512]{3,2,1,0:T(8,128)(2,1)S(1)}, bf16[4,2,64,512]{3,2,1,0:T(8,128)(2,1)S(1)}, u32[]{:S(2)}, u32[]{:S(2)}) collective-permute-start(bf16[4,2,64,512]{3,2,1,0:T(8,128)(2,1)S(1)} %pad_maximum_fusion.1.own_ref), channel_id=1, source_target_pairs={{0,8},{8,0},{16,24},{24,16},{32,40},{40,32},{48,56},{56,48},{64,72... | collective-permute-start | bytes 1572872 | tf_op jit(solution)/shard_map/ppermute | solution.py:69
  227.8 0.8 copy-start.21

commit v2 on v1

--- a/solution.py
+++ b/solution.py
@@ -99,11 +99,11 @@
                 parts = []
                 for j in (pair, pair + 1):
                     a, b = own_ref[y ^ j, z], other_ref[y ^ j, z]
-                    parts.append(jnp.where(core == c, a.astype(F32), b.astype(F32)))
+                    parts.append(jnp.where(core == c, a, b))
                 rows = jnp.concatenate(parts, 0)
                 lo = (c * 8 + z * 4 + pair) * chunk
-                left_ref[lo : lo + 2 * chunk, :] = rows[:, :cut]
-                right_ref[:, lo : lo + 2 * chunk] = jnp.transpose(rows[:, cut:])
+                left_ref[lo : lo + 2 * chunk, :] = rows[:, :cut].astype(F32)
+                right_ref[:, lo : lo + 2 * chunk] = jnp.transpose(rows[:, cut:]).astype(F32)
 
 
 def natural_chunks(own, other, dp, cut):
@@ -392,16 +392,22 @@
         out_ref[z, chunk:, :] = parts[z]
 
 
-def late_z(own_ref, got_ref, vec_ref, out_ref, sum_ref):
+def late_z(own_ref, got_ref, vec_ref, out_ref, down_ref, up_ref, query_ref, value_ref):
     chunk = out_ref.shape[1]
-    sum_ref[...] = vec_ref[...] + join(got_ref[0, chunk:, :], got_ref[1, chunk:, :])
+    vec = vec_ref[...] + join(got_ref[0, chunk:, :], got_ref[1, chunk:, :])
+    down_ref[...] = jnp.concatenate([vec[10:11], vec[11:12]], 1)
+    up_ref[...] = vec[12:13]
+    for ref, c in ((query_ref, 0), (value_ref, 2)):
+        ref[...] = jnp.concatenate([vec[13:14, head_part(h, c)] for h in range(2)], 1)
     for z in range(2):
         total = own_ref[z, :chunk, :].astype(F32) + got_ref[z, :chunk, :].astype(F32)
         out_ref[z] = total.astype(BF)
 
 
 def add_rows(mid_ref, got_ref, bias_ref, out_ref):
-    out_ref[...] = mid_ref[...] + (got_ref[0].astype(F32) + bias_ref[...])
+    for i in range(got_ref.shape[0]):
+        rows = slice(i * BLK, (i + 1) * BLK)
+        out_ref[rows, :] = mid_ref[rows, :] + (got_ref[i].astype(F32) + bias_ref[...])
 
 
 def simple(kernel, outs, *args):
@@ -413,6 +419,21 @@
         compiler_params=BIG,
         cost_estimate=TINY,
     )(*far(*args))
+
+
+def late_call(where, *args):
+    first = pl.BlockSpec((NT, BLK, 1024), lambda i: (0, 0, 0))
+    full = lambda a: pl.BlockSpec(a.shape, lambda i: (0, 0))
+    outs = [shaped(512, 512, dtype=BF), shaped(544, 512, dtype=BF), shaped(16, 512)]
+    return pl.pallas_call(
+        late_grads,
+        grid=(1,),
+        out_shape=outs,
+        in_specs=[SMEM_SPEC] + [first if a.ndim == 3 else full(a) for a in args],
+        out_specs=[pl.BlockSpec(o.shape, lambda i: (0, 0)) for o in outs],
+        compiler_params=BIG,
+        cost_estimate=LONG,
+    )(where, *far(*args))
 
 
 def simple_at(kernel, outs, where, *args, cost=None):
@@ -614,13 +635,12 @@
 
     e_three = z_add(e_two, e_z)
     e_y = y_spread(e_three)
-    l_keep, l_give, vec = simple_at(
-        late_grads,
-        [shaped(512, 512, dtype=BF), shaped(544, 512, dtype=BF), shaped(16, 512)],
+    l_keep, l_give, vec = late_call(
         where, act_one, qkv_grad_low, branch, context, norm_one_part, hidden_in, sums_two,
-        up_bias_part, down_bias_part, cost=LONG,
-    )
-    l_core, *e_y = tie(hop(l_give, 1), *e_y)
+        up_bias_part, down_bias_part,
+    )
+    l_give, *e_y = tie(l_give, *e_y)
+    l_core = hop(l_give, 1)
     l_own, *l_y, vec = simple_at(
         late_core,
         [shaped(2, 80, 512, dtype=BF)] * 4 + [shaped(16, 512)],
@@ -632,9 +652,7 @@
         late_y, [shaped(2, 80, 512, dtype=BF), shaped(16, 512)], l_own, *l_y, vec
     )
     one_got, l_two, vec, e_core, e_by_y = tie(one_got, l_two, vec, e_core, e_by_y)
-    l_three, vec = simple(
-        late_z, [shaped(2, 64, 512, dtype=BF), shaped(16, 512)], l_two, hop(l_two, 8), vec
-    )
+    l_z = hop(l_two, 8)
 
     in_send = pl.pallas_call(
         norm_one_back,
@@ -648,53 +666,54 @@
             out_specs=zero(NT, BLK + 16, width),
         ),
         compiler_params=BIG,
-        cost_estimate=TINY,
+        cost_estimate=LONG,
     )(me.reshape(1), *far(one_got, hid_pad, back_two), row(ln1_gain), *far(vec))
-    in_send, l_three, one_got, e_core, e_by_y = tie(in_send, l_three, one_got, e_core, e_by_y)
+    in_send, l_z, one_got, e_core, e_by_y = tie(in_send, l_z, one_got, e_core, e_by_y)
     in_got = exchange(in_send, T)
 
-    l_by_y = jnp.stack([l_three, *y_spread(l_three)])
+    l_three, down_bias_grad, up_bias_grad, query_bias_grad, value_bias_grad = simple(
+        late_z,
+        [shaped(2, 64, 512, dtype=BF)] + [shaped(1, n) for n in (width, 512, 128, 128)],
+        l_two, l_z, vec,
+    )
     up_weight_grad, down_weight_grad = natural_chunks(e_by_y, e_core, dp, 512)
     block_out = pl.pallas_call(
         add_rows,
-        grid=(NT,),
+        grid=(NT // 4,),
         out_shape=shaped(seq_len, width),
         in_specs=[
-            pl.BlockSpec((BLK, width), lambda i: (i, 0)),
-            pl.BlockSpec((1, BLK, width), lambda i: (i, 1, 0)),
+            pl.BlockSpec((4 * BLK, width), lambda i: (i, 0)),
+            pl.BlockSpec((4, BLK, width), lambda i: (i, 1, 0)),
             fixed(1, width),
         ],
-        out_specs=pl.BlockSpec((BLK, width), lambda i: (i, 0)),
+        out_specs=pl.BlockSpec((4 * BLK, width), lambda i: (i, 0)),
         compiler_params=BIG,
         cost_estimate=SHORT,
     )(*far(middle, one_got), row(down_bias))
-    in_got, l_by_y, up_weight_grad, down_weight_grad, block_out = tie(
-        in_got, l_by_y, up_weight_grad, down_weight_grad, block_out
-    )
+    up_weight_grad, block_out, *l_y = tie(up_weight_grad, block_out, *y_spread(l_three))
+    l_by_y = jnp.stack([l_three, *l_y])
     l_core = hop(l_by_y, 1)
+    qkv_weight_grad, dense_weight_grad = natural_chunks(l_by_y, l_core, dp, 384)
+    in_got, qkv_weight_grad = tie(in_got, qkv_weight_grad)
     shared = jnp.sum(in_got[:, BLK : BLK + 8].astype(F32) + in_got[:, BLK + 8 :].astype(F32), 0)
-    summed = vec.reshape(8, 1024)
+    shared = shared + hop(shared, 8)
     input_grad = out_grad + in_got[:, :BLK].reshape(PAD, width)[:seq_len].astype(F32)
-    qkv_weight_grad, dense_weight_grad = natural_chunks(l_by_y, l_core, dp, 384)
-    last = summed[6]
-    sums = last[512:896].reshape(2, 3, HEAD_DIM)
-
     return (
         block_out,
         input_grad,
         shared[0],
         shared[1],
         qkv_weight_grad,
-        sums[:, 0].reshape(-1),
-        sums[:, 2].reshape(-1),
+        query_bias_grad[0],
+        value_bias_grad[0],
         dense_weight_grad,
         shared[4],
         shared[2],
         shared[3],
         up_weight_grad,
-        last[:512],
+        up_bias_grad[0],
         down_weight_grad,
-        summed[5],
+        down_bias_grad[0],
     )
 
 

time: 234 us -> 223 us (0.953)
  local copies, waits for them, and re-layouts: 20.6 us -> 16 us
  Pallas kernels: 69.8 us -> 66.2 us
  waiting for transfers between devices: 81.8 us -> 79.1 us
    pallas_call x4 -> x3, Pallas kernels: 16.6 us -> 9.84 us  [simple_at(): pl.pallas_call(kernel, out_shape=outs, in_specs=[SMEM_SPEC] + whole(len(a...]
    pallas_call x1 -> x2, Pallas kernels: 6.09 us -> 9.29 us  [the longest x1 6.07 us: late_call(): pl.pallas_call(late_grads, grid=(1,), out_shape=outs, in_specs=[SMEM_SPEC...]
    ppermute x19 -> x20, waiting for transfers between devices: 40.5 us -> 37.6 us  [hop(): return lax.ppermute(a, DP, [(i, i ^ mask) for i in range(16)])]
    unnamed x57 -> x48, local copies, waits for them, and re-layouts: 5.87 us -> 3.99 us
    ppermute x19 -> x20, starting transfers between devices: 24.4 us -> 25 us  [hop(): return lax.ppermute(a, DP, [(i, i ^ mask) for i in range(16)])]
  transfers between devices with their start and end apart: 25 -> 26, of which waited for: 15 -> 17; matrix products, arithmetic and copies ran while one was open for 8% -> 6% of each run, Pallas kernels for 21% -> 24%
where the time goes in v2:
time: 223 us; the launch traced here: 222 us
  waiting for transfers between devices  79.1 us (35%)
  Pallas kernels  66.2 us (30%)
  starting transfers between devices  53.3 us (24%)
  local copies, waits for them, and re-layouts  16 us (7%)
  other arithmetic  4.61 us (2%)
    all_to_all x6, waiting for transfers between devices, exchange(): return lax.all_to_all(a, axis, 0, 0, tiled=True)  41.5 us
    ppermute x20, waiting for transfers between devices, hop(): return lax.ppermute(a, DP, [(i, i ^ mask) for i in range(16)])  37.6 us
    all_to_all x6, starting transfers between devices, exchange(): return lax.all_to_all(a, axis, 0, 0, tiled=True)  28.3 us
    ppermute x20, starting transfers between devices, hop(): return lax.ppermute(a, DP, [(i, i ^ mask) for i in range(16)])  25 us
    pallas_call x3, Pallas kernels, simple_at(): pl.pallas_call(kernel, out_shape=outs, in_specs=[SMEM_SPEC] + whole(len(a...  9.84 us
    pallas_call x1, Pallas kernels, per_device(): pl.pallas_call(attend_backward, out_shape=[shaped(PAD, 384, dtype=BF), sh...  9.22 us
    pallas_call x1, Pallas kernels, per_device(): pl.pallas_call(feed, grid=(PAD // rows,), out_shape=[shaped(PAD, width),...  9.11 us
    pad x3, local copies, waits for them, and re-layouts, pad_rows(): return jnp.pad(a, ((0, PAD - a.shape[0]), (0, 0)))  7.82 us
  transfers between devices with their start and end apart: 26, of which 17 were waited for; matrix products, arithmetic and copies ran while one was open for 6% of the time, Pallas kernels for 24%

profile of v2, /device:TPU:0, one launch (start us, length us, event | category | flops | bytes accessed | tf_op | source)
XLA Modules:
  0.0 222.2 jit_solution(17254960754483246997)
XLA Ops:
  0.7 0.9 constant_dynamic-slice_fusion
  1.6 1.1 broadcast_in_dim.2
  2.7 5.7 %all-to-all-start.1 = ((bf16[8,64,1024]{2,1,0:T(8,128)(2,1)}), bf16[8,64,1024]{2,1,0:T(8,128)(2,1)S(1)}, u32[]{:S(2)}, u32[]{:S(2)}) async-start(bf16[8,64,1024]{2,1,0:T(8,128)(2,1)} %broadcast_in_dim.2), calls=%async_computation.1 | async-start | bytes 2097152 | tf_op jit(solution)/shard_map/all_to_all | solution.py:61
  8.8 7.8 %shard_map.271 = (bf16[608,1024]{1,0:T(8,128)(2,1)}, bf16[608,384]{1,0:T(8,128)(2,1)}, bf16[608,128]{1,0:T(8,128)(2,1)}, bf16[8,640,128]{2,1,0:T(8,128)(2,1)}, f32[2,608,1]{2,1,0:T(8,128)}) custom-call(s32[3]{0:T(128)S(1)} %pad_add_fusion.1.where_ref, f32[608,1024]{1,0:T(8,128)} %hid_ref.3, f32[1,1024]{1,0:T(1,128)S(1)} %bitcast.46, f32[1,1024]{1,0:T(1,128)S(1)} %bitcast.45, ...), custom_call_target="tpu_custom_call" | custom-call | flops 4294967296 | bytes 25165824 | tf_op jit(solution)/shard_map/pallas_call | solution.py:503
  16.6 7.8 %all-to-all-done.1 = bf16[8,64,1024]{2,1,0:T(8,128)(2,1)S(1)} async-done(((bf16[8,64,1024]{2,1,0:T(8,128)(2,1)}), bf16[8,64,1024]{2,1,0:T(8,128)(2,1)S(1)}, u32[]{:S(2)}, u32[]{:S(2)}) %all-to-all-start.1) | async-done | bytes 1048608 | tf_op jit(solution)/shard_map/all_to_all | solution.py:61
  24.3 4.3 %all-to-all-start = ((bf16[8,640,128]{2,1,0:T(8,128)(2,1)}), bf16[8,640,128]{2,1,0:T(8,128)(2,1)}, u32[]{:S(2)}, u32[]{:S(2)}) async-start(bf16[8,640,128]{2,1,0:T(8,128)(2,1)} %get-tuple-element.93), calls=%async_computation | async-start | bytes 2621440 | tf_op jit(solution)/shard_map/all_to_all | solution.py:61
  28.7 3.7 %pad.11.hid_ref = f32[640,1024]{1,0:T(8,128)} pad(f32[608,1024]{1,0:T(8,128)} %hid_ref.3, f32[]{:T(128)} %constant.63.clone.1), padding=0_32x0_0 | pad | bytes 5111812 | tf_op jit(solution)/shard_map/jit(_pad)/pad | solution.py:53
  32.6 1.0 copy-done.11
  33.9 1.9 fusion.gin_ref
  35.9 11.2 %all-to-all-done.ctx_ref = bf16[8,640,128]{2,1,0:T(8,128)(2,1)} async-done(((bf16[8,640,128]{2,1,0:T(8,128)(2,1)}), bf16[8,640,128]{2,1,0:T(8,128)(2,1)}, u32[]{:S(2)}, u32[]{:S(2)}) %all-to-all-start) | async-done | bytes 1310752 | tf_op jit(solution)/shard_map/all_to_all | solution.py:61
  47.1 9.1 %shard_map.272 = (f32[640,1024]{1,0:T(8,128)}, bf16[640,1024]{1,0:T(8,128)(2,1)}, bf16[640,512]{1,0:T(8,128)(2,1)}, bf16[640,512]{1,0:T(8,128)(2,1)}, bf16[640,1024]{1,0:T(8,128)(2,1)}, /*index=5*/f32[1,512]{1,0:T(1,128)}) custom-call(bf16[8,640,128]{2,1,0:T(8,128)(2,1)} %all-to-all-done.ctx_ref, bf16[512,1024]{1,0:T(8,128)(2,1)} %bitcast.53, ...), custom_call_target="tpu_custom_call" | custom-call | flops 1 | bytes 1 | tf_op jit(solution)/shard_map/pallas_call | solution.py:537
  56.2 4.3 %all-to-all-start.2 = ((bf16[8,80,1024]{2,1,0:T(8,128)(2,1)}), bf16[8,80,1024]{2,1,0:T(8,128)(2,1)}, u32[]{:S(2)}, u32[]{:S(2)}) async-start(bf16[8,80,1024]{2,1,0:T(8,128)(2,1)} %bitcast.54), calls=%async_computation.2 | async-start | bytes 2621440 | tf_op jit(solution)/shard_map/all_to_all | solution.py:61
  60.5 2.4 %pad.12.grad_ref = bf16[640,1024]{1,0:T(8,128)(2,1)} pad(bf16[608,1024]{1,0:T(8,128)(2,1)} %copy-done.11, bf16[]{:T(256)} %constant.64.clone.1), padding=0_32x0_0 | pad | bytes 2555906 | tf_op jit(solution)/shard_map/jit(_pad)/pad | solution.py:53
  62.9 5.0 %shard_map.273 = (bf16[512,1024]{1,0:T(8,128)(2,1)}, bf16[512,1024]{1,0:T(8,128)(2,1)}, f32[1,1024]{1,0:T(1,128)}) custom-call(s32[3]{0:T(128)S(1)} %pad_add_fusion.1.where_ref, bf16[640,1024]{1,0:T(8,128)(2,1)} %get-tuple-element.95.act_ref, bf16[640,512]{1,0:T(8,128)(2,1)} %get-tuple-element.96.low_ref, bf16[640,1024]{1,0:T(8,128)(2,1)} %pad.12.grad_ref, ...), custom_call_target="tpu_custom_call" | custom-call | flops 1 | bytes 1 | tf_op jit(solution)/shard_map/pallas_call | solution.py:440
  68.0 1.7 pad.13.og_ref
  69.7 3.3 %shard_map.274 = bf16[640,1024]{1,0:T(8,128)(2,1)} custom-call(bf16[640,512]{1,0:T(8,128)(2,1)} %get-tuple-element.97.gelu_ref, bf16[512,1024]{1,0:T(8,128)(2,1)} %w_ref.4), custom_call_target="tpu_custom_call" | custom-call | flops 1 | bytes 1 | tf_op jit(solution)/shard_map/pallas_call | solution.py:574
  73.0 5.4 %all-to-all-done.2.got_ref = bf16[8,80,1024]{2,1,0:T(8,128)(2,1)} async-done(((bf16[8,80,1024]{2,1,0:T(8,128)(2,1)}), bf16[8,80,1024]{2,1,0:T(8,128)(2,1)}, u32[]{:S(2)}, u32[]{:S(2)}) %all-to-all-start.2) | async-done | bytes 1310752 | tf_op jit(solution)/shard_map/all_to_all | solution.py:61
  78.4 4.2 %shard_map.275 = (f32[80,1024]{1,0:T(8,128)}, bf16[8,160,1024]{2,1,0:T(8,128)(2,1)}, f32[8,1024]{1,0:T(8,128)}) custom-call(s32[1]{0:T(128)} %bitcast.2.me_ref, bf16[8,80,1024]{2,1,0:T(8,128)(2,1)} %all-to-all-done.2.got_ref, f32[640,1024]{1,0:T(8,128)} %get-tuple-element.100.mid_ref, f32[640,1024]{1,0:T(8,128)} %pad.13.og_ref, f32[1,1024]{1,0:T(1,128)S(1)} %bitcast.39, ...), custom_call_target="tpu_custom_call" | custom-call | flops 1 | bytes 1 | tf_op jit(solution)/shard_map/pallas_call | solution.py:592
  82.6 4.4 %all-to-all-start.3 = ((bf16[8,160,1024]{2,1,0:T(8,128)(2,1)}), bf16[8,160,1024]{2,1,0:T(8,128)(2,1)}, u32[]{:S(2)}, u32[]{:S(2)}) async-start(bf16[8,160,1024]{2,1,0:T(8,128)(2,1)} %get-tuple-element.102), calls=%async_computation.3 | async-start | bytes 5242880 | tf_op jit(solution)/shard_map/all_to_all | solution.py:61
  87.0 2.7 %shard_map.276 = (bf16[2,64,1024]{2,1,0:T(8,128)(2,1)}, bf16[2,64,1024]{2,1,0:T(8,128)(2,1)}, bf16[2,64,1024]{2,1,0:T(8,128)(2,1)}, bf16[2,64,1024]{2,1,0:T(8,128)(2,1)}) custom-call(s32[3]{0:T(128)S(1)} %pad_add_fusion.1.where_ref, bf16[2,4,64,1024]{3,2,1,0:T(8,128)(2,1)} %bitcast.55, bf16[2,4,64,1024]{3,2,1,0:T(8,128)(2,1)} %bitcast.16.got_ref), custom_call_target="tpu_custom_call" | custom-call | flops 1 | bytes 1 | tf_op jit(solution)/shard_map/pallas_call | solution.py:440
  89.7 1.6 collective-permute-start.2
  91.3 2.9 %collective-permute-start.3 = (bf16[2,64,1024]{2,1,0:T(8,128)(2,1)}, bf16[2,64,1024]{2,1,0:T(8,128)(2,1)S(1)}, u32[]{:S(2)}, u32[]{:S(2)}) collective-permute-start(bf16[2,64,1024]{2,1,0:T(8,128)(2,1)} %get-tuple-element.108), channel_id=1, source_target_pairs={{0,32},{8,40},{16,48},{24,56},{32,0},{40,8},{48,16},{56,24},{64,96... | collective-permute-start | bytes 786440 | tf_op jit(solution)/shard_map/ppermute | solution.py:69
  94.4 4.8 %collective-permute-done.2 = bf16[2,64,1024]{2,1,0:T(8,128)(2,1)S(1)} collective-permute-done((bf16[2,64,1024]{2,1,0:T(8,128)(2,1)}, bf16[2,64,1024]{2,1,0:T(8,128)(2,1)S(1)}, u32[]{:S(2)}, u32[]{:S(2)}) %collective-permute-start.2) | collective-permute-done | bytes 262176 | tf_op jit(solution)/shard_map/ppermute | solution.py:69
  99.1 5.5 %collective-permute-done.3 = bf16[2,64,1024]{2,1,0:T(8,128)(2,1)S(1)} collective-permute-done((bf16[2,64,1024]{2,1,0:T(8,128)(2,1)}, bf16[2,64,1024]{2,1,0:T(8,128)(2,1)S(1)}, u32[]{:S(2)}, u32[]{:S(2)}) %collective-permute-start.3) | collective-permute-done | bytes 262176 | tf_op jit(solution)/shard_map/ppermute | solution.py:69
  104.7 2.6 %collective-permute-done.4 = bf16[2,64,1024]{2,1,0:T(8,128)(2,1)S(1)} collective-permute-done((bf16[2,64,1024]{2,1,0:T(8,128)(2,1)}, bf16[2,64,1024]{2,1,0:T(8,128)(2,1)S(1)}, u32[]{:S(2)}, u32[]{:S(2)}) %collective-permute-start.4) | collective-permute-done | bytes 262176 | tf_op jit(solution)/shard_map/ppermute | solution.py:69
  107.2 1.1 add_convert_fusion.1
  108.4 15.3 %all-to-all-done.3.branch_ref = bf16[8,160,1024]{2,1,0:T(8,128)(2,1)} async-done(((bf16[8,160,1024]{2,1,0:T(8,128)(2,1)}), bf16[8,160,1024]{2,1,0:T(8,128)(2,1)}, u32[]{:S(2)}, u32[]{:S(2)}) %all-to-all-start.3) | async-done | bytes 2621472 | tf_op jit(solution)/shard_map/all_to_all | solution.py:61
  123.7 3.6 %collective-permute-start.5 = (bf16[2,64,1024]{2,1,0:T(8,128)(2,1)S(1)}, bf16[2,64,1024]{2,1,0:T(8,128)(2,1)S(1)}, u32[]{:S(2)}, u32[]{:S(2)}) collective-permute-start(bf16[2,64,1024]{2,1,0:T(8,128)(2,1)S(1)} %add_convert_fusion.1), channel_id=1, source_target_pairs={{0,64},{8,72},{16,80},{24,88},{32,96},{40,104},{48,112},{56,120},{... | collective-permute-start | bytes 786440 | tf_op jit(solution)/shard_map/ppermute | solution.py:69
  127.2 9.2 %shard_map.277 = (bf16[640,384]{1,0:T(8,128)(2,1)}, bf16[8,160,1024]{2,1,0:T(8,128)(2,1)}) custom-call(s32[3]{0:T(128)S(1)} %pad_add_fusion.1.where_ref, bf16[8,160,1024]{2,1,0:T(8,128)(2,1)} %all-to-all-done.3.branch_ref, bf16[128,1024]{1,0:T(8,128)(2,1)} %wd_ref.1, bf16[608,384]{1,0:T(8,128)(2,1)} %get-tuple-element.114.qkv_ref, ...), custom_call_target="tpu_custom_call" | custom-call | flops 4294967296 | bytes 25165824 | tf_op jit(solution)/shard_map/pallas_call | solution.py:624
  136.5 4.4 %all-to-all-start.4 = ((bf16[8,160,1024]{2,1,0:T(8,128)(2,1)}), bf16[8,160,1024]{2,1,0:T(8,128)(2,1)}, u32[]{:S(2)}, u32[]{:S(2)}) async-start(bf16[8,160,1024]{2,1,0:T(8,128)(2,1)} %get-tuple-element.118.part_ref), calls=%async_computation.4 | async-start | bytes 5242880 | tf_op jit(solution)/shard_map/all_to_all | solution.py:61
  140.9 1.7 collective-permute-start.6
  142.6 2.9 %collective-permute-start.7 = (bf16[2,64,1024]{2,1,0:T(8,128)(2,1)S(1)}, bf16[2,64,1024]{2,1,0:T(8,128)(2,1)S(1)}, u32[]{:S(2)}, u32[]{:S(2)}) collective-permute-start(bf16[2,64,1024]{2,1,0:T(8,128)(2,1)S(1)} %add_convert_fusion), channel_id=1, source_target_pairs={{0,32},{8,40},{16,48},{24,56},{32,0},{40,8},{48,16},{56,24},{64,96... | collective-permute-start | bytes 786440 | tf_op jit(solution)/shard_map/ppermute | solution.py:69
  145.7 6.1 %shard_map.278 = (bf16[512,512]{1,0:T(8,128)(2,1)}, bf16[544,512]{1,0:T(8,128)(2,1)}, f32[16,512]{1,0:T(8,128)}) custom-call(s32[3]{0:T(128)S(1)} %pad_add_fusion.1.where_ref, bf16[608,1024]{1,0:T(8,128)(2,1)} %get-tuple-element.119.act_ref, bf16[640,384]{1,0:T(8,128)(2,1)} %get-tuple-element.120.grad_ref, bf16[8,160,1024]{2,1,0:T(8,128)(2,1)} %all-to-all-done.3.branch_ref, ...), custom_call_target="tpu_custom_call" | custom-call | flops 4294967296 | bytes 25165824 | tf_op jit(solution)/shard_map/pallas_call | solution.py:428
  151.8 3.5 %collective-permute-done.7 = bf16[2,64,1024]{2,1,0:T(8,128)(2,1)S(1)} collective-permute-done((bf16[2,64,1024]{2,1,0:T(8,128)(2,1)S(1)}, bf16[2,64,1024]{2,1,0:T(8,128)(2,1)S(1)}, u32[]{:S(2)}, u32[]{:S(2)}) %collective-permute-start.7) | collective-permute-done | bytes 262176 | tf_op jit(solution)/shard_map/ppermute | solution.py:69
  155.3 2.6 %collective-permute-done.8 = bf16[2,64,1024]{2,1,0:T(8,128)(2,1)S(1)} collective-permute-done((bf16[2,64,1024]{2,1,0:T(8,128)(2,1)S(1)}, bf16[2,64,1024]{2,1,0:T(8,128)(2,1)S(1)}, u32[]{:S(2)}, u32[]{:S(2)}) %collective-permute-start.8) | collective-permute-done | bytes 262176 | tf_op jit(solution)/shard_map/ppermute | solution.py:69
  158.2 0.5 collective-permute-start.9
  158.7 2.9 %collective-permute-done.9.got_ref = bf16[544,512]{1,0:T(8,128)(2,1)S(1)} collective-permute-done((bf16[544,512]{1,0:T(8,128)(2,1)S(1)}, bf16[544,512]{1,0:T(8,128)(2,1)S(1)}, u32[]{:S(2)}, u32[]{:S(2)}) %collective-permute-start.9) | collective-permute-done | bytes 557088 | tf_op jit(solution)/shard_map/ppermute | solution.py:69
  161.7 0.8 copy-done.17
  162.5 2.1 shard_map.279
  164.6 1.7 collective-permute-start.12
  166.3 3.0 %collective-permute-start.13 = (bf16[2,80,512]{2,1,0:T(8,128)(2,1)}, bf16[2,80,512]{2,1,0:T(8,128)(2,1)S(1)}, u32[]{:S(2)}, u32[]{:S(2)}) collective-permute-start(bf16[2,80,512]{2,1,0:T(8,128)(2,1)} %get-tuple-element.136), channel_id=1, source_target_pairs={{0,48},{8,56},{16,32},{24,40},{32,16},{40,24},{48,0},{56,8},{64,11... | collective-permute-start | bytes 491528 | tf_op jit(solution)/shard_map/ppermute | solution.py:69
  169.3 2.6 %collective-permute-done.11.one_ref = bf16[2,80,512]{2,1,0:T(8,128)(2,1)S(1)} collective-permute-done((bf16[2,80,512]{2,1,0:T(8,128)(2,1)}, bf16[2,80,512]{2,1,0:T(8,128)(2,1)S(1)}, u32[]{:S(2)}, u32[]{:S(2)}) %collective-permute-start.11) | collective-permute-done | bytes 163872 | tf_op jit(solution)/shard_map/ppermute | solution.py:69
  171.8 2.5 %collective-permute-done.12.two_ref = bf16[2,80,512]{2,1,0:T(8,128)(2,1)S(1)} collective-permute-done((bf16[2,80,512]{2,1,0:T(8,128)(2,1)}, bf16[2,80,512]{2,1,0:T(8,128)(2,1)S(1)}, u32[]{:S(2)}, u32[]{:S(2)}) %collective-permute-start.12) | collective-permute-done | bytes 163872 | tf_op jit(solution)/shard_map/ppermute | solution.py:69
  174.3 2.6 %collective-permute-done.13.three_ref = bf16[2,80,512]{2,1,0:T(8,128)(2,1)S(1)} collective-permute-done((bf16[2,80,512]{2,1,0:T(8,128)(2,1)}, bf16[2,80,512]{2,1,0:T(8,128)(2,1)S(1)}, u32[]{:S(2)}, u32[]{:S(2)}) %collective-permute-start.13) | collective-permute-done | bytes 163872 | tf_op jit(solution)/shard_map/ppermute | solution.py:69
  176.9 1.0 copy-done.16
  177.9 1.9 shard_map.280
  179.8 0.3 collective-permute-start.14
  180.1 3.1 %shard_map.281 = bf16[8,96,1024]{2,1,0:T(8,128)(2,1)} custom-call(s32[1]{0:T(128)} %bitcast.2.me_ref, bf16[8,160,1024]{2,1,0:T(8,128)(2,1)} %all-to-all-done.4.got_ref, f32[640,1024]{1,0:T(8,128)} %pad.11.hid_ref, f32[80,1024]{1,0:T(8,128)} %get-tuple-element.145.back_ref, f32[1,1024]{1,0:T(1,128)S(1)} %bitcast.47, f32[16,512]{1,0:T(8,128)} %get-tuple-element.146.vec_ref), custom_call_target="tpu_custom_call" | custom-call | flops 4294967296 | bytes 25165824 | tf_op jit(solution)/shard_map/pallas_call | solution.py:657
  183.3 4.0 %collective-permute-done.14.got_ref = bf16[2,80,512]{2,1,0:T(8,128)(2,1)} collective-permute-done((bf16[2,80,512]{2,1,0:T(8,128)(2,1)}, bf16[2,80,512]{2,1,0:T(8,128)(2,1)}, u32[]{:S(2)}, u32[]{:S(2)}) %collective-permute-start.14) | collective-permute-done | bytes 163872 | tf_op jit(solution)/shard_map/ppermute | solution.py:69
  187.2 5.2 %all-to-all-start.5 = ((bf16[8,96,1024]{2,1,0:T(8,128)(2,1)}), bf16[8,96,1024]{2,1,0:T(8,128)(2,1)}, u32[]{:S(2)}, u32[]{:S(2)}) async-start(bf16[8,96,1024]{2,1,0:T(8,128)(2,1)} %shard_map.281), calls=%async_computation.5 | async-start | bytes 3145728 | tf_op jit(solution)/shard_map/all_to_all | solution.py:61
  192.4 1.7 shard_map.284
  194.1 4.4 %collective-permute-start.16 = (bf16[2,64,512]{2,1,0:T(8,128)(2,1)}, bf16[2,64,512]{2,1,0:T(8,128)(2,1)S(1)}, u32[]{:S(2)}, u32[]{:S(2)}) collective-permute-start(bf16[2,64,512]{2,1,0:T(8,128)(2,1)} %get-tuple-element.155), channel_id=1, source_target_pairs={{0,32},{8,40},{16,48},{24,56},{32,0},{40,8},{48,16},{56,24},{64,96... | collective-permute-start | bytes 393224 | tf_op jit(solution)/shard_map/ppermute | solution.py:69
  198.9 3.2 %shard_map.283 = f32[608,1024]{1,0:T(8,128)} custom-call(f32[640,1024]{1,0:T(8,128)} %get-tuple-element.100.mid_ref, bf16[8,160,1024]{2,1,0:T(8,128)(2,1)} %all-to-all-done.4.got_ref, f32[1,1024]{1,0:T(1,128)S(1)} %bitcast.42), custom_call_target="tpu_custom_call" | custom-call | flops 1048576 | bytes 10485760 | tf_op jit(solution)/shard_map/pallas_call | solution.py:680
  202.1 4.0 %shard_map.282 = (f32[1024,512]{1,0:T(8,128)}, f32[512,1024]{1,0:T(8,128)}) custom-call(s32[2]{0:T(128)S(1)} %pad_add_fusion.where_ref, bf16[4,2,64,1024]{3,2,1,0:T(8,128)(2,1)} %copy-done.13, bf16[4,2,64,1024]{3,2,1,0:T(8,128)(2,1)} %copy-done.16), custom_call_target="tpu_custom_call" | custom-call | flops 1048576 | bytes 10485760 | tf_op jit(solution)/shard_map/pallas_call | solution.py:112
  206.4 1.9 collective-permute-done.18.other_ref
  208.3 0.8 copy-done.18
  209.1 2.7 %shard_map.285 = (f32[1024,384]{1,0:T(8,128)}, f32[128,1024]{1,0:T(8,128)}) custom-call(s32[2]{0:T(128)S(1)} %pad_add_fusion.where_ref, bf16[4,2,64,512]{3,2,1,0:T(8,128)(2,1)} %copy-done.14, bf16[4,2,64,512]{3,2,1,0:T(8,128)(2,1)} %copy-done.18), custom_call_target="tpu_custom_call" | custom-call | flops 1048576 | bytes 10485760 | tf_op jit(solution)/shard_map/pallas_call | solution.py:112
  211.7 1.9 all-to-all-done.5
  213.6 1.4 slice.27
  215.0 1.0 add_reduce_fusion
  216.1 1.5 collective-permute-start.19
  217.6 1.9 convert_add_fusion
  219.4 2.1 collective-permute-done.19
  221.6 0.6 fusion.2
  (70 shorter events, 2.2 us)
Async XLA Ops:
  1.6 6.9 %copy-start.4 = (s32[1,608]{1,0:T(1,128)S(1)}, s32[1,608]{1,0:T(1,128)}, u32[]{:S(2)}) copy-start(s32[1,608]{1,0:T(1,128)} %srow_ref.3) | copy-start | bytes 7300
  1.6 7.1 %copy-start.6 = (f32[1024]{0:T(1024)S(1)}, f32[1024]{0:T(1024)}, u32[]{:S(2)}) copy-start(f32[1024]{0:T(1024)} %param.19) | copy-start | bytes 12292
  1.6 7.1 %copy-start.7 = (f32[1024]{0:T(1024)S(1)}, f32[1024]{0:T(1024)}, u32[]{:S(2)}) copy-start(f32[1024]{0:T(1024)} %param.18) | copy-start | bytes 12292
  1.6 7.1 %copy-start.8 = (f32[128]{0:T(128)S(1)}, f32[128]{0:T(128)}, u32[]{:S(2)}) copy-start(f32[128]{0:T(128)} %param.21) | copy-start | bytes 1540
  1.6 7.1 %copy-start.9 = (f32[128]{0:T(128)S(1)}, f32[128]{0:T(128)}, u32[]{:S(2)}) copy-start(f32[128]{0:T(128)} %param.22) | copy-start | bytes 1540
  2.7 21.6 %all-to-all-start.1 = ((bf16[8,64,1024]{2,1,0:T(8,128)(2,1)}), bf16[8,64,1024]{2,1,0:T(8,128)(2,1)S(1)}, u32[]{:S(2)}, u32[]{:S(2)}) async-start(bf16[8,64,1024]{2,1,0:T(8,128)(2,1)} %broadcast_in_dim.2), calls=%async_computation.1 | async-start | bytes 2097152 | tf_op jit(solution)/shard_map/all_to_all | solution.py:61
  24.3 4.3 %copy-start.12 = (bf16[8,64,1024]{2,1,0:T(8,128)(2,1)}, bf16[8,64,1024]{2,1,0:T(8,128)(2,1)S(1)}, u32[]{:S(2)}) copy-start(bf16[8,64,1024]{2,1,0:T(8,128)(2,1)S(1)} %all-to-all-done.1) | copy-start | bytes 3145732
  24.3 22.7 %all-to-all-start = ((bf16[8,640,128]{2,1,0:T(8,128)(2,1)}), bf16[8,640,128]{2,1,0:T(8,128)(2,1)}, u32[]{:S(2)}, u32[]{:S(2)}) async-start(bf16[8,640,128]{2,1,0:T(8,128)(2,1)} %get-tuple-element.93), calls=%async_computation | async-start | bytes 2621440 | tf_op jit(solution)/shard_map/all_to_all | solution.py:61
  28.6 3.8 %copy-start.10 = (f32[608,1024]{1,0:T(8,128)S(1)}, f32[608,1024]{1,0:T(8,128)}, u32[]{:S(2)}) copy-start(f32[608,1024]{1,0:T(8,128)} %param.31) | copy-start | bytes 7471108
  28.6 18.4 %collective-permute-start = (bf16[512,1024]{1,0:T(8,128)(2,1)}, bf16[512,1024]{1,0:T(8,128)(2,1)}, u32[]{:S(2)}, u32[]{:S(2)}) collective-permute-start(bf16[512,1024]{1,0:T(8,128)(2,1)} %bitcast.52), channel_id=1, source_target_pairs={{0,8},{8,0},{16,24},{24,16},{32,40},{40,32},{48,56},{56,48},{64,72... | collective-permute-start | bytes 3145736 | tf_op jit(solution)/shard_map/ppermute | solution.py:69
  32.4 1.5 copy-start.15
  32.6 1.0 copy-start.11
  33.9 13.1 %copy-start = (f32[1024]{0:T(1024)S(1)}, f32[1024]{0:T(1024)}, u32[]{:S(2)}) copy-start(f32[1024]{0:T(1024)} %param.25) | copy-start | bytes 12292
  33.9 13.1 %copy-start.1 = (f32[1024]{0:T(1024)S(1)}, f32[1024]{0:T(1024)}, u32[]{:S(2)}) copy-start(f32[1024]{0:T(1024)} %param.24) | copy-start | bytes 12292
  33.9 13.1 %copy-start.2 = (f32[1024]{0:T(1024)S(1)}, f32[1024]{0:T(1024)}, u32[]{:S(2)}) copy-start(f32[1024]{0:T(1024)} %param.26) | copy-start | bytes 12292
  33.9 13.2 %copy-start.5 = (f32[512]{0:T(512)S(1)}, f32[512]{0:T(512)}, u32[]{:S(2)}) copy-start(f32[512]{0:T(512)} %param.28) | copy-start | bytes 6148
  56.2 22.2 %all-to-all-start.2 = ((bf16[8,80,1024]{2,1,0:T(8,128)(2,1)}), bf16[8,80,1024]{2,1,0:T(8,128)(2,1)}, u32[]{:S(2)}, u32[]{:S(2)}) async-start(bf16[8,80,1024]{2,1,0:T(8,128)(2,1)} %bitcast.54), calls=%async_computation.2 | async-start | bytes 2621440 | tf_op jit(solution)/shard_map/all_to_all | solution.py:61
  68.0 5.0 %collective-permute-start.1 = (bf16[512,1024]{1,0:T(8,128)(2,1)}, bf16[512,1024]{1,0:T(8,128)(2,1)}, u32[]{:S(2)}, u32[]{:S(2)}) collective-permute-start(bf16[512,1024]{1,0:T(8,128)(2,1)} %get-tuple-element.98), channel_id=1, source_target_pairs={{0,8},{8,0},{16,24},{24,16},{32,40},{40,32},{48,56},{56,48},{64,72... | collective-permute-start | bytes 3145736 | tf_op jit(solution)/shard_map/ppermute | solution.py:69
  82.6 41.1 %all-to-all-start.3 = ((bf16[8,160,1024]{2,1,0:T(8,128)(2,1)}), bf16[8,160,1024]{2,1,0:T(8,128)(2,1)}, u32[]{:S(2)}, u32[]{:S(2)}) async-start(bf16[8,160,1024]{2,1,0:T(8,128)(2,1)} %get-tuple-element.102), calls=%async_computation.3 | async-start | bytes 5242880 | tf_op jit(solution)/shard_map/all_to_all | solution.py:61
  89.7 9.5 %collective-permute-start.2 = (bf16[2,64,1024]{2,1,0:T(8,128)(2,1)}, bf16[2,64,1024]{2,1,0:T(8,128)(2,1)S(1)}, u32[]{:S(2)}, u32[]{:S(2)}) collective-permute-start(bf16[2,64,1024]{2,1,0:T(8,128)(2,1)} %get-tuple-element.107), channel_id=1, source_target_pairs={{0,16},{8,24},{16,0},{24,8},{32,48},{40,56},{48,32},{56,40},{64,80... | collective-permute-start | bytes 786440 | tf_op jit(solution)/shard_map/ppermute | solution.py:69
  91.3 13.4 %collective-permute-start.3 = (bf16[2,64,1024]{2,1,0:T(8,128)(2,1)}, bf16[2,64,1024]{2,1,0:T(8,128)(2,1)S(1)}, u32[]{:S(2)}, u32[]{:S(2)}) collective-permute-start(bf16[2,64,1024]{2,1,0:T(8,128)(2,1)} %get-tuple-element.108), channel_id=1, source_target_pairs={{0,32},{8,40},{16,48},{24,56},{32,0},{40,8},{48,16},{56,24},{64,96... | collective-permute-start | bytes 786440 | tf_op jit(solution)/shard_map/ppermute | solution.py:69
  94.2 13.1 %collective-permute-start.4 = (bf16[2,64,1024]{2,1,0:T(8,128)(2,1)}, bf16[2,64,1024]{2,1,0:T(8,128)(2,1)S(1)}, u32[]{:S(2)}, u32[]{:S(2)}) collective-permute-start(bf16[2,64,1024]{2,1,0:T(8,128)(2,1)} %get-tuple-element.109), channel_id=1, source_target_pairs={{0,48},{8,56},{16,32},{24,40},{32,16},{40,24},{48,0},{56,8},{64,11... | collective-permute-start | bytes 786440 | tf_op jit(solution)/shard_map/ppermute | solution.py:69
  123.7 12.8 %collective-permute-start.5 = (bf16[2,64,1024]{2,1,0:T(8,128)(2,1)S(1)}, bf16[2,64,1024]{2,1,0:T(8,128)(2,1)S(1)}, u32[]{:S(2)}, u32[]{:S(2)}) collective-permute-start(bf16[2,64,1024]{2,1,0:T(8,128)(2,1)S(1)} %add_convert_fusion.1), channel_id=1, source_target_pairs={{0,64},{8,72},{16,80},{24,88},{32,96},{40,104},{48,112},{56,120},{... | collective-permute-start | bytes 786440 | tf_op jit(solution)/shard_map/ppermute | solution.py:69
  136.5 43.4 %all-to-all-start.4 = ((bf16[8,160,1024]{2,1,0:T(8,128)(2,1)}), bf16[8,160,1024]{2,1,0:T(8,128)(2,1)}, u32[]{:S(2)}, u32[]{:S(2)}) async-start(bf16[8,160,1024]{2,1,0:T(8,128)(2,1)} %get-tuple-element.118.part_ref), calls=%async_computation.4 | async-start | bytes 5242880 | tf_op jit(solution)/shard_map/all_to_all | solution.py:61
  140.9 10.9 %collective-permute-start.6 = (bf16[2,64,1024]{2,1,0:T(8,128)(2,1)S(1)}, bf16[2,64,1024]{2,1,0:T(8,128)(2,1)S(1)}, u32[]{:S(2)}, u32[]{:S(2)}) collective-permute-start(bf16[2,64,1024]{2,1,0:T(8,128)(2,1)S(1)} %add_convert_fusion), channel_id=1, source_target_pairs={{0,16},{8,24},{16,0},{24,8},{32,48},{40,56},{48,32},{56,40},{64,80... | collective-permute-start | bytes 786440 | tf_op jit(solution)/shard_map/ppermute | solution.py:69
  142.6 12.7 %collective-permute-start.7 = (bf16[2,64,1024]{2,1,0:T(8,128)(2,1)S(1)}, bf16[2,64,1024]{2,1,0:T(8,128)(2,1)S(1)}, u32[]{:S(2)}, u32[]{:S(2)}) collective-permute-start(bf16[2,64,1024]{2,1,0:T(8,128)(2,1)S(1)} %add_convert_fusion), channel_id=1, source_target_pairs={{0,32},{8,40},{16,48},{24,56},{32,0},{40,8},{48,16},{56,24},{64,96... | collective-permute-start | bytes 786440 | tf_op jit(solution)/shard_map/ppermute | solution.py:69
  145.5 12.5 %collective-permute-start.8 = (bf16[2,64,1024]{2,1,0:T(8,128)(2,1)S(1)}, bf16[2,64,1024]{2,1,0:T(8,128)(2,1)S(1)}, u32[]{:S(2)}, u32[]{:S(2)}) collective-permute-start(bf16[2,64,1024]{2,1,0:T(8,128)(2,1)S(1)} %add_convert_fusion), channel_id=1, source_target_pairs={{0,48},{8,56},{16,32},{24,40},{32,16},{40,24},{48,0},{56,8},{64,11... | collective-permute-start | bytes 786440 | tf_op jit(solution)/shard_map/ppermute | solution.py:69
  151.8 6.4 %copy-start.23 = (bf16[544,512]{1,0:T(8,128)(2,1)S(1)}, bf16[544,512]{1,0:T(8,128)(2,1)}, u32[]{:S(2)}) copy-start(bf16[544,512]{1,0:T(8,128)(2,1)} %get-tuple-element.128) | copy-start | bytes 1671172
  158.1 25.1 %copy-start.13 = (bf16[4,2,64,1024]{3,2,1,0:T(8,128)(2,1)}, bf16[4,2,64,1024]{3,2,1,0:T(8,128)(2,1)S(1)}, u32[]{:S(2)}) copy-start(bf16[4,2,64,1024]{3,2,1,0:T(8,128)(2,1)S(1)} %pad_maximum_fusion.own_ref) | copy-start | bytes 3145732
  158.1 18.8 %collective-permute-start.10 = (bf16[4,2,64,1024]{3,2,1,0:T(8,128)(2,1)S(1)}, bf16[4,2,64,1024]{3,2,1,0:T(8,128)(2,1)S(1)}, u32[]{:S(2)}, u32[]{:S(2)}) collective-permute-start(bf16[4,2,64,1024]{3,2,1,0:T(8,128)(2,1)S(1)} %pad_maximum_fusion.own_ref), channel_id=1, source_target_pairs={{0,8},{8,0},{16,24},{24,16},{32,40},{40,32},{48,56},{56,48},{64,72... | collective-permute-start | bytes 3145736 | tf_op jit(solution)/shard_map/ppermute | solution.py:69
  158.2 3.4 %collective-permute-start.9 = (bf16[544,512]{1,0:T(8,128)(2,1)S(1)}, bf16[544,512]{1,0:T(8,128)(2,1)S(1)}, u32[]{:S(2)}, u32[]{:S(2)}) collective-permute-start(bf16[544,512]{1,0:T(8,128)(2,1)S(1)} %copy-done.23), channel_id=1, source_target_pairs={{0,8},{8,0},{16,24},{24,16},{32,40},{40,32},{48,56},{56,48},{64,72... | collective-permute-start | bytes 1671176 | tf_op jit(solution)/shard_map/ppermute | solution.py:69
  161.7 0.8 copy-start.17
  164.6 7.3 %collective-permute-start.11 = (bf16[2,80,512]{2,1,0:T(8,128)(2,1)}, bf16[2,80,512]{2,1,0:T(8,128)(2,1)S(1)}, u32[]{:S(2)}, u32[]{:S(2)}) collective-permute-start(bf16[2,80,512]{2,1,0:T(8,128)(2,1)} %get-tuple-element.134), channel_id=1, source_target_pairs={{0,16},{8,24},{16,0},{24,8},{32,48},{40,56},{48,32},{56,40},{64,80... | collective-permute-start | bytes 491528 | tf_op jit(solution)/shard_map/ppermute | solution.py:69
  164.6 9.8 %collective-permute-start.12 = (bf16[2,80,512]{2,1,0:T(8,128)(2,1)}, bf16[2,80,512]{2,1,0:T(8,128)(2,1)S(1)}, u32[]{:S(2)}, u32[]{:S(2)}) collective-permute-start(bf16[2,80,512]{2,1,0:T(8,128)(2,1)} %get-tuple-element.135), channel_id=1, source_target_pairs={{0,32},{8,40},{16,48},{24,56},{32,0},{40,8},{48,16},{56,24},{64,96... | collective-permute-start | bytes 491528 | tf_op jit(solution)/shard_map/ppermute | solution.py:69
  166.3 10.6 %collective-permute-start.13 = (bf16[2,80,512]{2,1,0:T(8,128)(2,1)}, bf16[2,80,512]{2,1,0:T(8,128)(2,1)S(1)}, u32[]{:S(2)}, u32[]{:S(2)}) collective-permute-start(bf16[2,80,512]{2,1,0:T(8,128)(2,1)} %get-tuple-element.136), channel_id=1, source_target_pairs={{0,48},{8,56},{16,32},{24,40},{32,16},{40,24},{48,0},{56,8},{64,11... | collective-permute-start | bytes 491528 | tf_op jit(solution)/shard_map/ppermute | solution.py:69
  171.8 6.1 %copy-start.19 = (bf16[2,80,512]{2,1,0:T(8,128)(2,1)}, bf16[2,80,512]{2,1,0:T(8,128)(2,1)S(1)}, u32[]{:S(2)}) copy-start(bf16[2,80,512]{2,1,0:T(8,128)(2,1)S(1)} %collective-permute-done.11.one_ref) | copy-start | bytes 491524
  174.3 3.6 %copy-start.20 = (bf16[2,80,512]{2,1,0:T(8,128)(2,1)}, bf16[2,80,512]{2,1,0:T(8,128)(2,1)S(1)}, u32[]{:S(2)}) copy-start(bf16[2,80,512]{2,1,0:T(8,128)(2,1)S(1)} %collective-permute-done.12.two_ref) | copy-start | bytes 491524
  176.9 1.0 copy-start.21
  176.9 1.0 copy-start.16
  179.8 7.4 %collective-permute-start.14 = (bf16[2,80,512]{2,1,0:T(8,128)(2,1)}, bf16[2,80,512]{2,1,0:T(8,128)(2,1)}, u32[]{:S(2)}, u32[]{:S(2)}) collective-permute-start(bf16[2,80,512]{2,1,0:T(8,128)(2,1)} %get-tuple-element.147.own_ref), channel_id=1, source_target_pairs={{0,64},{8,72},{16,80},{24,88},{32,96},{40,104},{48,112},{56,120},{... | collective-permute-start | bytes 491528 | tf_op jit(solution)/shard_map/ppermute | solution.py:69
  183.3 15.7 %copy-start.3 = (f32[1024]{0:T(1024)S(1)}, f32[1024]{0:T(1024)}, u32[]{:S(2)}) copy-start(f32[1024]{0:T(1024)} %param.30) | copy-start | bytes 12292
  187.2 26.4 %all-to-all-start.5 = ((bf16[8,96,1024]{2,1,0:T(8,128)(2,1)}), bf16[8,96,1024]{2,1,0:T(8,128)(2,1)}, u32[]{:S(2)}, u32[]{:S(2)}) async-start(bf16[8,96,1024]{2,1,0:T(8,128)(2,1)} %shard_map.281), calls=%async_computation.5 | async-start | bytes 3145728 | tf_op jit(solution)/shard_map/all_to_all | solution.py:61
  194.1 12.0 %collective-permute-start.15 = (bf16[2,64,512]{2,1,0:T(8,128)(2,1)}, bf16[2,64,512]{2,1,0:T(8,128)(2,1)S(1)}, u32[]{:S(2)}, u32[]{:S(2)}) collective-permute-start(bf16[2,64,512]{2,1,0:T(8,128)(2,1)} %get-tuple-element.155), channel_id=1, source_target_pairs={{0,16},{8,24},{16,0},{24,8},{32,48},{40,56},{48,32},{56,40},{64,80... | collective-permute-start | bytes 393224 | tf_op jit(solution)/shard_map/ppermute | solution.py:69
  194.1 12.0 %collective-permute-start.16 = (bf16[2,64,512]{2,1,0:T(8,128)(2,1)}, bf16[2,64,512]{2,1,0:T(8,128)(2,1)S(1)}, u32[]{:S(2)}, u32[]{:S(2)}) collective-permute-start(bf16[2,64,512]{2,1,0:T(8,128)(2,1)} %get-tuple-element.155), channel_id=1, source_target_pairs={{0,32},{8,40},{16,48},{24,56},{32,0},{40,8},{48,16},{56,24},{64,96... | collective-permute-start | bytes 393224 | tf_op jit(solution)/shard_map/ppermute | solution.py:69
  198.6 7.6 %collective-permute-start.17 = (bf16[2,64,512]{2,1,0:T(8,128)(2,1)}, bf16[2,64,512]{2,1,0:T(8,128)(2,1)S(1)}, u32[]{:S(2)}, u32[]{:S(2)}) collective-permute-start(bf16[2,64,512]{2,1,0:T(8,128)(2,1)} %get-tuple-element.155), channel_id=1, source_target_pairs={{0,48},{8,56},{16,32},{24,40},{32,16},{40,24},{48,0},{56,8},{64,11... | collective-permute-start | bytes 393224 | tf_op jit(solution)/shard_map/ppermute | solution.py:69
  202.1 4.0 %copy-start.22 = (bf16[2,64,512]{2,1,0:T(8,128)(2,1)S(1)}, bf16[2,64,512]{2,1,0:T(8,128)(2,1)}, u32[]{:S(2)}) copy-start(bf16[2,64,512]{2,1,0:T(8,128)(2,1)} %get-tuple-element.155) | copy-start | bytes 393220
  206.3 2.0 copy-start.14
  206.3 2.0 collective-permute-start.18
  208.3 0.8 copy-start.18
  216.1 5.5 %collective-permute-start.19 = (f32[8,1024]{1,0:T(8,128)S(1)}, f32[8,1024]{1,0:T(8,128)S(1)}, u32[]{:S(2)}, u32[]{:S(2)}) collective-permute-start(f32[8,1024]{1,0:T(8,128)S(1)} %add_reduce_fusion), channel_id=1, source_target_pairs={{0,64},{8,72},{16,80},{24,88},{32,96},{40,104},{48,112},{56,120},{... | collective-permute-start | bytes 98312 | tf_op jit(solution)/shard_map/ppermute | solution.py:69

commit v3 on v2

--- a/solution.py
+++ b/solution.py
@@ -274,8 +274,7 @@
     back_ref[...] = back
     branch = (og_ref[...] + back).astype(BF)
     for i in range(NT):
-        send_ref[i, :BLK, :] = branch
-        send_ref[i, BLK:, :] = mlp_ref[i]
+        send_ref[i] = branch
     sum_ref[0:1, :] = jnp.sum(total * xhat, 0, keepdims=True)
     sum_ref[1:2, :] = jnp.sum(total, 0, keepdims=True)
     sum_ref[2:3, :] = jnp.sum(branch.astype(F32), 0, keepdims=True)
@@ -297,8 +296,11 @@
 
 
 def mlp_out(gelu_ref, w_ref, out_ref):
-    for lo in (0, 320):
-        out_ref[lo : lo + 320, :] = dot(gelu_ref[lo : lo + 320, :], w_ref[...]).astype(BF)
+    for lo in (0, 4):
+        rows = slice(lo * BLK, (lo + 4) * BLK)
+        part = dot(gelu_ref[rows, :], w_ref[...]).astype(BF)
+        for j in range(4):
+            out_ref[lo + j] = part[j * BLK : (j + 1) * BLK, :]
 
 
 def early_grads(where_ref, act_ref, low_ref, grad_ref, gelu_ref, keep_ref, give_ref, sum_ref):
@@ -495,9 +497,10 @@
     row = lambda v: v.reshape(1, -1)
     where = jnp.stack([me, core, (dp // 2) % 4]).astype(jnp.int32)
 
-    half_w = lax.dynamic_slice_in_dim(dense_weight, core * HEAD_DIM, HEAD_DIM, 0)
-    own_w = gather(half_w).reshape(NT * HEAD_DIM, width)
-    other_w = hop(own_w, 1)
+    part = HEAD_DIM // 2
+    odd = (dp // 2) % 2
+    piece = lax.dynamic_slice_in_dim(dense_weight, core * HEAD_DIM + odd * part, part, 0)
+    piece = gather(piece)
 
     seg_col = segments.reshape(seq_len, 1)
     act_one, qkv_low, context, ctx_send, lse = pl.pallas_call(
@@ -524,7 +527,14 @@
         segments,
         seg_col,
     )
+    piece, ctx_send = tie(piece, ctx_send)
     ctx_got = exchange(ctx_send, T)
+    beside = hop(piece, 2)
+    own_w = jnp.stack(
+        [jnp.where(odd == 0, piece, beside), jnp.where(odd == 0, beside, piece)], 1
+    ).reshape(NT * HEAD_DIM, width)
+    other_w = hop(own_w, 1)
+
 
     grad_pad = pad_rows(out_grad.astype(BF))
     gelu_in_grad = dot_nt(grad_pad, down_weight)
@@ -573,9 +583,10 @@
 
     mlp_part = pl.pallas_call(
         mlp_out,
-        out_shape=shaped(PAD, width, dtype=BF),
-        in_specs=whole(2),
-        out_specs=whole(1)[0],
+        grid=(1,),
+        out_shape=shaped(NT, 2 * BLK, width, dtype=BF),
+        in_specs=[fixed(PAD, 512), fixed(512, width)],
+        out_specs=pl.BlockSpec((NT, BLK, width), lambda i: (0, 1, 0)),
         compiler_params=BIG,
         cost_estimate=TINY,
     )(*far(gelu_low, down_weight))
@@ -596,17 +607,19 @@
             num_scalar_prefetch=1,
             grid=(1,),
             in_specs=[
-                zero(NT, BLK, width), mine, mine, zero(1, width), zero(NT, BLK, width)
+                zero(NT, BLK, width), mine, mine, zero(1, width),
+                pl.BlockSpec(memory_space=pl.ANY),
             ],
-            out_specs=[zero(BLK, width), zero(NT, 2 * BLK, width), zero(8, width)],
+            out_specs=[zero(BLK, width), zero(NT, BLK, width), zero(8, width)],
         ),
+        input_output_aliases={5: 1},
         compiler_params=BIG,
         cost_estimate=TINY,
     )(
         me.reshape(1),
         *far(two_got, middle, out_grad_pad),
         row(ln2_gain),
-        *far(mlp_part.reshape(NT, BLK, width)),
+        *far(mlp_part),
     )
     branch = exchange(branch_send, T)
 

time: 223 us -> 216 us (0.969)
  waiting for transfers between devices: 79.1 us -> 71.5 us
    all_to_all x6, waiting for transfers between devices: 41.5 us -> 28.6 us  [exchange(): return lax.all_to_all(a, axis, 0, 0, tiled=True)]
    ppermute x20 -> x21, waiting for transfers between devices: 37.6 us -> 42.8 us  [hop(): return lax.ppermute(a, DP, [(i, i ^ mask) for i in range(16)])]
    ppermute x20 -> x21, starting transfers between devices: 25 us -> 26.5 us  [hop(): return lax.ppermute(a, DP, [(i, i ^ mask) for i in range(16)])]
  transfers between devices with their start and end apart: 26 -> 27, of which waited for: 17 -> 18; matrix products, arithmetic and copies ran while one was open for 6% -> 6% of each run, Pallas kernels for 24% -> 25%
where the time goes in v3:
time: 216 us; the launch traced here: 215 us
  waiting for transfers between devices  71.5 us (33%)
  Pallas kernels  65.1 us (30%)
  starting transfers between devices  54.8 us (25%)
  local copies, waits for them, and re-layouts  14.8 us (7%)
  other arithmetic  5.87 us (3%)
    ppermute x21, waiting for transfers between devices, hop(): return lax.ppermute(a, DP, [(i, i ^ mask) for i in range(16)])  42.8 us
    all_to_all x6, waiting for transfers between devices, exchange(): return lax.all_to_all(a, axis, 0, 0, tiled=True)  28.6 us
    all_to_all x6, starting transfers between devices, exchange(): return lax.all_to_all(a, axis, 0, 0, tiled=True)  28.4 us
    ppermute x21, starting transfers between devices, hop(): return lax.ppermute(a, DP, [(i, i ^ mask) for i in range(16)])  26.5 us
    pallas_call x3, Pallas kernels, simple_at(): pl.pallas_call(kernel, out_shape=outs, in_specs=[SMEM_SPEC] + whole(len(a...  9.74 us
    pallas_call x1, Pallas kernels, per_device(): pl.pallas_call(attend_backward, out_shape=[shaped(PAD, 384, dtype=BF), sh...  9.21 us
    pallas_call x1, Pallas kernels, per_device(): pl.pallas_call(feed, grid=(PAD // rows,), out_shape=[shaped(PAD, width),...  9.12 us
    pallas_call x1, Pallas kernels, per_device(): pl.pallas_call(attend_forward, out_shape=[shaped(seq_len, width, dtype=BF...  7.82 us
  transfers between devices with their start and end apart: 27, of which 18 were waited for; matrix products, arithmetic and copies ran while one was open for 6% of the time, Pallas kernels for 25%

profile of v3, /device:TPU:0, one launch (start us, length us, event | category | flops | bytes accessed | tf_op | source)
XLA Modules:
  0.0 215.0 jit_solution(17736227967500987524)
XLA Ops:
  0.7 0.8 constant_dynamic-slice_fusion
  1.6 0.9 broadcast_in_dim.2
  2.4 5.7 %all-to-all-start = ((bf16[8,32,1024]{2,1,0:T(8,128)(2,1)}), bf16[8,32,1024]{2,1,0:T(8,128)(2,1)S(1)}, u32[]{:S(2)}, u32[]{:S(2)}) async-start(bf16[8,32,1024]{2,1,0:T(8,128)(2,1)} %broadcast_in_dim.2), calls=%async_computation | async-start | bytes 1048576 | tf_op jit(solution)/shard_map/all_to_all | solution.py:61
  8.5 7.8 %shard_map.271 = (bf16[608,1024]{1,0:T(8,128)(2,1)}, bf16[608,384]{1,0:T(8,128)(2,1)}, bf16[608,128]{1,0:T(8,128)(2,1)}, bf16[8,640,128]{2,1,0:T(8,128)(2,1)}, f32[2,608,1]{2,1,0:T(8,128)}) custom-call(s32[3]{0:T(128)S(1)} %pad_add_fusion.1.where_ref, f32[608,1024]{1,0:T(8,128)} %hid_ref.3, f32[1,1024]{1,0:T(1,128)S(1)} %bitcast.51, f32[1,1024]{1,0:T(1,128)S(1)} %bitcast.50, ...), custom_call_target="tpu_custom_call" | custom-call | flops 4294967296 | bytes 25165824 | tf_op jit(solution)/shard_map/pallas_call | solution.py:506
  16.3 1.4 all-to-all-done
  17.7 1.6 collective-permute-start
  19.2 4.3 %all-to-all-start.1 = ((bf16[8,640,128]{2,1,0:T(8,128)(2,1)}), bf16[8,640,128]{2,1,0:T(8,128)(2,1)}, u32[]{:S(2)}, u32[]{:S(2)}) async-start(bf16[8,640,128]{2,1,0:T(8,128)(2,1)} %get-tuple-element.96), calls=%async_computation.1 | async-start | bytes 2621440 | tf_op jit(solution)/shard_map/all_to_all | solution.py:61
  23.6 6.7 %collective-permute-done = bf16[8,32,1024]{2,1,0:T(8,128)(2,1)S(1)} collective-permute-done((bf16[8,32,1024]{2,1,0:T(8,128)(2,1)S(1)}, bf16[8,32,1024]{2,1,0:T(8,128)(2,1)S(1)}, u32[]{:S(2)}, u32[]{:S(2)}) %collective-permute-start) | collective-permute-done | bytes 524320 | tf_op jit(solution)/shard_map/ppermute | solution.py:69
  30.3 1.1 pad_maximum_fusion
  31.4 0.9 copy-done.13
  32.3 1.7 pad.11.hid_ref
  34.3 1.0 copy-done.11
  35.5 1.9 fusion.gin_ref
  37.5 4.3 %all-to-all-done.1.ctx_ref = bf16[8,640,128]{2,1,0:T(8,128)(2,1)} async-done(((bf16[8,640,128]{2,1,0:T(8,128)(2,1)}), bf16[8,640,128]{2,1,0:T(8,128)(2,1)}, u32[]{:S(2)}, u32[]{:S(2)}) %all-to-all-start.1) | async-done | bytes 1310752 | tf_op jit(solution)/shard_map/all_to_all | solution.py:61
  41.8 9.1 %shard_map.272 = (f32[640,1024]{1,0:T(8,128)}, bf16[640,1024]{1,0:T(8,128)(2,1)}, bf16[640,512]{1,0:T(8,128)(2,1)}, bf16[640,512]{1,0:T(8,128)(2,1)}, bf16[640,1024]{1,0:T(8,128)(2,1)}, /*index=5*/f32[1,512]{1,0:T(1,128)}) custom-call(bf16[8,640,128]{2,1,0:T(8,128)(2,1)} %all-to-all-done.1.ctx_ref, bf16[512,1024]{1,0:T(8,128)(2,1)} %bitcast.11.own_ref, ...), custom_call_target="tpu_custom_call" | custom-call | flops 1 | bytes 1 | tf_op jit(solution)/shard_map/pallas_call | solution.py:547
  51.0 4.3 %all-to-all-start.2 = ((bf16[8,80,1024]{2,1,0:T(8,128)(2,1)}), bf16[8,80,1024]{2,1,0:T(8,128)(2,1)}, u32[]{:S(2)}, u32[]{:S(2)}) async-start(bf16[8,80,1024]{2,1,0:T(8,128)(2,1)} %bitcast.56), calls=%async_computation.2 | async-start | bytes 2621440 | tf_op jit(solution)/shard_map/all_to_all | solution.py:61
  55.2 2.4 %pad.12.grad_ref = bf16[640,1024]{1,0:T(8,128)(2,1)} pad(bf16[608,1024]{1,0:T(8,128)(2,1)} %copy-done.11, bf16[]{:T(256)} %constant.72.clone.1), padding=0_32x0_0 | pad | bytes 2555906 | tf_op jit(solution)/shard_map/jit(_pad)/pad | solution.py:53
  57.7 4.9 %shard_map.273 = (bf16[512,1024]{1,0:T(8,128)(2,1)}, bf16[512,1024]{1,0:T(8,128)(2,1)}, f32[1,1024]{1,0:T(1,128)}) custom-call(s32[3]{0:T(128)S(1)} %pad_add_fusion.1.where_ref, bf16[640,1024]{1,0:T(8,128)(2,1)} %get-tuple-element.99.act_ref, bf16[640,512]{1,0:T(8,128)(2,1)} %get-tuple-element.100.low_ref, bf16[640,1024]{1,0:T(8,128)(2,1)} %pad.12.grad_ref, ...), custom_call_target="tpu_custom_call" | custom-call | flops 1 | bytes 1 | tf_op jit(solution)/shard_map/pallas_call | solution.py:442
  62.6 1.8 pad.13.og_ref
  64.4 3.4 %shard_map.274.mlp_ref = bf16[8,160,1024]{2,1,0:T(8,128)(2,1)} custom-call(bf16[640,512]{1,0:T(8,128)(2,1)} %get-tuple-element.101.gelu_ref, bf16[512,1024]{1,0:T(8,128)(2,1)} %w_ref.4), custom_call_target="tpu_custom_call" | custom-call | flops 1 | bytes 1 | tf_op jit(solution)/shard_map/pallas_call | solution.py:584
  67.8 5.2 %all-to-all-done.2.got_ref = bf16[8,80,1024]{2,1,0:T(8,128)(2,1)} async-done(((bf16[8,80,1024]{2,1,0:T(8,128)(2,1)}), bf16[8,80,1024]{2,1,0:T(8,128)(2,1)}, u32[]{:S(2)}, u32[]{:S(2)}) %all-to-all-start.2) | async-done | bytes 1310752 | tf_op jit(solution)/shard_map/all_to_all | solution.py:61
  73.0 3.2 %shard_map.275 = (f32[80,1024]{1,0:T(8,128)}, bf16[8,160,1024]{2,1,0:T(8,128)(2,1)}, f32[8,1024]{1,0:T(8,128)}) custom-call(s32[1]{0:T(128)} %bitcast.2.me_ref, bf16[8,80,1024]{2,1,0:T(8,128)(2,1)} %all-to-all-done.2.got_ref, f32[640,1024]{1,0:T(8,128)} %get-tuple-element.104.mid_ref, f32[640,1024]{1,0:T(8,128)} %pad.13.og_ref, ...), custom_call_target="tpu_custom_call", output_to_operand_aliasing={{1}: (5, {})} | custom-call | flops 1 | bytes 1 | tf_op jit(solution)/shard_map/pallas_call | solution.py:603
  76.2 4.4 %all-to-all-start.3 = ((bf16[8,160,1024]{2,1,0:T(8,128)(2,1)}), bf16[8,160,1024]{2,1,0:T(8,128)(2,1)}, u32[]{:S(2)}, u32[]{:S(2)}) async-start(bf16[8,160,1024]{2,1,0:T(8,128)(2,1)} %get-tuple-element.106), calls=%async_computation.3 | async-start | bytes 5242880 | tf_op jit(solution)/shard_map/all_to_all | solution.py:61
  80.6 2.7 %shard_map.276 = (bf16[2,64,1024]{2,1,0:T(8,128)(2,1)}, bf16[2,64,1024]{2,1,0:T(8,128)(2,1)}, bf16[2,64,1024]{2,1,0:T(8,128)(2,1)}, bf16[2,64,1024]{2,1,0:T(8,128)(2,1)}) custom-call(s32[3]{0:T(128)S(1)} %pad_add_fusion.1.where_ref, bf16[2,4,64,1024]{3,2,1,0:T(8,128)(2,1)} %bitcast.57, bf16[2,4,64,1024]{3,2,1,0:T(8,128)(2,1)} %bitcast.18.got_ref), custom_call_target="tpu_custom_call" | custom-call | flops 1 | bytes 1 | tf_op jit(solution)/shard_map/pallas_call | solution.py:442
  83.7 3.2 %collective-permute-start.4 = (bf16[2,64,1024]{2,1,0:T(8,128)(2,1)}, bf16[2,64,1024]{2,1,0:T(8,128)(2,1)S(1)}, u32[]{:S(2)}, u32[]{:S(2)}) collective-permute-start(bf16[2,64,1024]{2,1,0:T(8,128)(2,1)} %get-tuple-element.112), channel_id=1, source_target_pairs={{0,32},{8,40},{16,48},{24,56},{32,0},{40,8},{48,16},{56,24},{64,96... | collective-permute-start | bytes 786440 | tf_op jit(solution)/shard_map/ppermute | solution.py:69
  86.9 1.0 collective-permute-start.5
  88.0 4.6 %collective-permute-done.3 = bf16[2,64,1024]{2,1,0:T(8,128)(2,1)S(1)} collective-permute-done((bf16[2,64,1024]{2,1,0:T(8,128)(2,1)}, bf16[2,64,1024]{2,1,0:T(8,128)(2,1)S(1)}, u32[]{:S(2)}, u32[]{:S(2)}) %collective-permute-start.3) | collective-permute-done | bytes 262176 | tf_op jit(solution)/shard_map/ppermute | solution.py:69
  92.5 4.5 %collective-permute-done.4 = bf16[2,64,1024]{2,1,0:T(8,128)(2,1)S(1)} collective-permute-done((bf16[2,64,1024]{2,1,0:T(8,128)(2,1)}, bf16[2,64,1024]{2,1,0:T(8,128)(2,1)S(1)}, u32[]{:S(2)}, u32[]{:S(2)}) %collective-permute-start.4) | collective-permute-done | bytes 262176 | tf_op jit(solution)/shard_map/ppermute | solution.py:69
  97.0 2.6 %collective-permute-done.5 = bf16[2,64,1024]{2,1,0:T(8,128)(2,1)S(1)} collective-permute-done((bf16[2,64,1024]{2,1,0:T(8,128)(2,1)}, bf16[2,64,1024]{2,1,0:T(8,128)(2,1)S(1)}, u32[]{:S(2)}, u32[]{:S(2)}) %collective-permute-start.5) | collective-permute-done | bytes 262176 | tf_op jit(solution)/shard_map/ppermute | solution.py:69
  99.6 1.1 add_convert_fusion.1
  100.7 15.9 %all-to-all-done.3.branch_ref = bf16[8,160,1024]{2,1,0:T(8,128)(2,1)} async-done(((bf16[8,160,1024]{2,1,0:T(8,128)(2,1)}), bf16[8,160,1024]{2,1,0:T(8,128)(2,1)}, u32[]{:S(2)}, u32[]{:S(2)}) %all-to-all-start.3) | async-done | bytes 2621472 | tf_op jit(solution)/shard_map/all_to_all | solution.py:61
  116.6 3.6 %collective-permute-start.6 = (bf16[2,64,1024]{2,1,0:T(8,128)(2,1)S(1)}, bf16[2,64,1024]{2,1,0:T(8,128)(2,1)S(1)}, u32[]{:S(2)}, u32[]{:S(2)}) collective-permute-start(bf16[2,64,1024]{2,1,0:T(8,128)(2,1)S(1)} %add_convert_fusion.1), channel_id=1, source_target_pairs={{0,64},{8,72},{16,80},{24,88},{32,96},{40,104},{48,112},{56,120},{... | collective-permute-start | bytes 786440 | tf_op jit(solution)/shard_map/ppermute | solution.py:69
  120.2 9.2 %shard_map.277 = (bf16[640,384]{1,0:T(8,128)(2,1)}, bf16[8,160,1024]{2,1,0:T(8,128)(2,1)}) custom-call(s32[3]{0:T(128)S(1)} %pad_add_fusion.1.where_ref, bf16[8,160,1024]{2,1,0:T(8,128)(2,1)} %all-to-all-done.3.branch_ref, bf16[128,1024]{1,0:T(8,128)(2,1)} %wd_ref.1, bf16[608,384]{1,0:T(8,128)(2,1)} %get-tuple-element.118.qkv_ref, ...), custom_call_target="tpu_custom_call" | custom-call | flops 4294967296 | bytes 25165824 | tf_op jit(solution)/shard_map/pallas_call | solution.py:637
  129.4 4.4 %all-to-all-start.4 = ((bf16[8,160,1024]{2,1,0:T(8,128)(2,1)}), bf16[8,160,1024]{2,1,0:T(8,128)(2,1)}, u32[]{:S(2)}, u32[]{:S(2)}) async-start(bf16[8,160,1024]{2,1,0:T(8,128)(2,1)} %get-tuple-element.122.part_ref), calls=%async_computation.4 | async-start | bytes 5242880 | tf_op jit(solution)/shard_map/all_to_all | solution.py:61
  134.4 3.2 %collective-permute-start.8 = (bf16[2,64,1024]{2,1,0:T(8,128)(2,1)S(1)}, bf16[2,64,1024]{2,1,0:T(8,128)(2,1)S(1)}, u32[]{:S(2)}, u32[]{:S(2)}) collective-permute-start(bf16[2,64,1024]{2,1,0:T(8,128)(2,1)S(1)} %add_convert_fusion), channel_id=1, source_target_pairs={{0,32},{8,40},{16,48},{24,56},{32,0},{40,8},{48,16},{56,24},{64,96... | collective-permute-start | bytes 786440 | tf_op jit(solution)/shard_map/ppermute | solution.py:69
  137.6 1.1 collective-permute-start.9
  138.7 6.0 %shard_map.278 = (bf16[512,512]{1,0:T(8,128)(2,1)}, bf16[544,512]{1,0:T(8,128)(2,1)}, f32[16,512]{1,0:T(8,128)}) custom-call(s32[3]{0:T(128)S(1)} %pad_add_fusion.1.where_ref, bf16[608,1024]{1,0:T(8,128)(2,1)} %get-tuple-element.123.act_ref, bf16[640,384]{1,0:T(8,128)(2,1)} %get-tuple-element.124.grad_ref, bf16[8,160,1024]{2,1,0:T(8,128)(2,1)} %all-to-all-done.3.branch_ref, ...), custom_call_target="tpu_custom_call" | custom-call | flops 4294967296 | bytes 25165824 | tf_op jit(solution)/shard_map/pallas_call | solution.py:430
  144.7 2.6 %collective-permute-done.8 = bf16[2,64,1024]{2,1,0:T(8,128)(2,1)S(1)} collective-permute-done((bf16[2,64,1024]{2,1,0:T(8,128)(2,1)S(1)}, bf16[2,64,1024]{2,1,0:T(8,128)(2,1)S(1)}, u32[]{:S(2)}, u32[]{:S(2)}) %collective-permute-start.8) | collective-permute-done | bytes 262176 | tf_op jit(solution)/shard_map/ppermute | solution.py:69
  147.3 2.6 %collective-permute-done.9 = bf16[2,64,1024]{2,1,0:T(8,128)(2,1)S(1)} collective-permute-done((bf16[2,64,1024]{2,1,0:T(8,128)(2,1)S(1)}, bf16[2,64,1024]{2,1,0:T(8,128)(2,1)S(1)}, u32[]{:S(2)}, u32[]{:S(2)}) %collective-permute-start.9) | collective-permute-done | bytes 262176 | tf_op jit(solution)/shard_map/ppermute | solution.py:69
  150.7 2.9 %collective-permute-done.10.got_ref = bf16[544,512]{1,0:T(8,128)(2,1)S(1)} collective-permute-done((bf16[544,512]{1,0:T(8,128)(2,1)S(1)}, bf16[544,512]{1,0:T(8,128)(2,1)S(1)}, u32[]{:S(2)}, u32[]{:S(2)}) %collective-permute-start.10) | collective-permute-done | bytes 557088 | tf_op jit(solution)/shard_map/ppermute | solution.py:69
  154.4 2.1 shard_map.279
  156.5 2.5 %collective-permute-start.13 = (bf16[2,80,512]{2,1,0:T(8,128)(2,1)}, bf16[2,80,512]{2,1,0:T(8,128)(2,1)S(1)}, u32[]{:S(2)}, u32[]{:S(2)}) collective-permute-start(bf16[2,80,512]{2,1,0:T(8,128)(2,1)} %get-tuple-element.139), channel_id=1, source_target_pairs={{0,32},{8,40},{16,48},{24,56},{32,0},{40,8},{48,16},{56,24},{64,96... | collective-permute-start | bytes 491528 | tf_op jit(solution)/shard_map/ppermute | solution.py:69
  159.1 2.2 %collective-permute-start.14 = (bf16[2,80,512]{2,1,0:T(8,128)(2,1)}, bf16[2,80,512]{2,1,0:T(8,128)(2,1)S(1)}, u32[]{:S(2)}, u32[]{:S(2)}) collective-permute-start(bf16[2,80,512]{2,1,0:T(8,128)(2,1)} %get-tuple-element.140), channel_id=1, source_target_pairs={{0,48},{8,56},{16,32},{24,40},{32,16},{40,24},{48,0},{56,8},{64,11... | collective-permute-start | bytes 491528 | tf_op jit(solution)/shard_map/ppermute | solution.py:69
  161.2 2.6 %collective-permute-done.12.one_ref = bf16[2,80,512]{2,1,0:T(8,128)(2,1)S(1)} collective-permute-done((bf16[2,80,512]{2,1,0:T(8,128)(2,1)}, bf16[2,80,512]{2,1,0:T(8,128)(2,1)S(1)}, u32[]{:S(2)}, u32[]{:S(2)}) %collective-permute-start.12) | collective-permute-done | bytes 163872 | tf_op jit(solution)/shard_map/ppermute | solution.py:69
  163.8 3.3 %collective-permute-done.13.two_ref = bf16[2,80,512]{2,1,0:T(8,128)(2,1)S(1)} collective-permute-done((bf16[2,80,512]{2,1,0:T(8,128)(2,1)}, bf16[2,80,512]{2,1,0:T(8,128)(2,1)S(1)}, u32[]{:S(2)}, u32[]{:S(2)}) %collective-permute-start.13) | collective-permute-done | bytes 163872 | tf_op jit(solution)/shard_map/ppermute | solution.py:69
  167.1 2.6 %collective-permute-done.14.three_ref = bf16[2,80,512]{2,1,0:T(8,128)(2,1)S(1)} collective-permute-done((bf16[2,80,512]{2,1,0:T(8,128)(2,1)}, bf16[2,80,512]{2,1,0:T(8,128)(2,1)S(1)}, u32[]{:S(2)}, u32[]{:S(2)}) %collective-permute-start.14) | collective-permute-done | bytes 163872 | tf_op jit(solution)/shard_map/ppermute | solution.py:69
  169.7 1.0 copy-done.15
  170.7 1.9 shard_map.280
  172.9 3.1 %shard_map.281 = bf16[8,96,1024]{2,1,0:T(8,128)(2,1)} custom-call(s32[1]{0:T(128)} %bitcast.2.me_ref, bf16[8,160,1024]{2,1,0:T(8,128)(2,1)} %all-to-all-done.4.got_ref, f32[640,1024]{1,0:T(8,128)} %pad.11.hid_ref, f32[80,1024]{1,0:T(8,128)} %get-tuple-element.149.back_ref, f32[1,1024]{1,0:T(1,128)S(1)} %bitcast.52, f32[16,512]{1,0:T(8,128)} %get-tuple-element.150.vec_ref), custom_call_target="tpu_custom_call" | custom-call | flops 4294967296 | bytes 25165824 | tf_op jit(solution)/shard_map/pallas_call | solution.py:670
  176.0 4.0 %collective-permute-done.15.got_ref = bf16[2,80,512]{2,1,0:T(8,128)(2,1)} collective-permute-done((bf16[2,80,512]{2,1,0:T(8,128)(2,1)}, bf16[2,80,512]{2,1,0:T(8,128)(2,1)}, u32[]{:S(2)}, u32[]{:S(2)}) %collective-permute-start.15) | collective-permute-done | bytes 163872 | tf_op jit(solution)/shard_map/ppermute | solution.py:69
  180.0 5.2 %all-to-all-start.5 = ((bf16[8,96,1024]{2,1,0:T(8,128)(2,1)}), bf16[8,96,1024]{2,1,0:T(8,128)(2,1)}, u32[]{:S(2)}, u32[]{:S(2)}) async-start(bf16[8,96,1024]{2,1,0:T(8,128)(2,1)} %shard_map.281), calls=%async_computation.5 | async-start | bytes 3145728 | tf_op jit(solution)/shard_map/all_to_all | solution.py:61
  185.2 1.7 shard_map.284
  186.9 3.6 %collective-permute-start.17 = (bf16[2,64,512]{2,1,0:T(8,128)(2,1)}, bf16[2,64,512]{2,1,0:T(8,128)(2,1)S(1)}, u32[]{:S(2)}, u32[]{:S(2)}) collective-permute-start(bf16[2,64,512]{2,1,0:T(8,128)(2,1)} %get-tuple-element.159), channel_id=1, source_target_pairs={{0,32},{8,40},{16,48},{24,56},{32,0},{40,8},{48,16},{56,24},{64,96... | collective-permute-start | bytes 393224 | tf_op jit(solution)/shard_map/ppermute | solution.py:69
  190.6 1.1 collective-permute-start.18
  191.7 3.2 %shard_map.283 = f32[608,1024]{1,0:T(8,128)} custom-call(f32[640,1024]{1,0:T(8,128)} %get-tuple-element.104.mid_ref, bf16[8,160,1024]{2,1,0:T(8,128)(2,1)} %all-to-all-done.4.got_ref, f32[1,1024]{1,0:T(1,128)S(1)} %bitcast.47), custom_call_target="tpu_custom_call" | custom-call | flops 1048576 | bytes 10485760 | tf_op jit(solution)/shard_map/pallas_call | solution.py:693
  194.9 4.0 %shard_map.282 = (f32[1024,512]{1,0:T(8,128)}, f32[512,1024]{1,0:T(8,128)}) custom-call(s32[2]{0:T(128)S(1)} %pad_add_fusion.where_ref, bf16[4,2,64,1024]{3,2,1,0:T(8,128)(2,1)} %copy-done.12, bf16[4,2,64,1024]{3,2,1,0:T(8,128)(2,1)} %copy-done.15), custom_call_target="tpu_custom_call" | custom-call | flops 1048576 | bytes 10485760 | tf_op jit(solution)/shard_map/pallas_call | solution.py:112
  199.1 1.9 collective-permute-done.19.other_ref
  201.8 2.7 %shard_map.285 = (f32[1024,384]{1,0:T(8,128)}, f32[128,1024]{1,0:T(8,128)}) custom-call(s32[2]{0:T(128)S(1)} %pad_add_fusion.where_ref, bf16[4,2,64,512]{3,2,1,0:T(8,128)(2,1)} %copy-done.14, bf16[4,2,64,512]{3,2,1,0:T(8,128)(2,1)} %copy-done.18), custom_call_target="tpu_custom_call" | custom-call | flops 1048576 | bytes 10485760 | tf_op jit(solution)/shard_map/pallas_call | solution.py:112
  204.5 1.9 all-to-all-done.5
  206.4 1.4 slice.27
  207.8 1.0 add_reduce_fusion
  208.8 1.5 collective-permute-start.20
  210.3 2.0 convert_add_fusion
  212.4 2.0 collective-permute-done.20
  (74 shorter events, 5.4 us)
Async XLA Ops:
  0.6 7.6 %copy-start.4 = (s32[1,608]{1,0:T(1,128)S(1)}, s32[1,608]{1,0:T(1,128)}, u32[]{:S(2)}) copy-start(s32[1,608]{1,0:T(1,128)} %srow_ref.3) | copy-start | bytes 7300
  0.7 7.8 %copy-start.7 = (f32[1024]{0:T(1024)S(1)}, f32[1024]{0:T(1024)}, u32[]{:S(2)}) copy-start(f32[1024]{0:T(1024)} %param.18) | copy-start | bytes 12292
  0.7 7.8 %copy-start.6 = (f32[1024]{0:T(1024)S(1)}, f32[1024]{0:T(1024)}, u32[]{:S(2)}) copy-start(f32[1024]{0:T(1024)} %param.19) | copy-start | bytes 12292
  0.7 7.8 %copy-start.8 = (f32[128]{0:T(128)S(1)}, f32[128]{0:T(128)}, u32[]{:S(2)}) copy-start(f32[128]{0:T(128)} %param.21) | copy-start | bytes 1540
  0.7 7.8 %copy-start.9 = (f32[128]{0:T(128)S(1)}, f32[128]{0:T(128)}, u32[]{:S(2)}) copy-start(f32[128]{0:T(128)} %param.22) | copy-start | bytes 1540
  2.4 15.2 %all-to-all-start = ((bf16[8,32,1024]{2,1,0:T(8,128)(2,1)}), bf16[8,32,1024]{2,1,0:T(8,128)(2,1)S(1)}, u32[]{:S(2)}, u32[]{:S(2)}) async-start(bf16[8,32,1024]{2,1,0:T(8,128)(2,1)} %broadcast_in_dim.2), calls=%async_computation | async-start | bytes 1048576 | tf_op jit(solution)/shard_map/all_to_all | solution.py:61
  17.7 12.6 %collective-permute-start = (bf16[8,32,1024]{2,1,0:T(8,128)(2,1)S(1)}, bf16[8,32,1024]{2,1,0:T(8,128)(2,1)S(1)}, u32[]{:S(2)}, u32[]{:S(2)}) collective-permute-start(bf16[8,32,1024]{2,1,0:T(8,128)(2,1)S(1)} %all-to-all-done), channel_id=1, source_target_pairs={{0,16},{8,24},{16,0},{24,8},{32,48},{40,56},{48,32},{56,40},{64,80... | collective-permute-start | bytes 1572872 | tf_op jit(solution)/shard_map/ppermute | solution.py:69
  19.2 22.6 %all-to-all-start.1 = ((bf16[8,640,128]{2,1,0:T(8,128)(2,1)}), bf16[8,640,128]{2,1,0:T(8,128)(2,1)}, u32[]{:S(2)}, u32[]{:S(2)}) async-start(bf16[8,640,128]{2,1,0:T(8,128)(2,1)} %get-tuple-element.96), calls=%async_computation.1 | async-start | bytes 2621440 | tf_op jit(solution)/shard_map/all_to_all | solution.py:61
  30.3 2.1 copy-start.13
  31.4 2.7 %copy-start.10 = (f32[608,1024]{1,0:T(8,128)S(1)}, f32[608,1024]{1,0:T(8,128)}, u32[]{:S(2)}) copy-start(f32[608,1024]{1,0:T(8,128)} %param.31) | copy-start | bytes 7471108
  31.4 10.4 %collective-permute-start.1 = (bf16[512,1024]{1,0:T(8,128)(2,1)}, bf16[512,1024]{1,0:T(8,128)(2,1)}, u32[]{:S(2)}, u32[]{:S(2)}) collective-permute-start(bf16[512,1024]{1,0:T(8,128)(2,1)} %bitcast.11.own_ref), channel_id=1, source_target_pairs={{0,8},{8,0},{16,24},{24,16},{32,40},{40,32},{48,56},{56,48},{64,72... | collective-permute-start | bytes 3145736 | tf_op jit(solution)/shard_map/ppermute | solution.py:69
  34.0 1.5 copy-start.16
  34.2 1.0 copy-start.11
  35.5 6.3 %copy-start = (f32[1024]{0:T(1024)S(1)}, f32[1024]{0:T(1024)}, u32[]{:S(2)}) copy-start(f32[1024]{0:T(1024)} %param.25) | copy-start | bytes 12292
  35.5 6.3 %copy-start.1 = (f32[1024]{0:T(1024)S(1)}, f32[1024]{0:T(1024)}, u32[]{:S(2)}) copy-start(f32[1024]{0:T(1024)} %param.24) | copy-start | bytes 12292
  35.5 6.3 %copy-start.2 = (f32[1024]{0:T(1024)S(1)}, f32[1024]{0:T(1024)}, u32[]{:S(2)}) copy-start(f32[1024]{0:T(1024)} %param.26) | copy-start | bytes 12292
  35.5 6.3 %copy-start.5 = (f32[512]{0:T(512)S(1)}, f32[512]{0:T(512)}, u32[]{:S(2)}) copy-start(f32[512]{0:T(512)} %param.28) | copy-start | bytes 6148
  51.0 22.0 %all-to-all-start.2 = ((bf16[8,80,1024]{2,1,0:T(8,128)(2,1)}), bf16[8,80,1024]{2,1,0:T(8,128)(2,1)}, u32[]{:S(2)}, u32[]{:S(2)}) async-start(bf16[8,80,1024]{2,1,0:T(8,128)(2,1)} %bitcast.56), calls=%async_computation.2 | async-start | bytes 2621440 | tf_op jit(solution)/shard_map/all_to_all | solution.py:61
  62.6 5.2 %collective-permute-start.2 = (bf16[512,1024]{1,0:T(8,128)(2,1)}, bf16[512,1024]{1,0:T(8,128)(2,1)}, u32[]{:S(2)}, u32[]{:S(2)}) collective-permute-start(bf16[512,1024]{1,0:T(8,128)(2,1)} %get-tuple-element.102), channel_id=1, source_target_pairs={{0,8},{8,0},{16,24},{24,16},{32,40},{40,32},{48,56},{56,48},{64,72... | collective-permute-start | bytes 3145736 | tf_op jit(solution)/shard_map/ppermute | solution.py:69
  76.2 40.4 %all-to-all-start.3 = ((bf16[8,160,1024]{2,1,0:T(8,128)(2,1)}), bf16[8,160,1024]{2,1,0:T(8,128)(2,1)}, u32[]{:S(2)}, u32[]{:S(2)}) async-start(bf16[8,160,1024]{2,1,0:T(8,128)(2,1)} %get-tuple-element.106), calls=%async_computation.3 | async-start | bytes 5242880 | tf_op jit(solution)/shard_map/all_to_all | solution.py:61
  83.3 9.3 %collective-permute-start.3 = (bf16[2,64,1024]{2,1,0:T(8,128)(2,1)}, bf16[2,64,1024]{2,1,0:T(8,128)(2,1)S(1)}, u32[]{:S(2)}, u32[]{:S(2)}) collective-permute-start(bf16[2,64,1024]{2,1,0:T(8,128)(2,1)} %get-tuple-element.111), channel_id=1, source_target_pairs={{0,16},{8,24},{16,0},{24,8},{32,48},{40,56},{48,32},{56,40},{64,80... | collective-permute-start | bytes 786440 | tf_op jit(solution)/shard_map/ppermute | solution.py:69
  83.7 13.3 %collective-permute-start.4 = (bf16[2,64,1024]{2,1,0:T(8,128)(2,1)}, bf16[2,64,1024]{2,1,0:T(8,128)(2,1)S(1)}, u32[]{:S(2)}, u32[]{:S(2)}) collective-permute-start(bf16[2,64,1024]{2,1,0:T(8,128)(2,1)} %get-tuple-element.112), channel_id=1, source_target_pairs={{0,32},{8,40},{16,48},{24,56},{32,0},{40,8},{48,16},{56,24},{64,96... | collective-permute-start | bytes 786440 | tf_op jit(solution)/shard_map/ppermute | solution.py:69
  86.9 12.7 %collective-permute-start.5 = (bf16[2,64,1024]{2,1,0:T(8,128)(2,1)}, bf16[2,64,1024]{2,1,0:T(8,128)(2,1)S(1)}, u32[]{:S(2)}, u32[]{:S(2)}) collective-permute-start(bf16[2,64,1024]{2,1,0:T(8,128)(2,1)} %get-tuple-element.113), channel_id=1, source_target_pairs={{0,48},{8,56},{16,32},{24,40},{32,16},{40,24},{48,0},{56,8},{64,11... | collective-permute-start | bytes 786440 | tf_op jit(solution)/shard_map/ppermute | solution.py:69
  116.6 12.8 %collective-permute-start.6 = (bf16[2,64,1024]{2,1,0:T(8,128)(2,1)S(1)}, bf16[2,64,1024]{2,1,0:T(8,128)(2,1)S(1)}, u32[]{:S(2)}, u32[]{:S(2)}) collective-permute-start(bf16[2,64,1024]{2,1,0:T(8,128)(2,1)S(1)} %add_convert_fusion.1), channel_id=1, source_target_pairs={{0,64},{8,72},{16,80},{24,88},{32,96},{40,104},{48,112},{56,120},{... | collective-permute-start | bytes 786440 | tf_op jit(solution)/shard_map/ppermute | solution.py:69
  129.4 43.3 %all-to-all-start.4 = ((bf16[8,160,1024]{2,1,0:T(8,128)(2,1)}), bf16[8,160,1024]{2,1,0:T(8,128)(2,1)}, u32[]{:S(2)}, u32[]{:S(2)}) async-start(bf16[8,160,1024]{2,1,0:T(8,128)(2,1)} %get-tuple-element.122.part_ref), calls=%async_computation.4 | async-start | bytes 5242880 | tf_op jit(solution)/shard_map/all_to_all | solution.py:61
  133.9 10.8 %collective-permute-start.7 = (bf16[2,64,1024]{2,1,0:T(8,128)(2,1)S(1)}, bf16[2,64,1024]{2,1,0:T(8,128)(2,1)S(1)}, u32[]{:S(2)}, u32[]{:S(2)}) collective-permute-start(bf16[2,64,1024]{2,1,0:T(8,128)(2,1)S(1)} %add_convert_fusion), channel_id=1, source_target_pairs={{0,16},{8,24},{16,0},{24,8},{32,48},{40,56},{48,32},{56,40},{64,80... | collective-permute-start | bytes 786440 | tf_op jit(solution)/shard_map/ppermute | solution.py:69
  134.4 12.9 %collective-permute-start.8 = (bf16[2,64,1024]{2,1,0:T(8,128)(2,1)S(1)}, bf16[2,64,1024]{2,1,0:T(8,128)(2,1)S(1)}, u32[]{:S(2)}, u32[]{:S(2)}) collective-permute-start(bf16[2,64,1024]{2,1,0:T(8,128)(2,1)S(1)} %add_convert_fusion), channel_id=1, source_target_pairs={{0,32},{8,40},{16,48},{24,56},{32,0},{40,8},{48,16},{56,24},{64,96... | collective-permute-start | bytes 786440 | tf_op jit(solution)/shard_map/ppermute | solution.py:69
  137.6 12.3 %collective-permute-start.9 = (bf16[2,64,1024]{2,1,0:T(8,128)(2,1)S(1)}, bf16[2,64,1024]{2,1,0:T(8,128)(2,1)S(1)}, u32[]{:S(2)}, u32[]{:S(2)}) collective-permute-start(bf16[2,64,1024]{2,1,0:T(8,128)(2,1)S(1)} %add_convert_fusion), channel_id=1, source_target_pairs={{0,48},{8,56},{16,32},{24,40},{32,16},{40,24},{48,0},{56,8},{64,11... | collective-permute-start | bytes 786440 | tf_op jit(solution)/shard_map/ppermute | solution.py:69
  144.7 5.5 %copy-start.23 = (bf16[544,512]{1,0:T(8,128)(2,1)S(1)}, bf16[544,512]{1,0:T(8,128)(2,1)}, u32[]{:S(2)}) copy-start(bf16[544,512]{1,0:T(8,128)(2,1)} %get-tuple-element.132) | copy-start | bytes 1671172
  150.1 26.0 %copy-start.12 = (bf16[4,2,64,1024]{3,2,1,0:T(8,128)(2,1)}, bf16[4,2,64,1024]{3,2,1,0:T(8,128)(2,1)S(1)}, u32[]{:S(2)}) copy-start(bf16[4,2,64,1024]{3,2,1,0:T(8,128)(2,1)S(1)} %pad_maximum_fusion.1.own_ref) | copy-start | bytes 3145732
  150.1 19.6 %collective-permute-start.11 = (bf16[4,2,64,1024]{3,2,1,0:T(8,128)(2,1)S(1)}, bf16[4,2,64,1024]{3,2,1,0:T(8,128)(2,1)S(1)}, u32[]{:S(2)}, u32[]{:S(2)}) collective-permute-start(bf16[4,2,64,1024]{3,2,1,0:T(8,128)(2,1)S(1)} %pad_maximum_fusion.1.own_ref), channel_id=1, source_target_pairs={{0,8},{8,0},{16,24},{24,16},{32,40},{40,32},{48,56},{56,48},{64,72... | collective-permute-start | bytes 3145736 | tf_op jit(solution)/shard_map/ppermute | solution.py:69
  150.2 3.4 %collective-permute-start.10 = (bf16[544,512]{1,0:T(8,128)(2,1)S(1)}, bf16[544,512]{1,0:T(8,128)(2,1)S(1)}, u32[]{:S(2)}, u32[]{:S(2)}) collective-permute-start(bf16[544,512]{1,0:T(8,128)(2,1)S(1)} %copy-done.23), channel_id=1, source_target_pairs={{0,8},{8,0},{16,24},{24,16},{32,40},{40,32},{48,56},{56,48},{64,72... | collective-permute-start | bytes 1671176 | tf_op jit(solution)/shard_map/ppermute | solution.py:69
  153.6 0.8 copy-start.17
  156.5 7.3 %collective-permute-start.12 = (bf16[2,80,512]{2,1,0:T(8,128)(2,1)}, bf16[2,80,512]{2,1,0:T(8,128)(2,1)S(1)}, u32[]{:S(2)}, u32[]{:S(2)}) collective-permute-start(bf16[2,80,512]{2,1,0:T(8,128)(2,1)} %get-tuple-element.138), channel_id=1, source_target_pairs={{0,16},{8,24},{16,0},{24,8},{32,48},{40,56},{48,32},{56,40},{64,80... | collective-permute-start | bytes 491528 | tf_op jit(solution)/shard_map/ppermute | solution.py:69
  156.5 10.6 %collective-permute-start.13 = (bf16[2,80,512]{2,1,0:T(8,128)(2,1)}, bf16[2,80,512]{2,1,0:T(8,128)(2,1)S(1)}, u32[]{:S(2)}, u32[]{:S(2)}) collective-permute-start(bf16[2,80,512]{2,1,0:T(8,128)(2,1)} %get-tuple-element.139), channel_id=1, source_target_pairs={{0,32},{8,40},{16,48},{24,56},{32,0},{40,8},{48,16},{56,24},{64,96... | collective-permute-start | bytes 491528 | tf_op jit(solution)/shard_map/ppermute | solution.py:69
  159.1 10.6 %collective-permute-start.14 = (bf16[2,80,512]{2,1,0:T(8,128)(2,1)}, bf16[2,80,512]{2,1,0:T(8,128)(2,1)S(1)}, u32[]{:S(2)}, u32[]{:S(2)}) collective-permute-start(bf16[2,80,512]{2,1,0:T(8,128)(2,1)} %get-tuple-element.140), channel_id=1, source_target_pairs={{0,48},{8,56},{16,32},{24,40},{32,16},{40,24},{48,0},{56,8},{64,11... | collective-permute-start | bytes 491528 | tf_op jit(solution)/shard_map/ppermute | solution.py:69
  163.8 6.9 %copy-start.19 = (bf16[2,80,512]{2,1,0:T(8,128)(2,1)}, bf16[2,80,512]{2,1,0:T(8,128)(2,1)S(1)}, u32[]{:S(2)}) copy-start(bf16[2,80,512]{2,1,0:T(8,128)(2,1)S(1)} %collective-permute-done.12.one_ref) | copy-start | bytes 491524
  167.1 3.6 %copy-start.20 = (bf16[2,80,512]{2,1,0:T(8,128)(2,1)}, bf16[2,80,512]{2,1,0:T(8,128)(2,1)S(1)}, u32[]{:S(2)}) copy-start(bf16[2,80,512]{2,1,0:T(8,128)(2,1)S(1)} %collective-permute-done.13.two_ref) | copy-start | bytes 491524
  169.7 1.0 copy-start.21
  169.7 1.0 copy-start.15
  172.6 7.4 %collective-permute-start.15 = (bf16[2,80,512]{2,1,0:T(8,128)(2,1)}, bf16[2,80,512]{2,1,0:T(8,128)(2,1)}, u32[]{:S(2)}, u32[]{:S(2)}) collective-permute-start(bf16[2,80,512]{2,1,0:T(8,128)(2,1)} %get-tuple-element.151.own_ref), channel_id=1, source_target_pairs={{0,64},{8,72},{16,80},{24,88},{32,96},{40,104},{48,112},{56,120},{... | collective-permute-start | bytes 491528 | tf_op jit(solution)/shard_map/ppermute | solution.py:69
  176.0 15.7 %copy-start.3 = (f32[1024]{0:T(1024)S(1)}, f32[1024]{0:T(1024)}, u32[]{:S(2)}) copy-start(f32[1024]{0:T(1024)} %param.30) | copy-start | bytes 12292
  180.0 26.4 %all-to-all-start.5 = ((bf16[8,96,1024]{2,1,0:T(8,128)(2,1)}), bf16[8,96,1024]{2,1,0:T(8,128)(2,1)}, u32[]{:S(2)}, u32[]{:S(2)}) async-start(bf16[8,96,1024]{2,1,0:T(8,128)(2,1)} %shard_map.281), calls=%async_computation.5 | async-start | bytes 3145728 | tf_op jit(solution)/shard_map/all_to_all | solution.py:61
  186.9 12.0 %collective-permute-start.16 = (bf16[2,64,512]{2,1,0:T(8,128)(2,1)}, bf16[2,64,512]{2,1,0:T(8,128)(2,1)S(1)}, u32[]{:S(2)}, u32[]{:S(2)}) collective-permute-start(bf16[2,64,512]{2,1,0:T(8,128)(2,1)} %get-tuple-element.159), channel_id=1, source_target_pairs={{0,16},{8,24},{16,0},{24,8},{32,48},{40,56},{48,32},{56,40},{64,80... | collective-permute-start | bytes 393224 | tf_op jit(solution)/shard_map/ppermute | solution.py:69
  186.9 12.0 %collective-permute-start.17 = (bf16[2,64,512]{2,1,0:T(8,128)(2,1)}, bf16[2,64,512]{2,1,0:T(8,128)(2,1)S(1)}, u32[]{:S(2)}, u32[]{:S(2)}) collective-permute-start(bf16[2,64,512]{2,1,0:T(8,128)(2,1)} %get-tuple-element.159), channel_id=1, source_target_pairs={{0,32},{8,40},{16,48},{24,56},{32,0},{40,8},{48,16},{56,24},{64,96... | collective-permute-start | bytes 393224 | tf_op jit(solution)/shard_map/ppermute | solution.py:69
  190.6 8.4 %collective-permute-start.18 = (bf16[2,64,512]{2,1,0:T(8,128)(2,1)}, bf16[2,64,512]{2,1,0:T(8,128)(2,1)S(1)}, u32[]{:S(2)}, u32[]{:S(2)}) collective-permute-start(bf16[2,64,512]{2,1,0:T(8,128)(2,1)} %get-tuple-element.159), channel_id=1, source_target_pairs={{0,48},{8,56},{16,32},{24,40},{32,16},{40,24},{48,0},{56,8},{64,11... | collective-permute-start | bytes 393224 | tf_op jit(solution)/shard_map/ppermute | solution.py:69
  194.9 4.0 %copy-start.22 = (bf16[2,64,512]{2,1,0:T(8,128)(2,1)S(1)}, bf16[2,64,512]{2,1,0:T(8,128)(2,1)}, u32[]{:S(2)}) copy-start(bf16[2,64,512]{2,1,0:T(8,128)(2,1)} %get-tuple-element.159) | copy-start | bytes 393220
  199.0 2.0 copy-start.14
  199.1 2.0 collective-permute-start.19
  201.0 0.8 copy-start.18
  208.8 5.5 %collective-permute-start.20 = (f32[8,1024]{1,0:T(8,128)S(1)}, f32[8,1024]{1,0:T(8,128)S(1)}, u32[]{:S(2)}, u32[]{:S(2)}) collective-permute-start(f32[8,1024]{1,0:T(8,128)S(1)} %add_reduce_fusion), channel_id=1, source_target_pairs={{0,64},{8,72},{16,80},{24,88},{32,96},{40,104},{48,112},{56,120},{... | collective-permute-start | bytes 98312 | tf_op jit(solution)/shard_map/ppermute | solution.py:69

commit v4 on v3

--- a/solution.py
+++ b/solution.py
@@ -264,7 +264,7 @@
 
 
 def norm_two_back(
-    me_ref, got_ref, mid_ref, og_ref, gain_ref, mlp_ref, back_ref, send_ref, sum_ref
+    seq_len, me_ref, got_ref, mid_ref, og_ref, gain_ref, mlp_ref, back_ref, send_ref, sum_ref
 ):
     total = got_ref[0].astype(F32)
     for i in range(1, NT):
@@ -272,7 +272,8 @@
     xhat, recip = norm_stats(mid_ref[...])
     back = norm_backward(total, xhat, recip, gain_ref[...])
     back_ref[...] = back
-    branch = (og_ref[...] + back).astype(BF)
+    rows = me_ref[0] * BLK + lax.broadcasted_iota(jnp.int32, back.shape, 0)
+    branch = jnp.where(rows < seq_len, og_ref[...] + back, 0.0).astype(BF)
     for i in range(NT):
         send_ref[i] = branch
     sum_ref[0:1, :] = jnp.sum(total * xhat, 0, keepdims=True)
@@ -305,11 +306,12 @@
 
 def early_grads(where_ref, act_ref, low_ref, grad_ref, gelu_ref, keep_ref, give_ref, sum_ref):
     half = keep_ref.shape[0]
+    seq_len = grad_ref.shape[0]
     for ref, side in ((keep_ref, where_ref[1]), (give_ref, 1 - where_ref[1])):
         cols = pl.ds(pl.multiple_of(side * half, half), half)
         ref[:, :512] = dot_tn(act_ref[:, cols], low_ref[...]).astype(BF)
-        ref[:, 512:] = dot_tn(grad_ref[:, cols], gelu_ref[...]).astype(BF)
-    sum_ref[...] = jnp.sum(grad_ref[...].astype(F32), 0, keepdims=True)
+        ref[:, 512:] = dot_tn(grad_ref[:, cols].astype(BF), gelu_ref[:seq_len, :]).astype(BF)
+    sum_ref[...] = jnp.sum(grad_ref[...].astype(BF).astype(F32), 0, keepdims=True)
 
 
 def split(v):
@@ -539,7 +541,6 @@
     grad_pad = pad_rows(out_grad.astype(BF))
     gelu_in_grad = dot_nt(grad_pad, down_weight)
     hid_pad = pad_rows(hidden_in)
-    out_grad_pad = pad_rows(out_grad)
 
     rows = 320
     tile = lambda w: pl.BlockSpec((rows, w), lambda i: (i, 0))
@@ -593,7 +594,7 @@
     e_keep, e_give, down_bias_part = simple_at(
         early_grads,
         [shaped(512, width, dtype=BF), shaped(512, width, dtype=BF), shaped(1, width)],
-        where, act_two, up_low, grad_pad, gelu_low,
+        where, act_two, up_low, out_grad, gelu_low,
     )
     e_core = hop(e_give, 1)
     two_got, e_core, mlp_part = tie(two_got, e_core, mlp_part)
@@ -601,7 +602,7 @@
     mine = pl.BlockSpec((BLK, width), lambda i, m: (m[0], 0))
     zero = lambda *shape: pl.BlockSpec(shape, lambda i, m: (0,) * len(shape))
     back_two, branch_send, sums_two = pl.pallas_call(
-        norm_two_back,
+        partial(norm_two_back, seq_len),
         out_shape=[shaped(BLK, width), shaped(NT, 2 * BLK, width, dtype=BF), shaped(8, width)],
         grid_spec=pltpu.PrefetchScalarGridSpec(
             num_scalar_prefetch=1,
@@ -617,7 +618,7 @@
         cost_estimate=TINY,
     )(
         me.reshape(1),
-        *far(two_got, middle, out_grad_pad),
+        *far(two_got, middle, out_grad),
         row(ln2_gain),
         *far(mlp_part),
     )

time: 216 us -> 215 us (level)
  waiting for transfers between devices: 71.5 us -> 73.8 us
    all_to_all x6, waiting for transfers between devices: 28.6 us -> 33.6 us  [exchange(): return lax.all_to_all(a, axis, 0, 0, tiled=True)]
    pad x3 -> x1, local copies, waits for them, and re-layouts: 5.96 us -> 1.71 us  [pad_rows(): return jnp.pad(a, ((0, PAD - a.shape[0]), (0, 0)))]
    unnamed x48 -> x60, local copies, waits for them, and re-layouts: 4.92 us -> 7.79 us
    ppermute x21, waiting for transfers between devices: 42.8 us -> 40.2 us  [hop(): return lax.ppermute(a, DP, [(i, i ^ mask) for i in range(16)])]
  transfers between devices with their start and end apart: 27 -> 27, of which waited for: 18 -> 18; matrix products, arithmetic and copies ran while one was open for 6% -> 4% of each run, Pallas kernels for 25% -> 25%
where the time goes in v4:
time: 215 us; the launch traced here: 214 us
  waiting for transfers between devices  73.8 us (34%)
  Pallas kernels  65.5 us (30%)
  starting transfers between devices  53.5 us (25%)
  local copies, waits for them, and re-layouts  13.4 us (6%)
  other arithmetic  4.75 us (2%)
    ppermute x21, waiting for transfers between devices, hop(): return lax.ppermute(a, DP, [(i, i ^ mask) for i in range(16)])  40.2 us
    all_to_all x6, waiting for transfers between devices, exchange(): return lax.all_to_all(a, axis, 0, 0, tiled=True)  33.6 us
    ppermute x21, starting transfers between devices, hop(): return lax.ppermute(a, DP, [(i, i ^ mask) for i in range(16)])  27.3 us
    all_to_all x6, starting transfers between devices, exchange(): return lax.all_to_all(a, axis, 0, 0, tiled=True)  26.3 us
    pallas_call x3, Pallas kernels, simple_at(): pl.pallas_call(kernel, out_shape=outs, in_specs=[SMEM_SPEC] + whole(len(a...  10.1 us
    pallas_call x1, Pallas kernels, per_device(): pl.pallas_call(attend_backward, out_shape=[shaped(PAD, 384, dtype=BF), sh...  9.29 us
    pallas_call x1, Pallas kernels, per_device(): pl.pallas_call(feed, grid=(PAD // rows,), out_shape=[shaped(PAD, width),...  9.12 us
    pallas_call x1, Pallas kernels, per_device(): pl.pallas_call(attend_forward, out_shape=[shaped(seq_len, width, dtype=BF...  7.83 us
  transfers between devices with their start and end apart: 27, of which 18 were waited for; matrix products, arithmetic and copies ran while one was open for 4% of the time, Pallas kernels for 25%

profile of v4, /device:TPU:0, one launch (start us, length us, event | category | flops | bytes accessed | tf_op | source)
XLA Modules:
  0.0 213.9 jit_solution(9982138662321884668)
XLA Ops:
  0.7 0.8 constant_dynamic-slice_fusion
  1.6 0.9 broadcast_in_dim.2
  2.4 5.7 %all-to-all-start = ((bf16[8,32,1024]{2,1,0:T(8,128)(2,1)}), bf16[8,32,1024]{2,1,0:T(8,128)(2,1)S(1)}, u32[]{:S(2)}, u32[]{:S(2)}) async-start(bf16[8,32,1024]{2,1,0:T(8,128)(2,1)} %broadcast_in_dim.2), calls=%async_computation | async-start | bytes 1048576 | tf_op jit(solution)/shard_map/all_to_all | solution.py:61
  8.5 7.8 %shard_map.271 = (bf16[608,1024]{1,0:T(8,128)(2,1)}, bf16[608,384]{1,0:T(8,128)(2,1)}, bf16[608,128]{1,0:T(8,128)(2,1)}, bf16[8,640,128]{2,1,0:T(8,128)(2,1)}, f32[2,608,1]{2,1,0:T(8,128)}) custom-call(s32[3]{0:T(128)S(1)} %pad_add_fusion.1.where_ref, f32[608,1024]{1,0:T(8,128)} %hid_ref.3, f32[1,1024]{1,0:T(1,128)S(1)} %bitcast.51, f32[1,1024]{1,0:T(1,128)S(1)} %bitcast.50, ...), custom_call_target="tpu_custom_call" | custom-call | flops 4294967296 | bytes 25165824 | tf_op jit(solution)/shard_map/pallas_call | solution.py:508
  16.3 1.4 all-to-all-done
  17.7 1.6 collective-permute-start
  19.2 4.4 %all-to-all-start.1 = ((bf16[8,640,128]{2,1,0:T(8,128)(2,1)}), bf16[8,640,128]{2,1,0:T(8,128)(2,1)S(1)}, u32[]{:S(2)}, u32[]{:S(2)}) async-start(bf16[8,640,128]{2,1,0:T(8,128)(2,1)} %get-tuple-element.96), calls=%async_computation.1 | async-start | bytes 2621440 | tf_op jit(solution)/shard_map/all_to_all | solution.py:61
  23.6 6.7 %collective-permute-done = bf16[8,32,1024]{2,1,0:T(8,128)(2,1)S(1)} collective-permute-done((bf16[8,32,1024]{2,1,0:T(8,128)(2,1)S(1)}, bf16[8,32,1024]{2,1,0:T(8,128)(2,1)S(1)}, u32[]{:S(2)}, u32[]{:S(2)}) %collective-permute-start) | collective-permute-done | bytes 524320 | tf_op jit(solution)/shard_map/ppermute | solution.py:69
  30.6 1.8 copy-done.10
  33.1 1.7 pad.8.hid_ref
  34.8 1.9 fusion.gin_ref
  36.8 4.9 %all-to-all-done.1.ctx_ref = bf16[8,640,128]{2,1,0:T(8,128)(2,1)S(1)} async-done(((bf16[8,640,128]{2,1,0:T(8,128)(2,1)}), bf16[8,640,128]{2,1,0:T(8,128)(2,1)S(1)}, u32[]{:S(2)}, u32[]{:S(2)}) %all-to-all-start.1) | async-done | bytes 1310752 | tf_op jit(solution)/shard_map/all_to_all | solution.py:61
  41.7 1.1 copy-done.13
  42.8 9.1 %shard_map.272 = (f32[640,1024]{1,0:T(8,128)}, bf16[640,1024]{1,0:T(8,128)(2,1)}, bf16[640,512]{1,0:T(8,128)(2,1)}, bf16[640,512]{1,0:T(8,128)(2,1)}, bf16[640,1024]{1,0:T(8,128)(2,1)}, /*index=5*/f32[1,512]{1,0:T(1,128)}) custom-call(bf16[8,640,128]{2,1,0:T(8,128)(2,1)} %copy-done.13, bf16[512,1024]{1,0:T(8,128)(2,1)} %bitcast.57, ...), custom_call_target="tpu_custom_call" | custom-call | flops 1 | bytes 1 | tf_op jit(solution)/shard_map/pallas_call | solution.py:548
  51.9 3.6 %all-to-all-start.2 = ((bf16[8,80,1024]{2,1,0:T(8,128)(2,1)}), bf16[8,80,1024]{2,1,0:T(8,128)(2,1)S(1)}, u32[]{:S(2)}, u32[]{:S(2)}) async-start(bf16[8,80,1024]{2,1,0:T(8,128)(2,1)} %bitcast.58), calls=%async_computation.2 | async-start | bytes 2621440 | tf_op jit(solution)/shard_map/all_to_all | solution.py:61
  55.5 5.3 %shard_map.273 = (bf16[512,1024]{1,0:T(8,128)(2,1)}, bf16[512,1024]{1,0:T(8,128)(2,1)}, f32[1,1024]{1,0:T(1,128)}) custom-call(s32[3]{0:T(128)S(1)} %pad_add_fusion.1.where_ref, bf16[640,1024]{1,0:T(8,128)(2,1)} %get-tuple-element.99.act_ref, bf16[640,512]{1,0:T(8,128)(2,1)} %get-tuple-element.100.low_ref, f32[608,1024]{1,0:T(8,128)} %og_ref.1, ...), custom_call_target="tpu_custom_call" | custom-call | flops 1 | bytes 1 | tf_op jit(solution)/shard_map/pallas_call | solution.py:444
  60.8 3.4 %shard_map.274.mlp_ref = bf16[8,160,1024]{2,1,0:T(8,128)(2,1)} custom-call(bf16[640,512]{1,0:T(8,128)(2,1)} %get-tuple-element.101.gelu_ref, bf16[512,1024]{1,0:T(8,128)(2,1)} %w_ref.4), custom_call_target="tpu_custom_call" | custom-call | flops 1 | bytes 1 | tf_op jit(solution)/shard_map/pallas_call | solution.py:585
  64.1 9.0 %all-to-all-done.2.got_ref = bf16[8,80,1024]{2,1,0:T(8,128)(2,1)S(1)} async-done(((bf16[8,80,1024]{2,1,0:T(8,128)(2,1)}), bf16[8,80,1024]{2,1,0:T(8,128)(2,1)S(1)}, u32[]{:S(2)}, u32[]{:S(2)}) %all-to-all-start.2) | async-done | bytes 1310752 | tf_op jit(solution)/shard_map/all_to_all | solution.py:61
  73.2 1.1 copy-done.14
  74.2 3.2 %shard_map.275 = (f32[80,1024]{1,0:T(8,128)}, bf16[8,160,1024]{2,1,0:T(8,128)(2,1)}, f32[8,1024]{1,0:T(8,128)}) custom-call(s32[1]{0:T(128)} %bitcast.2.me_ref, bf16[8,80,1024]{2,1,0:T(8,128)(2,1)} %copy-done.14, f32[640,1024]{1,0:T(8,128)} %get-tuple-element.104.mid_ref, f32[608,1024]{1,0:T(8,128)} %og_ref.1, ...), custom_call_target="tpu_custom_call", output_to_operand_aliasing={{1}: (5, {})} | custom-call | flops 1 | bytes 1 | tf_op jit(solution)/shard_map/pallas_call | solution.py:604
  77.4 3.6 %all-to-all-start.3 = ((bf16[8,160,1024]{2,1,0:T(8,128)(2,1)}), bf16[8,160,1024]{2,1,0:T(8,128)(2,1)S(1)}, u32[]{:S(2)}, u32[]{:S(2)}) async-start(bf16[8,160,1024]{2,1,0:T(8,128)(2,1)} %get-tuple-element.106), calls=%async_computation.3 | async-start | bytes 5242880 | tf_op jit(solution)/shard_map/all_to_all | solution.py:61
  81.0 2.7 %shard_map.276 = (bf16[2,64,1024]{2,1,0:T(8,128)(2,1)}, bf16[2,64,1024]{2,1,0:T(8,128)(2,1)}, bf16[2,64,1024]{2,1,0:T(8,128)(2,1)}, bf16[2,64,1024]{2,1,0:T(8,128)(2,1)}) custom-call(s32[3]{0:T(128)S(1)} %pad_add_fusion.1.where_ref, bf16[2,4,64,1024]{3,2,1,0:T(8,128)(2,1)} %bitcast.59, bf16[2,4,64,1024]{3,2,1,0:T(8,128)(2,1)} %bitcast.18.got_ref), custom_call_target="tpu_custom_call" | custom-call | flops 1 | bytes 1 | tf_op jit(solution)/shard_map/pallas_call | solution.py:444
  84.2 3.2 %collective-permute-start.4 = (bf16[2,64,1024]{2,1,0:T(8,128)(2,1)}, bf16[2,64,1024]{2,1,0:T(8,128)(2,1)S(1)}, u32[]{:S(2)}, u32[]{:S(2)}) collective-permute-start(bf16[2,64,1024]{2,1,0:T(8,128)(2,1)} %get-tuple-element.112), channel_id=1, source_target_pairs={{0,32},{8,40},{16,48},{24,56},{32,0},{40,8},{48,16},{56,24},{64,96... | collective-permute-start | bytes 786440 | tf_op jit(solution)/shard_map/ppermute | solution.py:69
  87.4 1.1 collective-permute-start.5
  88.4 4.6 %collective-permute-done.3 = bf16[2,64,1024]{2,1,0:T(8,128)(2,1)S(1)} collective-permute-done((bf16[2,64,1024]{2,1,0:T(8,128)(2,1)}, bf16[2,64,1024]{2,1,0:T(8,128)(2,1)S(1)}, u32[]{:S(2)}, u32[]{:S(2)}) %collective-permute-start.3) | collective-permute-done | bytes 262176 | tf_op jit(solution)/shard_map/ppermute | solution.py:69
  93.0 4.5 %collective-permute-done.4 = bf16[2,64,1024]{2,1,0:T(8,128)(2,1)S(1)} collective-permute-done((bf16[2,64,1024]{2,1,0:T(8,128)(2,1)}, bf16[2,64,1024]{2,1,0:T(8,128)(2,1)S(1)}, u32[]{:S(2)}, u32[]{:S(2)}) %collective-permute-start.4) | collective-permute-done | bytes 262176 | tf_op jit(solution)/shard_map/ppermute | solution.py:69
  97.5 2.6 %collective-permute-done.5 = bf16[2,64,1024]{2,1,0:T(8,128)(2,1)S(1)} collective-permute-done((bf16[2,64,1024]{2,1,0:T(8,128)(2,1)}, bf16[2,64,1024]{2,1,0:T(8,128)(2,1)S(1)}, u32[]{:S(2)}, u32[]{:S(2)}) %collective-permute-start.5) | collective-permute-done | bytes 262176 | tf_op jit(solution)/shard_map/ppermute | solution.py:69
  100.1 1.1 add_convert_fusion.1
  101.2 15.8 %all-to-all-done.3.branch_ref = bf16[8,160,1024]{2,1,0:T(8,128)(2,1)S(1)} async-done(((bf16[8,160,1024]{2,1,0:T(8,128)(2,1)}), bf16[8,160,1024]{2,1,0:T(8,128)(2,1)S(1)}, u32[]{:S(2)}, u32[]{:S(2)}) %all-to-all-start.3) | async-done | bytes 2621472 | tf_op jit(solution)/shard_map/all_to_all | solution.py:61
  117.0 3.6 %collective-permute-start.6 = (bf16[2,64,1024]{2,1,0:T(8,128)(2,1)S(1)}, bf16[2,64,1024]{2,1,0:T(8,128)(2,1)S(1)}, u32[]{:S(2)}, u32[]{:S(2)}) collective-permute-start(bf16[2,64,1024]{2,1,0:T(8,128)(2,1)S(1)} %add_convert_fusion.1), channel_id=1, source_target_pairs={{0,64},{8,72},{16,80},{24,88},{32,96},{40,104},{48,112},{56,120},{... | collective-permute-start | bytes 786440 | tf_op jit(solution)/shard_map/ppermute | solution.py:69
  120.5 9.3 %shard_map.277 = (bf16[640,384]{1,0:T(8,128)(2,1)}, bf16[8,160,1024]{2,1,0:T(8,128)(2,1)}) custom-call(s32[3]{0:T(128)S(1)} %pad_add_fusion.1.where_ref, bf16[8,160,1024]{2,1,0:T(8,128)(2,1)} %copy-done.17, bf16[128,1024]{1,0:T(8,128)(2,1)} %wd_ref.1, bf16[608,384]{1,0:T(8,128)(2,1)} %get-tuple-element.118.qkv_ref, f32[2,608,1]{2,1,0:T(8,128)} %get-tuple-element.119.lse_ref, ...), custom_call_target="tpu_custom_call" | custom-call | flops 4294967296 | bytes 25165824 | tf_op jit(solution)/shard_map/pallas_call | solution.py:638
  129.8 3.6 %all-to-all-start.4 = ((bf16[8,160,1024]{2,1,0:T(8,128)(2,1)}), bf16[8,160,1024]{2,1,0:T(8,128)(2,1)S(1)}, u32[]{:S(2)}, u32[]{:S(2)}) async-start(bf16[8,160,1024]{2,1,0:T(8,128)(2,1)} %get-tuple-element.122.part_ref), calls=%async_computation.4 | async-start | bytes 5242880 | tf_op jit(solution)/shard_map/all_to_all | solution.py:61
  133.6 2.3 %collective-permute-start.9 = (bf16[2,64,1024]{2,1,0:T(8,128)(2,1)S(1)}, bf16[2,64,1024]{2,1,0:T(8,128)(2,1)S(1)}, u32[]{:S(2)}, u32[]{:S(2)}) collective-permute-start(bf16[2,64,1024]{2,1,0:T(8,128)(2,1)S(1)} %add_convert_fusion), channel_id=1, source_target_pairs={{0,48},{8,56},{16,32},{24,40},{32,16},{40,24},{48,0},{56,8},{64,11... | collective-permute-start | bytes 786440 | tf_op jit(solution)/shard_map/ppermute | solution.py:69
  135.8 0.8 collective-permute-start.8
  136.6 1.1 collective-permute-start.7
  137.7 6.0 %shard_map.278 = (bf16[512,512]{1,0:T(8,128)(2,1)}, bf16[544,512]{1,0:T(8,128)(2,1)}, f32[16,512]{1,0:T(8,128)}) custom-call(s32[3]{0:T(128)S(1)} %pad_add_fusion.1.where_ref, bf16[608,1024]{1,0:T(8,128)(2,1)} %get-tuple-element.123.act_ref, bf16[640,384]{1,0:T(8,128)(2,1)} %get-tuple-element.124.grad_ref, bf16[8,160,1024]{2,1,0:T(8,128)(2,1)} %copy-done.17, ...), custom_call_target="tpu_custom_call" | custom-call | flops 4294967296 | bytes 25165824 | tf_op jit(solution)/shard_map/pallas_call | solution.py:432
  143.8 2.7 %collective-permute-done.9 = bf16[2,64,1024]{2,1,0:T(8,128)(2,1)S(1)} collective-permute-done((bf16[2,64,1024]{2,1,0:T(8,128)(2,1)S(1)}, bf16[2,64,1024]{2,1,0:T(8,128)(2,1)S(1)}, u32[]{:S(2)}, u32[]{:S(2)}) %collective-permute-start.9) | collective-permute-done | bytes 262176 | tf_op jit(solution)/shard_map/ppermute | solution.py:69
  147.9 2.9 %collective-permute-done.10.got_ref = bf16[544,512]{1,0:T(8,128)(2,1)S(1)} collective-permute-done((bf16[544,512]{1,0:T(8,128)(2,1)S(1)}, bf16[544,512]{1,0:T(8,128)(2,1)S(1)}, u32[]{:S(2)}, u32[]{:S(2)}) %collective-permute-start.10) | collective-permute-done | bytes 557088 | tf_op jit(solution)/shard_map/ppermute | solution.py:69
  150.8 0.8 copy-done.22
  151.6 2.1 shard_map.279
  153.8 1.2 collective-permute-start.12
  155.0 2.4 %collective-permute-start.13 = (bf16[2,80,512]{2,1,0:T(8,128)(2,1)}, bf16[2,80,512]{2,1,0:T(8,128)(2,1)S(1)}, u32[]{:S(2)}, u32[]{:S(2)}) collective-permute-start(bf16[2,80,512]{2,1,0:T(8,128)(2,1)} %get-tuple-element.139), channel_id=1, source_target_pairs={{0,32},{8,40},{16,48},{24,56},{32,0},{40,8},{48,16},{56,24},{64,96... | collective-permute-start | bytes 491528 | tf_op jit(solution)/shard_map/ppermute | solution.py:69
  157.4 1.1 collective-permute-start.14
  158.5 2.6 %collective-permute-done.12.one_ref = bf16[2,80,512]{2,1,0:T(8,128)(2,1)S(1)} collective-permute-done((bf16[2,80,512]{2,1,0:T(8,128)(2,1)}, bf16[2,80,512]{2,1,0:T(8,128)(2,1)S(1)}, u32[]{:S(2)}, u32[]{:S(2)}) %collective-permute-start.12) | collective-permute-done | bytes 163872 | tf_op jit(solution)/shard_map/ppermute | solution.py:69
  161.0 4.4 %collective-permute-done.13.two_ref = bf16[2,80,512]{2,1,0:T(8,128)(2,1)S(1)} collective-permute-done((bf16[2,80,512]{2,1,0:T(8,128)(2,1)}, bf16[2,80,512]{2,1,0:T(8,128)(2,1)S(1)}, u32[]{:S(2)}, u32[]{:S(2)}) %collective-permute-start.13) | collective-permute-done | bytes 163872 | tf_op jit(solution)/shard_map/ppermute | solution.py:69
  165.4 2.6 %collective-permute-done.14.three_ref = bf16[2,80,512]{2,1,0:T(8,128)(2,1)S(1)} collective-permute-done((bf16[2,80,512]{2,1,0:T(8,128)(2,1)}, bf16[2,80,512]{2,1,0:T(8,128)(2,1)S(1)}, u32[]{:S(2)}, u32[]{:S(2)}) %collective-permute-start.14) | collective-permute-done | bytes 163872 | tf_op jit(solution)/shard_map/ppermute | solution.py:69
  169.0 1.9 shard_map.280
  170.9 1.9 collective-permute-start.15
  172.8 3.1 %shard_map.281 = bf16[8,96,1024]{2,1,0:T(8,128)(2,1)} custom-call(s32[1]{0:T(128)} %bitcast.2.me_ref, bf16[8,160,1024]{2,1,0:T(8,128)(2,1)} %copy-done.12, f32[640,1024]{1,0:T(8,128)} %pad.8.hid_ref, f32[80,1024]{1,0:T(8,128)} %get-tuple-element.149.back_ref, f32[1,1024]{1,0:T(1,128)S(1)} %bitcast.52, f32[16,512]{1,0:T(8,128)} %get-tuple-element.150.vec_ref), custom_call_target="tpu_custom_call" | custom-call | flops 4294967296 | bytes 25165824 | tf_op jit(solution)/shard_map/pallas_call | solution.py:671
  175.9 2.3 %collective-permute-done.15.got_ref = bf16[2,80,512]{2,1,0:T(8,128)(2,1)S(1)} collective-permute-done((bf16[2,80,512]{2,1,0:T(8,128)(2,1)}, bf16[2,80,512]{2,1,0:T(8,128)(2,1)S(1)}, u32[]{:S(2)}, u32[]{:S(2)}) %collective-permute-start.15) | collective-permute-done | bytes 163872 | tf_op jit(solution)/shard_map/ppermute | solution.py:69
  178.9 5.3 %all-to-all-start.5 = ((bf16[8,96,1024]{2,1,0:T(8,128)(2,1)}), bf16[8,96,1024]{2,1,0:T(8,128)(2,1)}, u32[]{:S(2)}, u32[]{:S(2)}) async-start(bf16[8,96,1024]{2,1,0:T(8,128)(2,1)} %shard_map.281), calls=%async_computation.5 | async-start | bytes 3145728 | tf_op jit(solution)/shard_map/all_to_all | solution.py:61
  184.2 1.7 shard_map.284
  185.9 1.1 collective-permute-start.18
  187.3 2.7 %collective-permute-start.16 = (bf16[2,64,512]{2,1,0:T(8,128)(2,1)}, bf16[2,64,512]{2,1,0:T(8,128)(2,1)S(1)}, u32[]{:S(2)}, u32[]{:S(2)}) collective-permute-start(bf16[2,64,512]{2,1,0:T(8,128)(2,1)} %get-tuple-element.159), channel_id=1, source_target_pairs={{0,16},{8,24},{16,0},{24,8},{32,48},{40,56},{48,32},{56,40},{64,80... | collective-permute-start | bytes 393224 | tf_op jit(solution)/shard_map/ppermute | solution.py:69
  190.1 3.2 %shard_map.283 = f32[608,1024]{1,0:T(8,128)} custom-call(f32[640,1024]{1,0:T(8,128)} %get-tuple-element.104.mid_ref, bf16[8,160,1024]{2,1,0:T(8,128)(2,1)} %copy-done.12, f32[1,1024]{1,0:T(1,128)S(1)} %bitcast.47), custom_call_target="tpu_custom_call" | custom-call | flops 1048576 | bytes 10485760 | tf_op jit(solution)/shard_map/pallas_call | solution.py:694
  193.3 4.0 %shard_map.282 = (f32[1024,512]{1,0:T(8,128)}, f32[512,1024]{1,0:T(8,128)}) custom-call(s32[2]{0:T(128)S(1)} %pad_add_fusion.where_ref, bf16[4,2,64,1024]{3,2,1,0:T(8,128)(2,1)} %copy-done.16, bf16[4,2,64,1024]{3,2,1,0:T(8,128)(2,1)} %copy-done.20), custom_call_target="tpu_custom_call" | custom-call | flops 1048576 | bytes 10485760 | tf_op jit(solution)/shard_map/pallas_call | solution.py:112
  197.5 1.9 collective-permute-done.19.other_ref
  200.2 2.7 %shard_map.285 = (f32[1024,384]{1,0:T(8,128)}, f32[128,1024]{1,0:T(8,128)}) custom-call(s32[2]{0:T(128)S(1)} %pad_add_fusion.where_ref, bf16[4,2,64,512]{3,2,1,0:T(8,128)(2,1)} %copy-done.19, bf16[4,2,64,512]{3,2,1,0:T(8,128)(2,1)} %copy-done.23), custom_call_target="tpu_custom_call" | custom-call | flops 1048576 | bytes 10485760 | tf_op jit(solution)/shard_map/pallas_call | solution.py:112
  202.9 2.5 %all-to-all-done.5 = bf16[8,96,1024]{2,1,0:T(8,128)(2,1)} async-done(((bf16[8,96,1024]{2,1,0:T(8,128)(2,1)}), bf16[8,96,1024]{2,1,0:T(8,128)(2,1)}, u32[]{:S(2)}, u32[]{:S(2)}) %all-to-all-start.5) | async-done | bytes 1572896 | tf_op jit(solution)/shard_map/all_to_all | solution.py:61
  205.4 1.0 add_reduce_fusion
  206.4 1.4 slice.27
  207.8 1.9 collective-permute-start.20
  209.7 1.9 convert_add_fusion
  211.5 1.8 collective-permute-done.20
  (84 shorter events, 6.9 us)
Async XLA Ops:
  0.6 7.6 %copy-start.4 = (s32[1,608]{1,0:T(1,128)S(1)}, s32[1,608]{1,0:T(1,128)}, u32[]{:S(2)}) copy-start(s32[1,608]{1,0:T(1,128)} %srow_ref.3) | copy-start | bytes 7300
  0.7 7.8 %copy-start.9 = (f32[128]{0:T(128)S(1)}, f32[128]{0:T(128)}, u32[]{:S(2)}) copy-start(f32[128]{0:T(128)} %param.22) | copy-start | bytes 1540
  0.7 7.8 %copy-start.8 = (f32[128]{0:T(128)S(1)}, f32[128]{0:T(128)}, u32[]{:S(2)}) copy-start(f32[128]{0:T(128)} %param.21) | copy-start | bytes 1540
  0.7 7.8 %copy-start.6 = (f32[1024]{0:T(1024)S(1)}, f32[1024]{0:T(1024)}, u32[]{:S(2)}) copy-start(f32[1024]{0:T(1024)} %param.19) | copy-start | bytes 12292
  0.7 7.8 %copy-start.7 = (f32[1024]{0:T(1024)S(1)}, f32[1024]{0:T(1024)}, u32[]{:S(2)}) copy-start(f32[1024]{0:T(1024)} %param.18) | copy-start | bytes 12292
  2.4 15.2 %all-to-all-start = ((bf16[8,32,1024]{2,1,0:T(8,128)(2,1)}), bf16[8,32,1024]{2,1,0:T(8,128)(2,1)S(1)}, u32[]{:S(2)}, u32[]{:S(2)}) async-start(bf16[8,32,1024]{2,1,0:T(8,128)(2,1)} %broadcast_in_dim.2), calls=%async_computation | async-start | bytes 1048576 | tf_op jit(solution)/shard_map/all_to_all | solution.py:61
  17.7 12.6 %collective-permute-start = (bf16[8,32,1024]{2,1,0:T(8,128)(2,1)S(1)}, bf16[8,32,1024]{2,1,0:T(8,128)(2,1)S(1)}, u32[]{:S(2)}, u32[]{:S(2)}) collective-permute-start(bf16[8,32,1024]{2,1,0:T(8,128)(2,1)S(1)} %all-to-all-done), channel_id=1, source_target_pairs={{0,16},{8,24},{16,0},{24,8},{32,48},{40,56},{48,32},{56,40},{64,80... | collective-permute-start | bytes 1572872 | tf_op jit(solution)/shard_map/ppermute | solution.py:69
  19.2 22.5 %all-to-all-start.1 = ((bf16[8,640,128]{2,1,0:T(8,128)(2,1)}), bf16[8,640,128]{2,1,0:T(8,128)(2,1)S(1)}, u32[]{:S(2)}, u32[]{:S(2)}) async-start(bf16[8,640,128]{2,1,0:T(8,128)(2,1)} %get-tuple-element.96), calls=%async_computation.1 | async-start | bytes 2621440 | tf_op jit(solution)/shard_map/all_to_all | solution.py:61
  30.3 2.1 copy-start.10
  30.5 2.1 copy-start.15
  30.5 2.6 %copy-start.18 = (f32[608,1024]{1,0:T(8,128)S(1)}, f32[608,1024]{1,0:T(8,128)}, u32[]{:S(2)}) copy-start(f32[608,1024]{1,0:T(8,128)} %hid_ref.3) | copy-start | bytes 7471108
  30.5 11.2 %collective-permute-start.1 = (bf16[512,1024]{1,0:T(8,128)(2,1)S(1)}, bf16[512,1024]{1,0:T(8,128)(2,1)}, u32[]{:S(2)}, u32[]{:S(2)}) collective-permute-start(bf16[512,1024]{1,0:T(8,128)(2,1)S(1)} %bitcast.56), channel_id=1, source_target_pairs={{0,8},{8,0},{16,24},{24,16},{32,40},{40,32},{48,56},{56,48},{64,72... | collective-permute-start | bytes 3145736 | tf_op jit(solution)/shard_map/ppermute | solution.py:69
  33.1 1.7 copy-start.21
  34.8 8.0 %copy-start = (f32[1024]{0:T(1024)S(1)}, f32[1024]{0:T(1024)}, u32[]{:S(2)}) copy-start(f32[1024]{0:T(1024)} %param.25) | copy-start | bytes 12292
  34.8 8.0 %copy-start.1 = (f32[1024]{0:T(1024)S(1)}, f32[1024]{0:T(1024)}, u32[]{:S(2)}) copy-start(f32[1024]{0:T(1024)} %param.24) | copy-start | bytes 12292
  34.8 8.0 %copy-start.2 = (f32[1024]{0:T(1024)S(1)}, f32[1024]{0:T(1024)}, u32[]{:S(2)}) copy-start(f32[1024]{0:T(1024)} %param.26) | copy-start | bytes 12292
  34.8 8.0 %copy-start.5 = (f32[512]{0:T(512)S(1)}, f32[512]{0:T(512)}, u32[]{:S(2)}) copy-start(f32[512]{0:T(512)} %param.28) | copy-start | bytes 6148
  41.7 1.1 copy-start.13
  51.9 21.3 %all-to-all-start.2 = ((bf16[8,80,1024]{2,1,0:T(8,128)(2,1)}), bf16[8,80,1024]{2,1,0:T(8,128)(2,1)S(1)}, u32[]{:S(2)}, u32[]{:S(2)}) async-start(bf16[8,80,1024]{2,1,0:T(8,128)(2,1)} %bitcast.58), calls=%async_computation.2 | async-start | bytes 2621440 | tf_op jit(solution)/shard_map/all_to_all | solution.py:61
  60.8 3.4 %collective-permute-start.2 = (bf16[512,1024]{1,0:T(8,128)(2,1)}, bf16[512,1024]{1,0:T(8,128)(2,1)}, u32[]{:S(2)}, u32[]{:S(2)}) collective-permute-start(bf16[512,1024]{1,0:T(8,128)(2,1)} %get-tuple-element.102), channel_id=1, source_target_pairs={{0,8},{8,0},{16,24},{24,16},{32,40},{40,32},{48,56},{56,48},{64,72... | collective-permute-start | bytes 3145736 | tf_op jit(solution)/shard_map/ppermute | solution.py:69
  73.2 1.1 copy-start.14
  77.4 39.6 %all-to-all-start.3 = ((bf16[8,160,1024]{2,1,0:T(8,128)(2,1)}), bf16[8,160,1024]{2,1,0:T(8,128)(2,1)S(1)}, u32[]{:S(2)}, u32[]{:S(2)}) async-start(bf16[8,160,1024]{2,1,0:T(8,128)(2,1)} %get-tuple-element.106), calls=%async_computation.3 | async-start | bytes 5242880 | tf_op jit(solution)/shard_map/all_to_all | solution.py:61
  83.7 9.3 %collective-permute-start.3 = (bf16[2,64,1024]{2,1,0:T(8,128)(2,1)}, bf16[2,64,1024]{2,1,0:T(8,128)(2,1)S(1)}, u32[]{:S(2)}, u32[]{:S(2)}) collective-permute-start(bf16[2,64,1024]{2,1,0:T(8,128)(2,1)} %get-tuple-element.111), channel_id=1, source_target_pairs={{0,16},{8,24},{16,0},{24,8},{32,48},{40,56},{48,32},{56,40},{64,80... | collective-permute-start | bytes 786440 | tf_op jit(solution)/shard_map/ppermute | solution.py:69
  84.2 13.3 %collective-permute-start.4 = (bf16[2,64,1024]{2,1,0:T(8,128)(2,1)}, bf16[2,64,1024]{2,1,0:T(8,128)(2,1)S(1)}, u32[]{:S(2)}, u32[]{:S(2)}) collective-permute-start(bf16[2,64,1024]{2,1,0:T(8,128)(2,1)} %get-tuple-element.112), channel_id=1, source_target_pairs={{0,32},{8,40},{16,48},{24,56},{32,0},{40,8},{48,16},{56,24},{64,96... | collective-permute-start | bytes 786440 | tf_op jit(solution)/shard_map/ppermute | solution.py:69
  87.4 12.7 %collective-permute-start.5 = (bf16[2,64,1024]{2,1,0:T(8,128)(2,1)}, bf16[2,64,1024]{2,1,0:T(8,128)(2,1)S(1)}, u32[]{:S(2)}, u32[]{:S(2)}) collective-permute-start(bf16[2,64,1024]{2,1,0:T(8,128)(2,1)} %get-tuple-element.113), channel_id=1, source_target_pairs={{0,48},{8,56},{16,32},{24,40},{32,16},{40,24},{48,0},{56,8},{64,11... | collective-permute-start | bytes 786440 | tf_op jit(solution)/shard_map/ppermute | solution.py:69
  117.0 3.6 %copy-start.17 = (bf16[8,160,1024]{2,1,0:T(8,128)(2,1)}, bf16[8,160,1024]{2,1,0:T(8,128)(2,1)S(1)}, u32[]{:S(2)}) copy-start(bf16[8,160,1024]{2,1,0:T(8,128)(2,1)S(1)} %all-to-all-done.3.branch_ref) | copy-start | bytes 7864324
  117.0 12.9 %collective-permute-start.6 = (bf16[2,64,1024]{2,1,0:T(8,128)(2,1)S(1)}, bf16[2,64,1024]{2,1,0:T(8,128)(2,1)S(1)}, u32[]{:S(2)}, u32[]{:S(2)}) collective-permute-start(bf16[2,64,1024]{2,1,0:T(8,128)(2,1)S(1)} %add_convert_fusion.1), channel_id=1, source_target_pairs={{0,64},{8,72},{16,80},{24,88},{32,96},{40,104},{48,112},{56,120},{... | collective-permute-start | bytes 786440 | tf_op jit(solution)/shard_map/ppermute | solution.py:69
  129.8 41.1 %all-to-all-start.4 = ((bf16[8,160,1024]{2,1,0:T(8,128)(2,1)}), bf16[8,160,1024]{2,1,0:T(8,128)(2,1)S(1)}, u32[]{:S(2)}, u32[]{:S(2)}) async-start(bf16[8,160,1024]{2,1,0:T(8,128)(2,1)} %get-tuple-element.122.part_ref), calls=%async_computation.4 | async-start | bytes 5242880 | tf_op jit(solution)/shard_map/all_to_all | solution.py:61
  133.6 13.0 %collective-permute-start.9 = (bf16[2,64,1024]{2,1,0:T(8,128)(2,1)S(1)}, bf16[2,64,1024]{2,1,0:T(8,128)(2,1)S(1)}, u32[]{:S(2)}, u32[]{:S(2)}) collective-permute-start(bf16[2,64,1024]{2,1,0:T(8,128)(2,1)S(1)} %add_convert_fusion), channel_id=1, source_target_pairs={{0,48},{8,56},{16,32},{24,40},{32,16},{40,24},{48,0},{56,8},{64,11... | collective-permute-start | bytes 786440 | tf_op jit(solution)/shard_map/ppermute | solution.py:69
  135.8 10.7 %collective-permute-start.8 = (bf16[2,64,1024]{2,1,0:T(8,128)(2,1)S(1)}, bf16[2,64,1024]{2,1,0:T(8,128)(2,1)S(1)}, u32[]{:S(2)}, u32[]{:S(2)}) collective-permute-start(bf16[2,64,1024]{2,1,0:T(8,128)(2,1)S(1)} %add_convert_fusion), channel_id=1, source_target_pairs={{0,32},{8,40},{16,48},{24,56},{32,0},{40,8},{48,16},{56,24},{64,96... | collective-permute-start | bytes 786440 | tf_op jit(solution)/shard_map/ppermute | solution.py:69
  136.6 10.5 %collective-permute-start.7 = (bf16[2,64,1024]{2,1,0:T(8,128)(2,1)S(1)}, bf16[2,64,1024]{2,1,0:T(8,128)(2,1)S(1)}, u32[]{:S(2)}, u32[]{:S(2)}) collective-permute-start(bf16[2,64,1024]{2,1,0:T(8,128)(2,1)S(1)} %add_convert_fusion), channel_id=1, source_target_pairs={{0,16},{8,24},{16,0},{24,8},{32,48},{40,56},{48,32},{56,40},{64,80... | collective-permute-start | bytes 786440 | tf_op jit(solution)/shard_map/ppermute | solution.py:69
  143.8 3.6 %copy-start.29 = (bf16[544,512]{1,0:T(8,128)(2,1)S(1)}, bf16[544,512]{1,0:T(8,128)(2,1)}, u32[]{:S(2)}) copy-start(bf16[544,512]{1,0:T(8,128)(2,1)} %get-tuple-element.132) | copy-start | bytes 1671172
  147.3 20.7 %copy-start.16 = (bf16[4,2,64,1024]{3,2,1,0:T(8,128)(2,1)}, bf16[4,2,64,1024]{3,2,1,0:T(8,128)(2,1)S(1)}, u32[]{:S(2)}) copy-start(bf16[4,2,64,1024]{3,2,1,0:T(8,128)(2,1)S(1)} %pad_maximum_fusion.1.own_ref) | copy-start | bytes 3145732
  147.3 20.7 %collective-permute-start.11 = (bf16[4,2,64,1024]{3,2,1,0:T(8,128)(2,1)S(1)}, bf16[4,2,64,1024]{3,2,1,0:T(8,128)(2,1)S(1)}, u32[]{:S(2)}, u32[]{:S(2)}) collective-permute-start(bf16[4,2,64,1024]{3,2,1,0:T(8,128)(2,1)S(1)} %pad_maximum_fusion.1.own_ref), channel_id=1, source_target_pairs={{0,8},{8,0},{16,24},{24,16},{32,40},{40,32},{48,56},{56,48},{64,72... | collective-permute-start | bytes 3145736 | tf_op jit(solution)/shard_map/ppermute | solution.py:69
  147.4 3.4 %collective-permute-start.10 = (bf16[544,512]{1,0:T(8,128)(2,1)S(1)}, bf16[544,512]{1,0:T(8,128)(2,1)S(1)}, u32[]{:S(2)}, u32[]{:S(2)}) collective-permute-start(bf16[544,512]{1,0:T(8,128)(2,1)S(1)} %copy-done.29), channel_id=1, source_target_pairs={{0,8},{8,0},{16,24},{24,16},{32,40},{40,32},{48,56},{56,48},{64,72... | collective-permute-start | bytes 1671176 | tf_op jit(solution)/shard_map/ppermute | solution.py:69
  150.8 0.8 copy-start.22
  153.8 7.3 %collective-permute-start.12 = (bf16[2,80,512]{2,1,0:T(8,128)(2,1)}, bf16[2,80,512]{2,1,0:T(8,128)(2,1)S(1)}, u32[]{:S(2)}, u32[]{:S(2)}) collective-permute-start(bf16[2,80,512]{2,1,0:T(8,128)(2,1)} %get-tuple-element.138), channel_id=1, source_target_pairs={{0,16},{8,24},{16,0},{24,8},{32,48},{40,56},{48,32},{56,40},{64,80... | collective-permute-start | bytes 491528 | tf_op jit(solution)/shard_map/ppermute | solution.py:69
  155.0 10.5 %collective-permute-start.13 = (bf16[2,80,512]{2,1,0:T(8,128)(2,1)}, bf16[2,80,512]{2,1,0:T(8,128)(2,1)S(1)}, u32[]{:S(2)}, u32[]{:S(2)}) collective-permute-start(bf16[2,80,512]{2,1,0:T(8,128)(2,1)} %get-tuple-element.139), channel_id=1, source_target_pairs={{0,32},{8,40},{16,48},{24,56},{32,0},{40,8},{48,16},{56,24},{64,96... | collective-permute-start | bytes 491528 | tf_op jit(solution)/shard_map/ppermute | solution.py:69
  157.4 10.6 %collective-permute-start.14 = (bf16[2,80,512]{2,1,0:T(8,128)(2,1)}, bf16[2,80,512]{2,1,0:T(8,128)(2,1)S(1)}, u32[]{:S(2)}, u32[]{:S(2)}) collective-permute-start(bf16[2,80,512]{2,1,0:T(8,128)(2,1)} %get-tuple-element.140), channel_id=1, source_target_pairs={{0,48},{8,56},{16,32},{24,40},{32,16},{40,24},{48,0},{56,8},{64,11... | collective-permute-start | bytes 491528 | tf_op jit(solution)/shard_map/ppermute | solution.py:69
  161.0 7.0 %copy-start.25 = (bf16[2,80,512]{2,1,0:T(8,128)(2,1)}, bf16[2,80,512]{2,1,0:T(8,128)(2,1)S(1)}, u32[]{:S(2)}) copy-start(bf16[2,80,512]{2,1,0:T(8,128)(2,1)S(1)} %collective-permute-done.12.one_ref) | copy-start | bytes 491524
  165.4 2.6 %copy-start.26 = (bf16[2,80,512]{2,1,0:T(8,128)(2,1)}, bf16[2,80,512]{2,1,0:T(8,128)(2,1)S(1)}, u32[]{:S(2)}) copy-start(bf16[2,80,512]{2,1,0:T(8,128)(2,1)S(1)} %collective-permute-done.13.two_ref) | copy-start | bytes 491524
  168.0 0.7 copy-start.27
  168.0 1.0 copy-start.20
  170.9 1.9 copy-start.12
  170.9 7.2 %collective-permute-start.15 = (bf16[2,80,512]{2,1,0:T(8,128)(2,1)}, bf16[2,80,512]{2,1,0:T(8,128)(2,1)S(1)}, u32[]{:S(2)}, u32[]{:S(2)}) collective-permute-start(bf16[2,80,512]{2,1,0:T(8,128)(2,1)} %get-tuple-element.151.own_ref), channel_id=1, source_target_pairs={{0,64},{8,72},{16,80},{24,88},{32,96},{40,104},{48,112},{56,120},{... | collective-permute-start | bytes 491528 | tf_op jit(solution)/shard_map/ppermute | solution.py:69
  175.9 14.1 %copy-start.3 = (f32[1024]{0:T(1024)S(1)}, f32[1024]{0:T(1024)}, u32[]{:S(2)}) copy-start(f32[1024]{0:T(1024)} %param.30) | copy-start | bytes 12292
  178.2 0.7 copy-start.24
  178.9 26.5 %all-to-all-start.5 = ((bf16[8,96,1024]{2,1,0:T(8,128)(2,1)}), bf16[8,96,1024]{2,1,0:T(8,128)(2,1)}, u32[]{:S(2)}, u32[]{:S(2)}) async-start(bf16[8,96,1024]{2,1,0:T(8,128)(2,1)} %shard_map.281), calls=%async_computation.5 | async-start | bytes 3145728 | tf_op jit(solution)/shard_map/all_to_all | solution.py:61
  185.9 11.4 %collective-permute-start.18 = (bf16[2,64,512]{2,1,0:T(8,128)(2,1)}, bf16[2,64,512]{2,1,0:T(8,128)(2,1)S(1)}, u32[]{:S(2)}, u32[]{:S(2)}) collective-permute-start(bf16[2,64,512]{2,1,0:T(8,128)(2,1)} %get-tuple-element.159), channel_id=1, source_target_pairs={{0,48},{8,56},{16,32},{24,40},{32,16},{40,24},{48,0},{56,8},{64,11... | collective-permute-start | bytes 393224 | tf_op jit(solution)/shard_map/ppermute | solution.py:69
  186.9 10.4 %collective-permute-start.17 = (bf16[2,64,512]{2,1,0:T(8,128)(2,1)}, bf16[2,64,512]{2,1,0:T(8,128)(2,1)S(1)}, u32[]{:S(2)}, u32[]{:S(2)}) collective-permute-start(bf16[2,64,512]{2,1,0:T(8,128)(2,1)} %get-tuple-element.159), channel_id=1, source_target_pairs={{0,32},{8,40},{16,48},{24,56},{32,0},{40,8},{48,16},{56,24},{64,96... | collective-permute-start | bytes 393224 | tf_op jit(solution)/shard_map/ppermute | solution.py:69
  187.3 10.0 %collective-permute-start.16 = (bf16[2,64,512]{2,1,0:T(8,128)(2,1)}, bf16[2,64,512]{2,1,0:T(8,128)(2,1)S(1)}, u32[]{:S(2)}, u32[]{:S(2)}) collective-permute-start(bf16[2,64,512]{2,1,0:T(8,128)(2,1)} %get-tuple-element.159), channel_id=1, source_target_pairs={{0,16},{8,24},{16,0},{24,8},{32,48},{40,56},{48,32},{56,40},{64,80... | collective-permute-start | bytes 393224 | tf_op jit(solution)/shard_map/ppermute | solution.py:69
  193.3 4.0 %copy-start.28 = (bf16[2,64,512]{2,1,0:T(8,128)(2,1)S(1)}, bf16[2,64,512]{2,1,0:T(8,128)(2,1)}, u32[]{:S(2)}) copy-start(bf16[2,64,512]{2,1,0:T(8,128)(2,1)} %get-tuple-element.159) | copy-start | bytes 393220
  197.4 2.0 copy-start.19
  197.4 2.0 collective-permute-start.19
  199.4 0.8 copy-start.23
  202.9 6.8 %copy-start.11 = (f32[608,1024]{1,0:T(8,128)S(1)}, f32[608,1024]{1,0:T(8,128)}, u32[]{:S(2)}) copy-start(f32[608,1024]{1,0:T(8,128)} %og_ref.1) | copy-start | bytes 7471108
  207.8 5.5 %collective-permute-start.20 = (f32[8,1024]{1,0:T(8,128)S(1)}, f32[8,1024]{1,0:T(8,128)S(1)}, u32[]{:S(2)}, u32[]{:S(2)}) collective-permute-start(f32[8,1024]{1,0:T(8,128)S(1)} %add_reduce_fusion), channel_id=1, source_target_pairs={{0,64},{8,72},{16,80},{24,88},{32,96},{40,104},{48,112},{56,120},{... | collective-permute-start | bytes 98312 | tf_op jit(solution)/shard_map/ppermute | solution.py:69
